TPU v7x, 32 devices: a whole 2x2x4 slice. The times are simulated.
32 devices in a mesh: dp: 4 (over y, core), expert: 8 (over z, x).
Axes of the slice: x: 2, y: 2, z: 4, core: 2. Of those that a mesh axis runs over, the one named last changes fastest.
Arguments:
- tokens: bfloat16 [128, 4096], P('dp'), may hold values from -6 to 6
- cotangent: bfloat16 [128, 4096], P('dp'), may hold values from -0.29882812 to 0.29882812
- logits: float32 [128, 32], P('dp'), may hold values from 0 to 320
- routes: int32 [128, 8], P('dp'), may hold values from 0 to 31, as said below
- gate_weight: bfloat16 [32, 1536, 4096], P('expert', 'dp'), may hold values from -0.09375 to 0.09375
- up_weight: bfloat16 [32, 1536, 4096], P('expert', 'dp'), may hold values from -0.09375 to 0.09375
- down_weight: bfloat16 [32, 1536, 4096], P('expert', 'dp'), may hold values from -0.15625 to 0.15625
Outputs:
- logit_grad: float32 [128, 32], P('dp')
- router_grad: float32 [4096, 32], P('dp')
Inputs may be any that keep to these rules, and one draw needn't show every extreme that they name: `routes`: each row names 8 different experts.
All inputs are finite; a program needn't handle non-finite values.
Results may differ from a plain program's by a relative error of at most 0.0028.
Values may be sent and summed in bfloat16 or wider, within the bound.
No kernel may reach another device: no remote copies, remote signals or barrier semaphores. Data moves between devices by JAX's collectives and lax.ppermute only.
A program may use at most 128 MiB of HBM per device.

v0:
```python
import jax
import jax.numpy as jnp
from jax import lax
from jax.sharding import PartitionSpec as P


def per_device(tokens, cotangent, logits, routes, gate_weight, up_weight, down_weight):
    data_count = lax.axis_size("dp")
    expert_count = lax.axis_size("expert")
    data_index = lax.axis_index("dp")
    expert_index = lax.axis_index("expert")
    tok_dev = tokens.shape[0]
    local_experts = gate_weight.shape[0]
    ff_dev = gate_weight.shape[1]
    model_width = gate_weight.shape[2]
    unit_count = local_experts * ff_dev
    total_tokens = tok_dev * data_count
    gate_flat = gate_weight.reshape(unit_count, model_width)
    up_flat = up_weight.reshape(unit_count, model_width)
    down_flat = down_weight.reshape(unit_count, model_width)
    contract = (((1,), (1,)), ((), ()))
    rows_x = lax.all_gather(tokens, "dp", axis=0, tiled=True)
    rows_g = lax.all_gather(cotangent, "dp", axis=0, tiled=True)
    row_count = rows_x.shape[0]
    gate_pre = lax.dot_general(rows_x, gate_flat, contract, preferred_element_type=jnp.float32)
    up_pre = lax.dot_general(rows_x, up_flat, contract, preferred_element_type=jnp.float32)
    hidden = jax.nn.silu(gate_pre) * up_pre
    paired = lax.dot_general(rows_g, down_flat, contract, preferred_element_type=jnp.float32)
    partial_value = jnp.sum((hidden * paired).reshape(row_count, local_experts, ff_dev), axis=2)
    experts_all = local_experts * expert_count
    placed = lax.dynamic_update_slice(
        jnp.zeros((total_tokens, experts_all), jnp.float32),
        partial_value,
        (0, expert_index * local_experts),
    )
    summed = lax.psum(placed, ("dp", "expert"))
    scores = lax.dynamic_slice_in_dim(summed, data_index * tok_dev, tok_dev, 0)
    shifted = logits - jnp.max(logits, axis=1, keepdims=True)
    raised = jnp.exp(shifted)
    probs = raised / jnp.sum(raised, axis=1, keepdims=True)
    experts_range = jnp.arange(experts_all, dtype=jnp.int32)
    chosen = jnp.sum(
        (routes[:, :, None] == experts_range[None, None, :]).astype(jnp.float32), axis=1
    )
    mass = jnp.sum(probs * chosen, axis=1, keepdims=True)
    weighted = jnp.sum(probs * chosen * scores, axis=1, keepdims=True)
    prob_grad = scores / mass - chosen * weighted / (mass * mass)
    logit_grad = probs * (prob_grad - jnp.sum(probs * prob_grad, axis=1, keepdims=True))
    grad_bf = logit_grad.astype(jnp.bfloat16)
    router_grad = lax.psum_scatter(
        lax.dot_general(
            tokens, grad_bf, (((0,), (0,)), ((), ())), preferred_element_type=jnp.float32
        ),
        "dp",
        scatter_dimension=0,
        tiled=True,
    )
    return (logit_grad, router_grad)


def solution(mesh):
    placed = (
        P("dp", None),
        P("dp", None),
        P("dp", None),
        P("dp", None),
        P("expert", "dp", None),
        P("expert", "dp", None),
        P("expert", "dp", None),
    )
    return jax.shard_map(
        per_device,
        mesh=mesh,
        in_specs=placed,
        out_specs=(P("dp", None), P("dp", None)),
        check_vma=False,
    )
```

profile of v0, /device:TPU:0, one launch (start us, length us, event | category | flops | bytes accessed | tf_op | source)
XLA Modules:
  0.0 128.0 jit_solution(7309021678069686588)
XLA Ops:
  7.2 0.0 all-gather.3.cloned.1.call-start
  7.2 0.7 all-gather.3.cloned.1.call-update
  7.9 0.0 all-gather.5.cloned.1.call-start
  7.9 0.7 all-gather.5.cloned.1.call-update
  8.6 0.0 reduce-scatter.2.cloned.1.call-start
  8.7 0.8 reduce_max.9
  9.5 0.9 fusion.1
  10.4 0.8 copy.10
  11.2 0.1 convert_reduce_fusion
  11.3 17.7 %all-gather.3.cloned.1.call-done = bf16[128,4096]{1,0:T(8,128)(2,1)} async-done(((bf16[32,4096]{1,0:T(8,128)(2,1)}), bf16[128,4096]{1,0:T(8,128)(2,1)}) %all-gather.3.cloned.1.call-update) | async-done | bytes 1048592 | tf_op jit(solution)/shard_map/all_gather | solution.py:22
  29.1 9.3 %fusion.3 = f32[128,1536]{1,0:T(8,128)S(1)} fusion(bf16[128,4096]{1,0:T(8,128)(2,1)} %all-gather.3.cloned.1.call-done, bf16[1536,4096]{1,0:T(8,128)(2,1)} %bitcast.12), kind=kOutput, calls=%fused_computation.14 | convolution fusion | flops 1610612736 | bytes 14417920 | tf_op jit(solution)/shard_map/dot_general | solution.py:25
  38.3 8.9 %convolution_multiply_fusion.1 = f32[128,1536]{1,0:T(8,128)S(1)} fusion(bf16[128,4096]{1,0:T(8,128)(2,1)S(1)} %copy-done, bf16[1536,4096]{1,0:T(8,128)(2,1)} %bitcast.14, f32[128,1536]{1,0:T(8,128)S(1)} %fusion.3), kind=kOutput, calls=%fused_computation.2 | convolution fusion | flops 1611595776 | bytes 15204352 | tf_op jit(solution)/shard_map/dot_general | solution.py:26
  47.3 0.1 all-gather.5.cloned.1.call-done
  47.4 9.2 %convolution_multiply_fusion = f32[128,1536]{1,0:T(8,128)S(1)} fusion(f32[128,1536]{1,0:T(8,128)S(1)} %convolution_multiply_fusion.1, bf16[128,4096]{1,0:T(8,128)(2,1)} %all-gather.5.cloned.1.call-done, bf16[1536,4096]{1,0:T(8,128)(2,1)} %bitcast.13), kind=kOutput, calls=%fused_computation.1 | convolution fusion | flops 1610809344 | bytes 15204352 | tf_op jit(solution)/shard_map/dot_general | solution.py:28
  56.6 0.3 reshape.29
  56.9 0.2 reduce_sum.55
  57.1 0.4 dynamic_update_slice.3
  57.5 40.0 %psum.7 = f32[128,32]{1,0:T(8,128)S(1)} all-reduce(f32[128,32]{1,0:T(8,128)S(1)} %dynamic_update_slice.3), channel_id=1, replica_groups=mesh['dp'=4,'expert'=8] {'dp','expert'}, use_global_device_ids=true, to_apply=%region_3.4 | all-reduce | flops 4096 | bytes 32768 | tf_op jit(solution)/shard_map/psum | solution.py:36
  97.6 0.2 multiply_reduce_fusion.1
  97.8 0.2 multiply_reduce_fusion
  98.0 0.1 subtract_multiply_fusion
  98.1 1.0 convolution_bitcast_fusion
  99.1 0.0 reduce-scatter.2.cloned.1.call-update
  99.2 22.3 %reduce-scatter.2.cloned.1.call-done = f32[1024,32]{0,1:T(8,128)} async-done(((f32[4096,32]{0,1:T(8,128)}), f32[1024,32]{0,1:T(8,128)}) %reduce-scatter.2.cloned.1.call-update) | async-done | bytes 131088 | tf_op jit(solution)/shard_map/reduce_scatter | solution.py:50
  (10 shorter events, 0.0 us)
Async XLA Ops:
  7.2 21.9 %all-gather.3.cloned.1.call-start = ((), (), s32[]{:S(2)}) async-start(), calls=%async_computation.1 | async-start | bytes 1310720 | tf_op jit(solution)/shard_map/all_gather | solution.py:22
  7.9 39.5 %all-gather.5.cloned.1.call-start = ((), (), s32[]{:S(2)}) async-start(), calls=%async_computation.2 | async-start | bytes 1310720 | tf_op jit(solution)/shard_map/all_gather | solution.py:23
  8.6 112.8 %reduce-scatter.2.cloned.1.call-start = ((), (), s32[]{:S(2)}) async-start(), calls=%async_computation.3 | async-start | bytes 655360 | tf_op jit(solution)/shard_map/reduce_scatter | solution.py:50
  29.1 9.3 %copy-start = (bf16[128,4096]{1,0:T(8,128)(2,1)S(1)}, bf16[128,4096]{1,0:T(8,128)(2,1)}, u32[]{:S(2)}) copy-start(bf16[128,4096]{1,0:T(8,128)(2,1)} %all-gather.3.cloned.1.call-done) | copy-start | bytes 3145732
  47.3 50.3 %copy-start.2 = (f32[32,32]{1,0:T(8,128)S(1)}, f32[32,32]{1,0:T(8,128)}, u32[]{:S(2)}) copy-start(f32[32,32]{1,0:T(8,128)} %param.9) | copy-start | bytes 12292
  47.3 50.8 %copy-start.1 = (bf16[32,4096]{1,0:T(8,128)(2,1)S(1)}, bf16[32,4096]{1,0:T(8,128)(2,1)}, u32[]{:S(2)}) copy-start(bf16[32,4096]{1,0:T(8,128)(2,1)} %param.7) | copy-start | bytes 786436
  98.1 23.4 %copy-start.3 = (f32[32,32]{1,0:T(8,128)}, f32[32,32]{1,0:T(8,128)S(1)}, u32[]{:S(2)}) copy-start(f32[32,32]{1,0:T(8,128)S(1)} %subtract_multiply_fusion) | copy-start | bytes 12292
Sparse Core Ops, SparseCore 0:
  9.6 19.4 all-gather.2
  30.6 16.7 all-gather.4
  99.3 22.1 reduce-scatter.1
where the time goes:
time: 128 us
  waiting for transfers between devices  41.5 us (32%)
  blocking collectives  40 us (31%)
  matrix products  28.4 us (22%)
  between operations  13.9 us (11%)
  other arithmetic  2.56 us (2%)
  local copies, waits for them, and re-layouts  1.48 us (1%)
    psum x1, blocking collectives, per_device(): summed = lax.psum(placed, ('dp', 'expert'))  40 us
    reduce_scatter x1, waiting for transfers between devices, per_device(): lax.psum_scatter(lax.dot_general(tokens, grad_bf, (((0,), (0,)), ((), ())...  22.3 us
    all_gather x1, waiting for transfers between devices, per_device(): rows_x = lax.all_gather(tokens, 'dp', axis=0, tiled=True)  17.7 us
    dot_general x1, matrix products, per_device(): lax.dot_general(rows_x, gate_flat, contract, preferred_element_type=jnp.f...  9.25 us
    dot_general x1, matrix products, per_device(): lax.dot_general(rows_g, down_flat, contract, preferred_element_type=jnp.f...  9.2 us
    dot_general x1, matrix products, per_device(): lax.dot_general(rows_x, up_flat, contract, preferred_element_type=jnp.flo...  8.93 us
  transfers between devices with their start and end apart: 3, of which 3 were waited for; matrix products, arithmetic and copies ran while one was open for 16% of the time, Pallas kernels for 0%

commit v1 on v0

v1 whole, which is shorter than its diff:
```python
import functools

import jax
import jax.numpy as jnp
from jax import lax
from jax.experimental import pallas as pl
from jax.experimental.pallas import tpu as pltpu
from jax.sharding import PartitionSpec as P

CORES = 2


def dot_rows(a, b):
    return lax.dot_general(a, b, (((1,), (1,)), ((), ())), preferred_element_type=jnp.float32)


def place_rows(pieces, distances, rows):
    me = lax.axis_index("dp")
    tok_dev = pieces[0].shape[0]
    for piece, distance in zip(pieces, distances):
        start = pl.multiple_of(jnp.bitwise_xor(me, distance) * tok_dev, tok_dev)
        rows[pl.ds(start, tok_dev), :] = piece[...]


def start_loads(plan, sources, nears, sems):
    copies, number = [], 0
    for (first, last), source, near in zip(plan, sources, nears):
        for chunk in range(first, last):
            copies.append(pltpu.make_async_copy(source.at[chunk], near.at[chunk - first], sems.at[number]))
            number += 1
    for copy in copies:
        copy.start()
    return copies


def load_kernel(plan, source, after, near, sems):
    for copy in start_loads(plan, [source], [near], sems):
        copy.wait()


def pack_load_kernel(plan, logits, routes, cotangent, source, after, packed, near, *scratch):
    logits_near, routes_near, columns, pack_sems, sems = scratch
    model_width = cotangent.shape[1]
    copies = [
        pltpu.make_async_copy(logits, logits_near, pack_sems.at[0]),
        pltpu.make_async_copy(routes, routes_near, pack_sems.at[1]),
        pltpu.make_async_copy(cotangent, packed.at[:, :model_width], pack_sems.at[2]),
    ]
    for copy in copies:
        copy.start()
    loads = start_loads(plan, [source], [near], sems)
    columns[...] = jnp.zeros(columns.shape, jnp.float32)
    copies[0].wait()
    left = logits_near[...]
    experts_all = left.shape[1]
    for term in range(3):
        rounded = left.astype(jnp.bfloat16).astype(jnp.float32)
        columns[:, term * experts_all : (term + 1) * experts_all] = rounded
        left = left - rounded
    copies[1].wait()
    columns[:, 3 * experts_all : 3 * experts_all + routes.shape[0]] = routes_near[...].astype(jnp.float32).T
    packed[:, model_width:] = columns[...].astype(jnp.bfloat16)
    copies[2].wait()
    for copy in loads:
        copy.wait()


def find_chunk(parts, chunk):
    for first, buffer in reversed(parts):
        if chunk >= first:
            return buffer[chunk - first]


def hidden_chunk(rows, gate_rows, up_rows):
    gate_pre = dot_rows(rows[...], gate_rows)
    up_pre = dot_rows(rows[...], up_rows)
    return gate_pre / (1.0 + jnp.exp(-gate_pre)) * up_pre


def first_hidden_kernel(distances, plan, *refs):
    count = len(distances)
    pieces, refs = refs[:count], refs[count:]
    gate, up, up_far, down_far, hidden, mine, rows, up_near, down_near, sems, mine_sem = refs
    loads = start_loads(plan, [up_far, down_far], [up_near, down_near], sems)
    place_rows(pieces, distances, rows)
    width = mine.shape[1]
    start = pl.multiple_of(lax.axis_index("dp") * width, width)
    own = pltpu.make_async_copy(rows.at[:, pl.ds(start, width)], mine, mine_sem)
    own.start()
    for chunk in range(hidden.shape[0]):
        hidden[chunk] = hidden_chunk(rows, gate[chunk], up[chunk])
    own.wait()
    for copy in loads:
        copy.wait()


def second_hidden_kernel(up_starts, plan, rows, gate, up_0, up_1, down_far, after, hidden, down_near, sems):
    loads = start_loads(plan, [down_far], [down_near], sems)
    up_parts = list(zip(up_starts, (up_0, up_1)))
    for number in range(hidden.shape[0]):
        chunk = plan[0][0] + number
        hidden[number] = hidden_chunk(rows, gate[chunk], find_chunk(up_parts, chunk))
    for copy in loads:
        copy.wait()


def score_kernel(distances, top, *refs):
    count = len(distances)
    pieces, refs = refs[:count], refs[count:]
    hidden, down, partial, probs, chosen, rows, total = refs[:2], refs[2:4], *refs[4:]
    model_width = down[0].shape[2]
    experts_all = probs.shape[0]
    place_rows(pieces, distances, rows)
    packed = rows[:, model_width:].astype(jnp.float32).T
    terms = [packed[term * experts_all : (term + 1) * experts_all] for term in range(3)]
    logits = terms[0] + terms[1] + terms[2]
    raised = jnp.exp(logits - jnp.max(logits, axis=0, keepdims=True))
    probs[...] = raised / jnp.sum(raised, axis=0, keepdims=True)
    number = lax.broadcasted_iota(jnp.int32, logits.shape, 0).astype(jnp.float32)
    named = jnp.zeros(logits.shape, jnp.float32)
    for slot in range(3 * experts_all, 3 * experts_all + top):
        named = named + (packed[slot : slot + 1] == number).astype(jnp.float32)
    chosen[...] = named
    local_experts, _, unit = total.shape
    half, chunks = down[0].shape[0], down[0].shape[0] + down[1].shape[0]
    per_chunk = down[0].shape[1] // unit
    per_expert = chunks * per_chunk // local_experts
    sums = [None] * local_experts
    for chunk in range(chunks):
        side, at = chunk // half, chunk % half
        product = hidden[side][at] * dot_rows(rows[:, :model_width], down[side][at])
        for part in range(per_chunk):
            expert = (chunk * per_chunk + part) // per_expert
            term = product[:, part * unit : (part + 1) * unit]
            sums[expert] = term if sums[expert] is None else sums[expert] + term
    for expert in range(local_experts):
        total[expert] = sums[expert]
        partial[:, expert : expert + 1, :] = jnp.broadcast_to(
            jnp.sum(total[expert].T, axis=0, keepdims=True)[None], (partial.shape[0], 1, partial.shape[2])
        )


def gradient_kernel(data_count, blocks, probs_ref, chosen_ref, mine, logit_grad, router_grad, grads):
    experts_all, total_tokens = probs_ref.shape
    scores = jnp.sum(blocks[...].reshape((data_count, experts_all, total_tokens)), axis=0)
    probs, chosen = probs_ref[...], chosen_ref[...]
    mass = jnp.sum(probs * chosen, axis=0, keepdims=True)
    weighted = jnp.sum(probs * chosen * scores, axis=0, keepdims=True)
    prob_grad = scores / mass - chosen * weighted / (mass * mass)
    grad = probs * (prob_grad - jnp.sum(probs * prob_grad, axis=0, keepdims=True))
    router_grad[...] = jnp.dot(grad.astype(jnp.bfloat16), mine[...], preferred_element_type=jnp.float32)
    grads[...] = grad.T
    tok_dev = logit_grad.shape[0]
    logit_grad[...] = grads[pl.ds(pl.multiple_of(lax.axis_index("dp") * tok_dev, tok_dev), tok_dev), :]


def swap(value, axis, distance):
    return lax.ppermute(value, axis, [(index, index ^ distance) for index in range(lax.axis_size(axis))])


def per_device(tokens, cotangent, logits, routes, gate_weight, up_weight, down_weight):
    data_count = lax.axis_size("dp")
    expert_count = lax.axis_size("expert")
    tok_dev, model_width = tokens.shape
    local_experts, ff_dev = gate_weight.shape[:2]
    total_tokens = tok_dev * data_count
    experts_all = local_experts * expert_count
    top = routes.shape[1]
    unit = 128 if ff_dev % 128 == 0 else ff_dev
    units = local_experts * ff_dev // unit
    chunk_rows = unit * (2 if unit == 128 and units % 2 == 0 else 1)
    chunks = local_experts * ff_dev // chunk_rows
    extra = -(-(3 * experts_all + top) // 128) * 128
    chips = data_count // CORES
    distances = [chip * CORES + core for chip in range(chips) for core in range(CORES)]
    half = chunks // 2
    up_cut = 5 * chunks // 6

    vmem = pl.BlockSpec(memory_space=pltpu.VMEM)
    hbm = pl.BlockSpec(memory_space=pltpu.HBM)
    anywhere = pl.BlockSpec(memory_space=pl.ANY)
    row_bytes = total_tokens * model_width * 2
    chunk_bytes = chunk_rows * model_width * 2
    chunk_flops = 2 * chunk_rows * model_width * total_tokens

    def keep_far(value):
        return pltpu.with_memory_space_constraint(value, pltpu.HBM)

    def near(first, last):
        return pltpu.VMEM((last - first, chunk_rows, model_width), jnp.bfloat16)

    def cost(loads, dots):
        return pl.CostEstimate(flops=dots * chunk_flops, bytes_accessed=loads * chunk_bytes, transcendentals=0)

    def scoped(size):
        return pltpu.CompilerParams(vmem_limit_bytes=size + (2 << 20))

    def load(part, source, after):
        return pl.pallas_call(
            functools.partial(load_kernel, [part]),
            out_shape=near(*part),
            in_specs=[hbm, anywhere],
            out_specs=vmem,
            scratch_shapes=[pltpu.SemaphoreType.DMA((part[1] - part[0],))],
            compiler_params=scoped(0),
            cost_estimate=cost(part[1] - part[0], 0),
            name="load_up",
        )(source, after)

    cut = (chunks, chunk_rows, model_width)
    gate, up, down = (keep_far(weight.reshape(cut)) for weight in (gate_weight, up_weight, down_weight))

    tokens_beside = swap(tokens, "dp", 1)
    tokens_far = [swap(tokens, "dp", chip * CORES) for chip in range(1, chips)]
    packed, gate_near = pl.pallas_call(
        functools.partial(pack_load_kernel, [(0, chunks)]),
        out_shape=(jax.ShapeDtypeStruct((tok_dev, model_width + extra), jnp.bfloat16), near(0, chunks)),
        in_specs=[hbm] * 4 + [anywhere],
        out_specs=(vmem, vmem),
        scratch_shapes=[
            pltpu.VMEM((tok_dev, experts_all), jnp.float32),
            pltpu.VMEM((top, tok_dev), jnp.int32),
            pltpu.VMEM((tok_dev, extra), jnp.float32),
            pltpu.SemaphoreType.DMA((3,)),
            pltpu.SemaphoreType.DMA((chunks,)),
        ],
        compiler_params=scoped(0),
        cost_estimate=cost(chunks, 0),
        name="load_gate_pack",
    )(keep_far(logits), keep_far(routes.T), keep_far(cotangent), gate, tokens_beside)
    packed_far = [swap(packed, "dp", chip * CORES) for chip in range(1, chips)]
    packed_beside = swap(packed, "dp", 1)

    tokens_far, gate_near = lax.optimization_barrier((tokens_far, gate_near))
    token_pieces = [tokens, tokens_beside]
    for far in tokens_far:
        token_pieces += [far, swap(far, "dp", 1)]
    up_0 = load((0, up_cut), up, tokens_far[0])

    plan = [(up_cut, chunks), (0, half)]
    loads = sum(last - first for first, last in plan)
    hidden_0, mine, rows, up_1, down_0 = pl.pallas_call(
        functools.partial(first_hidden_kernel, distances, plan),
        out_shape=(
            jax.ShapeDtypeStruct((half, total_tokens, chunk_rows), jnp.float32),
            jax.ShapeDtypeStruct((total_tokens, model_width // data_count), jnp.bfloat16),
            jax.ShapeDtypeStruct((total_tokens, model_width), jnp.bfloat16),
            near(*plan[0]),
            near(*plan[1]),
        ),
        in_specs=[vmem] * (data_count + 2) + [hbm] * 2,
        out_specs=(vmem,) * 5,
        scratch_shapes=[pltpu.SemaphoreType.DMA((loads,)), pltpu.SemaphoreType.DMA],
        compiler_params=scoped(0),
        cost_estimate=cost(loads, 2 * half),
        name="hidden_first",
    )(*token_pieces, gate_near, up_0, up, down)

    packed_far, hidden_0, rows = lax.optimization_barrier((packed_far, hidden_0, rows))
    packed_pieces = [packed, packed_beside]
    for far in packed_far:
        packed_pieces += [far, swap(far, "dp", 1)]

    plan = [(half, chunks)]
    hidden_1, down_1 = pl.pallas_call(
        functools.partial(second_hidden_kernel, (0, up_cut), plan),
        out_shape=(
            jax.ShapeDtypeStruct((chunks - half, total_tokens, chunk_rows), jnp.float32),
            near(*plan[0]),
        ),
        in_specs=[vmem] * 4 + [hbm, anywhere],
        out_specs=(vmem, vmem),
        scratch_shapes=[pltpu.SemaphoreType.DMA((chunks - half,))],
        compiler_params=scoped(0),
        cost_estimate=cost(chunks - half, 2 * (chunks - half)),
        name="hidden_second",
    )(rows, gate_near, up_0, up_1, down, packed_far[0])

    table = jax.ShapeDtypeStruct((experts_all, total_tokens), jnp.float32)
    partial, probs, chosen = pl.pallas_call(
        functools.partial(score_kernel, distances, top),
        out_shape=(
            jax.ShapeDtypeStruct((data_count * expert_count, local_experts, total_tokens), jnp.float32),
            table,
            table,
        ),
        in_specs=[vmem] * (data_count + 4),
        out_specs=(vmem, vmem, vmem),
        scratch_shapes=[
            pltpu.VMEM((total_tokens, model_width + extra), jnp.bfloat16),
            pltpu.VMEM((local_experts, total_tokens, unit), jnp.float32),
        ],
        compiler_params=scoped(2 * row_bytes),
        cost_estimate=cost(0, chunks),
        name="scores",
    )(*packed_pieces, hidden_0, hidden_1, down_0, down_1)

    score_blocks = lax.all_to_all(partial, ("dp", "expert"), split_axis=0, concat_axis=0, tiled=True)

    logit_grad, router_grad = pl.pallas_call(
        functools.partial(gradient_kernel, data_count),
        out_shape=(
            jax.ShapeDtypeStruct((tok_dev, experts_all), jnp.float32),
            jax.ShapeDtypeStruct((experts_all, model_width // data_count), jnp.float32),
        ),
        in_specs=[vmem] * 4,
        out_specs=(vmem, vmem),
        scratch_shapes=[pltpu.VMEM((total_tokens, experts_all), jnp.float32)],
        compiler_params=scoped(4 << 20),
        name="gradient",
    )(score_blocks, probs, chosen, mine)
    return logit_grad, router_grad.T


def solution(mesh):
    placed = (
        P("dp", None),
        P("dp", None),
        P("dp", None),
        P("dp", None),
        P("expert", "dp", None),
        P("expert", "dp", None),
        P("expert", "dp", None),
    )
    return jax.shard_map(
        per_device,
        mesh=mesh,
        in_specs=placed,
        out_specs=(P("dp", None), P("dp", None)),
        check_vma=False,
    )
```

time: 128 us -> 46.1 us (0.36)
  waiting for transfers between devices: 41.5 us -> 2.25 us
  matrix products: 28.4 us -> 0 us
  blocking collectives: 40 us -> 12 us
  Pallas kernels: 0 us -> 25.5 us
  between operations: 13.9 us -> 0.72 us
  starting transfers between devices: 0.11 us -> 5.45 us
  other arithmetic: 2.56 us -> 0 us
  local copies, waits for them, and re-layouts: 1.48 us -> 0.01 us
    psum x1 -> x0, blocking collectives: 40 us -> none  [per_device(): summed = lax.psum(placed, ('dp', 'expert'))]
    dot_general x4 -> x0, matrix products: 28.4 us -> none  [the longest x1 9.25 us: per_device(): lax.dot_general(rows_x, gate_flat, contract, preferred_element_type=jnp.f...]
    pallas_call x0 -> x6, Pallas kernels: none -> 25.5 us  [the longest x1 7 us: per_device(): pl.pallas_call(functools.partial(second_hidden_kernel, (0, up_cut), plan)...]
    reduce_scatter x1 -> x0, waiting for transfers between devices: 22.3 us -> none  [per_device(): lax.psum_scatter(lax.dot_general(tokens, grad_bf, (((0,), (0,)), ((), ())...]
    all_gather x2 -> x0, waiting for transfers between devices: 17.8 us -> none  [the longest x1 17.7 us: per_device(): rows_x = lax.all_gather(tokens, 'dp', axis=0, tiled=True)]
    all_to_all x0 -> x1, blocking collectives: none -> 12 us  [per_device(): lax.all_to_all(partial, ('dp', 'expert'), split_axis=0, concat_axis=0, ti...]
    ppermute x0 -> x6, starting transfers between devices: none -> 5.45 us  [swap(): lax.ppermute(value, axis, [(index, index ^ distance) for index in range(l...]
    ppermute x0 -> x6, waiting for transfers between devices: none -> 2.25 us  [swap(): lax.ppermute(value, axis, [(index, index ^ distance) for index in range(l...]
  transfers between devices with their start and end apart: 3 -> 6, of which waited for: 3 -> 1; matrix products, arithmetic and copies ran while one was open for 16% -> 0% of each run, Pallas kernels for 0% -> 44%
where the time goes in v1:
time: 46.1 us; the launch traced here: 45.9 us
  Pallas kernels  25.5 us (55%)
  blocking collectives  12 us (26%)
  starting transfers between devices  5.45 us (12%)
  waiting for transfers between devices  2.25 us (5%)
  between operations  0.72 us (2%)
    all_to_all x1, blocking collectives, per_device(): lax.all_to_all(partial, ('dp', 'expert'), split_axis=0, concat_axis=0, ti...  12 us
    pallas_call x1, Pallas kernels, per_device(): pl.pallas_call(functools.partial(second_hidden_kernel, (0, up_cut), plan)...  7 us
    ppermute x6, starting transfers between devices, swap(): lax.ppermute(value, axis, [(index, index ^ distance) for index in range(l...  5.45 us
    pallas_call x1, Pallas kernels, per_device(): pl.pallas_call(functools.partial(pack_load_kernel, [(0, chunks)]), out_sh...  4.85 us
    pallas_call x1, Pallas kernels, per_device(): pl.pallas_call(functools.partial(first_hidden_kernel, distances, plan), o...  4.45 us
    pallas_call x1, Pallas kernels, per_device(): pl.pallas_call(functools.partial(score_kernel, distances, top), out_shape...  4.28 us
    pallas_call x1, Pallas kernels, load(): pl.pallas_call(functools.partial(load_kernel, [part]), out_shape=near(*pa...  4.11 us
    ppermute x6, waiting for transfers between devices, swap(): lax.ppermute(value, axis, [(index, index ^ distance) for index in range(l...  2.25 us
  transfers between devices with their start and end apart: 6, of which 1 were waited for; matrix products, arithmetic and copies ran while one was open for 0% of the time, Pallas kernels for 44%

profile of v1, /device:TPU:0, one launch (start us, length us, event | category | flops | bytes accessed | tf_op | source)
XLA Modules:
  0.0 45.9 jit_solution(10549254502539432626)
XLA Ops:
  0.6 0.5 %collective-permute-start = (bf16[32,4096]{1,0:T(8,128)(2,1)}, bf16[32,4096]{1,0:T(8,128)(2,1)S(1)}, u32[]{:S(2)}, u32[]{:S(2)}) collective-permute-start(bf16[32,4096]{1,0:T(8,128)(2,1)} %refs_0_.1), channel_id=1, source_target_pairs={{0,8},{8,0},{16,24},{24,16},{1,9},{9,1},{17,25},{25,17},{2,10},{10... | collective-permute-start | bytes 786440 | tf_op jit(solution)/shard_map/ppermute | solution.py:158
  1.1 2.6 %collective-permute-start.3 = (bf16[32,4096]{1,0:T(8,128)(2,1)}, bf16[32,4096]{1,0:T(8,128)(2,1)S(1)}, u32[]{:S(2)}, u32[]{:S(2)}) collective-permute-start(bf16[32,4096]{1,0:T(8,128)(2,1)} %refs_0_.1), channel_id=1, source_target_pairs={{0,16},{8,24},{16,0},{24,8},{1,17},{9,25},{17,1},{25,9},{2,18},{10... | collective-permute-start | bytes 786440 | tf_op jit(solution)/shard_map/ppermute | solution.py:158
  3.7 0.0 collective-permute-done.after.refs_1_
  3.7 4.8 %load_gate_pack.1 = (bf16[32,4224]{1,0:T(8,128)(2,1)S(1)}, bf16[6,256,4096]{2,1,0:T(8,128)(2,1)S(1)}) custom-call(f32[32,32]{1,0:T(8,128)} %logits.1, s32[8,32]{1,0:T(8,128)} %bitcast.10, bf16[32,4096]{1,0:T(8,128)(2,1)} %cotangent.1, bf16[6,256,4096]{2,1,0:T(8,128)(2,1)} %bitcast.9, bf16[32,4096]{1,0:T(8,128)(2,1)S(1)} %collective-permute-done.after.refs_1_), custom_call_target="tpu_custom_call" | custom-call | bytes 12582912 | tf_op jit(solution)/shard_map/load_gate_pack/pallas_call | solution.py:215
  8.6 0.0 copy-start
  8.6 2.2 %collective-permute-done.3.after.refs_2_ = bf16[32,4096]{1,0:T(8,128)(2,1)S(1)} collective-permute-done((bf16[32,4096]{1,0:T(8,128)(2,1)}, bf16[32,4096]{1,0:T(8,128)(2,1)S(1)}, u32[]{:S(2)}, u32[]{:S(2)}) %collective-permute-start.3) | collective-permute-done | bytes 262176 | tf_op jit(solution)/shard_map/ppermute | solution.py:158
  10.9 0.0 collective-permute-start.4
  10.9 1.8 %collective-permute-start.2 = (bf16[32,4224]{1,0:T(8,128)(2,1)S(1)}, bf16[32,4224]{1,0:T(8,128)(2,1)S(1)}, u32[]{:S(2)}, u32[]{:S(2)}) collective-permute-start(bf16[32,4224]{1,0:T(8,128)(2,1)S(1)} %get-tuple-element.21.refs_0_), channel_id=1, source_target_pairs={{0,16},{8,24},{16,0},{24,8},{1,17},{9,25},{17,1},{25,9},{2,18},{10... | collective-permute-start | bytes 811016 | tf_op jit(solution)/shard_map/ppermute | solution.py:158
  12.6 0.2 collective-permute-start.1
  12.8 4.1 %load_up.1.refs_5_.up_0 = bf16[5,256,4096]{2,1,0:T(8,128)(2,1)S(1)} custom-call(bf16[6,256,4096]{2,1,0:T(8,128)(2,1)} %bitcast.5, bf16[32,4096]{1,0:T(8,128)(2,1)S(1)} %collective-permute-done.3.after.refs_2_), custom_call_target="tpu_custom_call" | custom-call | bytes 10485760 | tf_op jit(solution)/shard_map/load_up/pallas_call | solution.py:199
  17.0 0.0 collective-permute-done.4.refs_3_
  17.0 0.0 copy-done
  17.0 4.5 %hidden_first.1 = (f32[3,128,256]{2,1,0:T(8,128)S(1)}, bf16[128,1024]{1,0:T(8,128)(2,1)S(1)}, bf16[128,4096]{1,0:T(8,128)(2,1)S(1)}, bf16[1,256,4096]{2,1,0:T(8,128)(2,1)S(1)}, bf16[3,256,4096]{2,1,0:T(8,128)(2,1)S(1)}) custom-call(bf16[32,4096]{1,0:T(8,128)(2,1)S(1)} %copy-done, bf16[32,4096]{1,0:T(8,128)(2,1)S(1)} %collective-permute-done.after.refs_1_, ...), custom_call_target="tpu_custom_call" | custom-call | flops 1610612736 | bytes 8388608 | tf_op jit(solution)/shard_map/hidden_first/pallas_call | solution.py:242
  21.4 0.0 collective-permute-done.2.after.refs_2_
  21.4 0.3 collective-permute-start.5
  21.8 7.0 %hidden_second.1 = (f32[3,128,256]{2,1,0:T(8,128)S(1)}, bf16[3,256,4096]{2,1,0:T(8,128)(2,1)S(1)}) custom-call(bf16[128,4096]{1,0:T(8,128)(2,1)S(1)} %get-tuple-element.29.rows, bf16[6,256,4096]{2,1,0:T(8,128)(2,1)S(1)} %get-tuple-element.24.refs_4_.gate, bf16[5,256,4096]{2,1,0:T(8,128)(2,1)S(1)} %load_up.1.refs_5_.up_0, ...), custom_call_target="tpu_custom_call" | custom-call | flops 1610612736 | bytes 6291456 | tf_op jit(solution)/shard_map/hidden_second/pallas_call | solution.py:265
  28.8 0.0 collective-permute-done.1.refs_1_
  28.8 0.0 collective-permute-done.5.refs_3_
  28.8 4.3 %scores.1 = (f32[32,4,128]{2,1,0:T(4,128)S(1)}, f32[32,128]{1,0:T(8,128)S(1)}, f32[32,128]{1,0:T(8,128)S(1)}) custom-call(bf16[32,4224]{1,0:T(8,128)(2,1)S(1)} %get-tuple-element.21.refs_0_, bf16[32,4224]{1,0:T(8,128)(2,1)S(1)} %collective-permute-done.1.refs_1_, bf16[32,4224]{1,0:T(8,128)(2,1)S(1)} %collective-permute-done.2.after.refs_2_, ...), custom_call_target="tpu_custom_call" | custom-call | flops 1610612736 | tf_op jit(solution)/shard_map/scores/pallas_call | solution.py:280
  33.1 12.0 %all_to_all.5.blocks = f32[32,4,128]{2,1,0:T(4,128)S(1)} all-to-all(f32[32,4,128]{2,1,0:T(4,128)S(1)} %get-tuple-element.34), channel_id=1, replica_groups=mesh['dp'=4,'expert'=8] {'dp','expert'}, dimensions={0} | all-to-all | bytes 131072 | tf_op jit(solution)/shard_map/all_to_all | solution.py:298
  45.1 0.8 %gradient.1 = (f32[32,32]{1,0:T(8,128)}, f32[32,1024]{1,0:T(8,128)}) custom-call(f32[32,4,128]{2,1,0:T(4,128)S(1)} %all_to_all.5.blocks, f32[32,128]{1,0:T(8,128)S(1)} %get-tuple-element.35.probs_ref, f32[32,128]{1,0:T(8,128)S(1)} %get-tuple-element.36.chosen_ref, bf16[128,1024]{1,0:T(8,128)(2,1)S(1)} %get-tuple-element.37.mine), custom_call_target="tpu_custom_call" | custom-call | tf_op jit(solution)/shard_map/gradient/pallas_call | solution.py:300
Async XLA Ops:
  0.6 3.1 %collective-permute-start = (bf16[32,4096]{1,0:T(8,128)(2,1)}, bf16[32,4096]{1,0:T(8,128)(2,1)S(1)}, u32[]{:S(2)}, u32[]{:S(2)}) collective-permute-start(bf16[32,4096]{1,0:T(8,128)(2,1)} %refs_0_.1), channel_id=1, source_target_pairs={{0,8},{8,0},{16,24},{24,16},{1,9},{9,1},{17,25},{25,17},{2,10},{10... | collective-permute-start | bytes 786440 | tf_op jit(solution)/shard_map/ppermute | solution.py:158
  1.1 9.7 %collective-permute-start.3 = (bf16[32,4096]{1,0:T(8,128)(2,1)}, bf16[32,4096]{1,0:T(8,128)(2,1)S(1)}, u32[]{:S(2)}, u32[]{:S(2)}) collective-permute-start(bf16[32,4096]{1,0:T(8,128)(2,1)} %refs_0_.1), channel_id=1, source_target_pairs={{0,16},{8,24},{16,0},{24,8},{1,17},{9,25},{17,1},{25,9},{2,18},{10... | collective-permute-start | bytes 786440 | tf_op jit(solution)/shard_map/ppermute | solution.py:158
  8.6 8.4 %copy-start = (bf16[32,4096]{1,0:T(8,128)(2,1)S(1)}, bf16[32,4096]{1,0:T(8,128)(2,1)}, u32[]{:S(2)}) copy-start(bf16[32,4096]{1,0:T(8,128)(2,1)} %refs_0_.1) | copy-start | bytes 786436
  10.9 6.1 %collective-permute-start.4 = (bf16[32,4096]{1,0:T(8,128)(2,1)S(1)}, bf16[32,4096]{1,0:T(8,128)(2,1)S(1)}, u32[]{:S(2)}, u32[]{:S(2)}) collective-permute-start(bf16[32,4096]{1,0:T(8,128)(2,1)S(1)} %collective-permute-done.3.after.refs_2_), channel_id=1, source_target_pairs={{0,8},{8,0},{16,24},{24,16},{1,9},{9,1},{17,25},{25,17},{2,10},{10... | collective-permute-start | bytes 786440 | tf_op jit(solution)/shard_map/ppermute | solution.py:158
  10.9 10.6 %collective-permute-start.2 = (bf16[32,4224]{1,0:T(8,128)(2,1)S(1)}, bf16[32,4224]{1,0:T(8,128)(2,1)S(1)}, u32[]{:S(2)}, u32[]{:S(2)}) collective-permute-start(bf16[32,4224]{1,0:T(8,128)(2,1)S(1)} %get-tuple-element.21.refs_0_), channel_id=1, source_target_pairs={{0,16},{8,24},{16,0},{24,8},{1,17},{9,25},{17,1},{25,9},{2,18},{10... | collective-permute-start | bytes 811016 | tf_op jit(solution)/shard_map/ppermute | solution.py:158
  12.6 16.2 %collective-permute-start.1 = (bf16[32,4224]{1,0:T(8,128)(2,1)S(1)}, bf16[32,4224]{1,0:T(8,128)(2,1)S(1)}, u32[]{:S(2)}, u32[]{:S(2)}) collective-permute-start(bf16[32,4224]{1,0:T(8,128)(2,1)S(1)} %get-tuple-element.21.refs_0_), channel_id=1, source_target_pairs={{0,8},{8,0},{16,24},{24,16},{1,9},{9,1},{17,25},{25,17},{2,10},{10... | collective-permute-start | bytes 811016 | tf_op jit(solution)/shard_map/ppermute | solution.py:158
  21.4 7.4 %collective-permute-start.5 = (bf16[32,4224]{1,0:T(8,128)(2,1)S(1)}, bf16[32,4224]{1,0:T(8,128)(2,1)S(1)}, u32[]{:S(2)}, u32[]{:S(2)}) collective-permute-start(bf16[32,4224]{1,0:T(8,128)(2,1)S(1)} %collective-permute-done.2.after.refs_2_), channel_id=1, source_target_pairs={{0,8},{8,0},{16,24},{24,16},{1,9},{9,1},{17,25},{25,17},{2,10},{10... | collective-permute-start | bytes 811016 | tf_op jit(solution)/shard_map/ppermute | solution.py:158

commit v2 on v1

--- a/solution.py
+++ b/solution.py
@@ -12,6 +12,40 @@
 
 def dot_rows(a, b):
     return lax.dot_general(a, b, (((1,), (1,)), ((), ())), preferred_element_type=jnp.float32)
+
+
+def unit_dots(rows, weights, accs):
+    edge = weights[0].shape[0]
+    steps = weights[0].shape[1] // edge
+
+    def push(step):
+        for unit, weight in enumerate(weights):
+            part = weight[:, step * edge : (step + 1) * edge]
+            pltpu.matmul_push_rhs(part, step % 2, unit, transpose=True)
+
+    push(0)
+    for step in range(steps):
+        if step + 1 < steps:
+            push(step + 1)
+        for acc in accs[: len(weights)]:
+            pltpu.matmul_acc_lhs(acc, rows[:, step * edge : (step + 1) * edge], load_staged_rhs=step % 2)
+    return [pltpu.matmul_pop(acc) for acc in accs[: len(weights)]]
+
+
+def with_accs(kernel, shapes):
+    if not shapes:
+        return kernel
+
+    def body(*refs):
+        pl.run_scoped(lambda *accs: kernel(*refs, accs=(accs[:2], accs[2:])), *shapes)
+
+    return body
+
+
+def pair_dots(rows, weights, accs):
+    if accs:
+        return unit_dots(rows, weights, accs)
+    return [dot_rows(rows[...], weight[...]) for weight in weights]
 
 
 def place_rows(pieces, distances, rows):
@@ -68,16 +102,15 @@
 def find_chunk(parts, chunk):
     for first, buffer in reversed(parts):
         if chunk >= first:
-            return buffer[chunk - first]
-
-
-def hidden_chunk(rows, gate_rows, up_rows):
-    gate_pre = dot_rows(rows[...], gate_rows)
-    up_pre = dot_rows(rows[...], up_rows)
+            return buffer.at[chunk - first]
+
+
+def hidden_chunk(rows, gate_rows, up_rows, accs):
+    gate_pre, up_pre = pair_dots(rows, [gate_rows, up_rows], accs)
     return gate_pre / (1.0 + jnp.exp(-gate_pre)) * up_pre
 
 
-def first_hidden_kernel(distances, plan, *refs):
+def first_hidden_kernel(distances, plan, *refs, accs=()):
     count = len(distances)
     pieces, refs = refs[:count], refs[count:]
     gate, up, up_far, down_far, hidden, mine, rows, up_near, down_near, sems, mine_sem = refs
@@ -88,23 +121,23 @@
     own = pltpu.make_async_copy(rows.at[:, pl.ds(start, width)], mine, mine_sem)
     own.start()
     for chunk in range(hidden.shape[0]):
-        hidden[chunk] = hidden_chunk(rows, gate[chunk], up[chunk])
+        hidden[chunk] = hidden_chunk(rows, gate.at[chunk], up.at[chunk], accs and accs[chunk % 2])
     own.wait()
     for copy in loads:
         copy.wait()
 
 
-def second_hidden_kernel(up_starts, plan, rows, gate, up_0, up_1, down_far, after, hidden, down_near, sems):
+def second_hidden_kernel(up_starts, plan, rows, gate, up_0, up_1, down_far, after, hidden, down_near, sems, accs=()):
     loads = start_loads(plan, [down_far], [down_near], sems)
     up_parts = list(zip(up_starts, (up_0, up_1)))
     for number in range(hidden.shape[0]):
         chunk = plan[0][0] + number
-        hidden[number] = hidden_chunk(rows, gate[chunk], find_chunk(up_parts, chunk))
+        hidden[number] = hidden_chunk(rows, gate.at[chunk], find_chunk(up_parts, chunk), accs and accs[chunk % 2])
     for copy in loads:
         copy.wait()
 
 
-def score_kernel(distances, top, *refs):
+def score_kernel(distances, top, *refs, accs=()):
     count = len(distances)
     pieces, refs = refs[:count], refs[count:]
     hidden, down, partial, probs, chosen, rows, total = refs[:2], refs[2:4], *refs[4:]
@@ -126,13 +159,16 @@
     per_chunk = down[0].shape[1] // unit
     per_expert = chunks * per_chunk // local_experts
     sums = [None] * local_experts
-    for chunk in range(chunks):
-        side, at = chunk // half, chunk % half
-        product = hidden[side][at] * dot_rows(rows[:, :model_width], down[side][at])
-        for part in range(per_chunk):
-            expert = (chunk * per_chunk + part) // per_expert
-            term = product[:, part * unit : (part + 1) * unit]
-            sums[expert] = term if sums[expert] is None else sums[expert] + term
+    near = rows.at[:, :model_width]
+    for first in range(0, chunks, 2):
+        places = [(chunk // half, chunk % half) for chunk in range(first, min(first + 2, chunks))]
+        paired = pair_dots(near, [down[side].at[at] for side, at in places], accs and accs[first // 2 % 2])
+        for number, (side, at) in enumerate(places):
+            product = hidden[side][at] * paired[number]
+            for part in range(per_chunk):
+                expert = ((first + number) * per_chunk + part) // per_expert
+                term = product[:, part * unit : (part + 1) * unit]
+                sums[expert] = term if sums[expert] is None else sums[expert] + term
     for expert in range(local_experts):
         total[expert] = sums[expert]
         partial[:, expert : expert + 1, :] = jnp.broadcast_to(
@@ -140,9 +176,13 @@
         )
 
 
-def gradient_kernel(data_count, blocks, probs_ref, chosen_ref, mine, logit_grad, router_grad, grads):
+def add_kernel(parts, copies):
+    copies[...] = jnp.broadcast_to(jnp.sum(parts[...], axis=0, keepdims=True), copies.shape)
+
+
+def gradient_kernel(blocks, probs_ref, chosen_ref, mine, logit_grad, router_grad, grads):
     experts_all, total_tokens = probs_ref.shape
-    scores = jnp.sum(blocks[...].reshape((data_count, experts_all, total_tokens)), axis=0)
+    scores = blocks[...].reshape((experts_all, total_tokens))
     probs, chosen = probs_ref[...], chosen_ref[...]
     mass = jnp.sum(probs * chosen, axis=0, keepdims=True)
     weighted = jnp.sum(probs * chosen * scores, axis=0, keepdims=True)
@@ -207,6 +247,10 @@
             name="load_up",
         )(source, after)
 
+    edge = pltpu.get_tpu_info().mxu_column_size
+    accs = []
+    if chunk_rows == edge and model_width % edge == 0 and total_tokens <= 512:
+        accs = [pltpu.ACC(number % 2)((total_tokens, edge), jnp.float32) for number in range(4)]
     cut = (chunks, chunk_rows, model_width)
     gate, up, down = (keep_far(weight.reshape(cut)) for weight in (gate_weight, up_weight, down_weight))
 
@@ -240,7 +284,7 @@
     plan = [(up_cut, chunks), (0, half)]
     loads = sum(last - first for first, last in plan)
     hidden_0, mine, rows, up_1, down_0 = pl.pallas_call(
-        functools.partial(first_hidden_kernel, distances, plan),
+        with_accs(functools.partial(first_hidden_kernel, distances, plan), accs),
         out_shape=(
             jax.ShapeDtypeStruct((half, total_tokens, chunk_rows), jnp.float32),
             jax.ShapeDtypeStruct((total_tokens, model_width // data_count), jnp.bfloat16),
@@ -263,7 +307,7 @@
 
     plan = [(half, chunks)]
     hidden_1, down_1 = pl.pallas_call(
-        functools.partial(second_hidden_kernel, (0, up_cut), plan),
+        with_accs(functools.partial(second_hidden_kernel, (0, up_cut), plan), accs),
         out_shape=(
             jax.ShapeDtypeStruct((chunks - half, total_tokens, chunk_rows), jnp.float32),
             near(*plan[0]),
@@ -278,9 +322,9 @@
 
     table = jax.ShapeDtypeStruct((experts_all, total_tokens), jnp.float32)
     partial, probs, chosen = pl.pallas_call(
-        functools.partial(score_kernel, distances, top),
+        with_accs(functools.partial(score_kernel, distances, top), accs),
         out_shape=(
-            jax.ShapeDtypeStruct((data_count * expert_count, local_experts, total_tokens), jnp.float32),
+            jax.ShapeDtypeStruct((data_count, local_experts, total_tokens), jnp.float32),
             table,
             table,
         ),
@@ -289,16 +333,26 @@
         scratch_shapes=[
             pltpu.VMEM((total_tokens, model_width + extra), jnp.bfloat16),
             pltpu.VMEM((local_experts, total_tokens, unit), jnp.float32),
-        ],
+        ]
+       ,
         compiler_params=scoped(2 * row_bytes),
         cost_estimate=cost(0, chunks),
         name="scores",
     )(*packed_pieces, hidden_0, hidden_1, down_0, down_1)
 
-    score_blocks = lax.all_to_all(partial, ("dp", "expert"), split_axis=0, concat_axis=0, tiled=True)
+    parts = lax.all_to_all(partial, "dp", split_axis=0, concat_axis=0, tiled=True)
+    summed = pl.pallas_call(
+        add_kernel,
+        out_shape=jax.ShapeDtypeStruct((expert_count, local_experts, total_tokens), jnp.float32),
+        in_specs=[vmem],
+        out_specs=vmem,
+        compiler_params=scoped(0),
+        name="add_parts",
+    )(parts)
+    score_blocks = lax.all_to_all(summed, "expert", split_axis=0, concat_axis=0, tiled=True)
 
     logit_grad, router_grad = pl.pallas_call(
-        functools.partial(gradient_kernel, data_count),
+        gradient_kernel,
         out_shape=(
             jax.ShapeDtypeStruct((tok_dev, experts_all), jnp.float32),
             jax.ShapeDtypeStruct((experts_all, model_width // data_count), jnp.float32),
@@ -322,10 +376,16 @@
         P("expert", "dp", None),
         P("expert", "dp", None),
     )
-    return jax.shard_map(
+    mapped = jax.shard_map(
         per_device,
         mesh=mesh,
         in_specs=placed,
         out_specs=(P("dp", None), P("dp", None)),
         check_vma=False,
     )
+
+    def run(*args):
+        with jax.sharding.use_abstract_mesh(mesh.abstract_mesh):
+            return mapped(*args)
+
+    return run

time: 46.1 us -> 49.5 us (1.074)
  blocking collectives: 12 us -> 18.3 us
  Pallas kernels: 25.5 us -> 22.6 us
    all_to_all x1 -> x2, blocking collectives: 12 us -> 18.3 us  [the longest x1 12.2 us: per_device(): lax.all_to_all(summed, 'expert', split_axis=0, concat_axis=0, tiled=True)]
    pallas_call x4 -> x5, Pallas kernels: 16.6 us -> 13.6 us  [the longest x1 4.47 us: per_device(): pl.pallas_call(with_accs(functools.partial(first_hidden_kernel, distances...]
  transfers between devices with their start and end apart: 6 -> 6, of which waited for: 1 -> 1; matrix products, arithmetic and copies ran while one was open for 0% -> 0% of each run, Pallas kernels for 44% -> 36%
where the time goes in v2:
time: 49.5 us; the launch traced here: 49.3 us
  Pallas kernels  22.6 us (46%)
  blocking collectives  18.3 us (37%)
  starting transfers between devices  5.45 us (11%)
  waiting for transfers between devices  2.25 us (5%)
  between operations  0.72 us (1%)
    all_to_all x1, blocking collectives, per_device(): lax.all_to_all(summed, 'expert', split_axis=0, concat_axis=0, tiled=True)  12.2 us
    all_to_all x1, blocking collectives, per_device(): lax.all_to_all(partial, 'dp', split_axis=0, concat_axis=0, tiled=True)  6.15 us
    ppermute x6, starting transfers between devices, swap(): lax.ppermute(value, axis, [(index, index ^ distance) for index in range(l...  5.45 us
    pallas_call x1, Pallas kernels, per_device(): pl.pallas_call(functools.partial(pack_load_kernel, [(0, chunks)]), out_sh...  4.85 us
    pallas_call x1, Pallas kernels, per_device(): pl.pallas_call(with_accs(functools.partial(first_hidden_kernel, distances...  4.47 us
    pallas_call x1, Pallas kernels, per_device(): pl.pallas_call(with_accs(functools.partial(second_hidden_kernel, (0, up_c...  4.34 us
    pallas_call x1, Pallas kernels, load(): pl.pallas_call(functools.partial(load_kernel, [part]), out_shape=near(*pa...  4.11 us
    pallas_call x1, Pallas kernels, per_device(): pl.pallas_call(with_accs(functools.partial(score_kernel, distances, top),...  3.97 us
  transfers between devices with their start and end apart: 6, of which 1 were waited for; matrix products, arithmetic and copies ran while one was open for 0% of the time, Pallas kernels for 36%

profile of v2, /device:TPU:0, one launch (start us, length us, event | category | flops | bytes accessed | tf_op | source)
XLA Modules:
  0.0 49.3 jit_solution(17675778830002940594)
XLA Ops:
  0.6 0.5 %collective-permute-start = (bf16[32,4096]{1,0:T(8,128)(2,1)}, bf16[32,4096]{1,0:T(8,128)(2,1)S(1)}, u32[]{:S(2)}, u32[]{:S(2)}) collective-permute-start(bf16[32,4096]{1,0:T(8,128)(2,1)} %refs_0_.1), channel_id=1, source_target_pairs={{0,8},{8,0},{16,24},{24,16},{1,9},{9,1},{17,25},{25,17},{2,10},{10... | collective-permute-start | bytes 786440 | tf_op jit(solution)/shard_map/ppermute | solution.py:198
  1.1 2.6 %collective-permute-start.3 = (bf16[32,4096]{1,0:T(8,128)(2,1)}, bf16[32,4096]{1,0:T(8,128)(2,1)S(1)}, u32[]{:S(2)}, u32[]{:S(2)}) collective-permute-start(bf16[32,4096]{1,0:T(8,128)(2,1)} %refs_0_.1), channel_id=1, source_target_pairs={{0,16},{8,24},{16,0},{24,8},{1,17},{9,25},{17,1},{25,9},{2,18},{10... | collective-permute-start | bytes 786440 | tf_op jit(solution)/shard_map/ppermute | solution.py:198
  3.7 0.0 collective-permute-done.after.refs_1_
  3.7 4.8 %load_gate_pack.1 = (bf16[32,4224]{1,0:T(8,128)(2,1)S(1)}, bf16[6,256,4096]{2,1,0:T(8,128)(2,1)S(1)}) custom-call(f32[32,32]{1,0:T(8,128)} %logits.1, s32[8,32]{1,0:T(8,128)} %bitcast.10, bf16[32,4096]{1,0:T(8,128)(2,1)} %cotangent.1, bf16[6,256,4096]{2,1,0:T(8,128)(2,1)} %bitcast.9, bf16[32,4096]{1,0:T(8,128)(2,1)S(1)} %collective-permute-done.after.refs_1_), custom_call_target="tpu_custom_call" | custom-call | bytes 12582912 | tf_op jit(solution)/shard_map/load_gate_pack/pallas_call | solution.py:259
  8.6 0.0 copy-start
  8.6 2.2 %collective-permute-done.3.after.refs_2_ = bf16[32,4096]{1,0:T(8,128)(2,1)S(1)} collective-permute-done((bf16[32,4096]{1,0:T(8,128)(2,1)}, bf16[32,4096]{1,0:T(8,128)(2,1)S(1)}, u32[]{:S(2)}, u32[]{:S(2)}) %collective-permute-start.3) | collective-permute-done | bytes 262176 | tf_op jit(solution)/shard_map/ppermute | solution.py:198
  10.9 0.0 collective-permute-start.4
  10.9 1.8 %collective-permute-start.2 = (bf16[32,4224]{1,0:T(8,128)(2,1)S(1)}, bf16[32,4224]{1,0:T(8,128)(2,1)S(1)}, u32[]{:S(2)}, u32[]{:S(2)}) collective-permute-start(bf16[32,4224]{1,0:T(8,128)(2,1)S(1)} %get-tuple-element.21.refs_0_), channel_id=1, source_target_pairs={{0,16},{8,24},{16,0},{24,8},{1,17},{9,25},{17,1},{25,9},{2,18},{10... | collective-permute-start | bytes 811016 | tf_op jit(solution)/shard_map/ppermute | solution.py:198
  12.6 0.2 collective-permute-start.1
  12.8 4.1 %load_up.1.refs_5_.refs_2_ = bf16[5,256,4096]{2,1,0:T(8,128)(2,1)S(1)} custom-call(bf16[6,256,4096]{2,1,0:T(8,128)(2,1)} %bitcast.5, bf16[32,4096]{1,0:T(8,128)(2,1)S(1)} %collective-permute-done.3.after.refs_2_), custom_call_target="tpu_custom_call" | custom-call | bytes 10485760 | tf_op jit(solution)/shard_map/load_up/pallas_call | solution.py:239
  17.0 0.0 collective-permute-done.4.refs_3_
  17.0 0.0 copy-done
  17.0 4.5 %hidden_first.1 = (f32[3,128,256]{2,1,0:T(8,128)S(1)}, bf16[128,1024]{1,0:T(8,128)(2,1)S(1)}, bf16[128,4096]{1,0:T(8,128)(2,1)S(1)}, bf16[1,256,4096]{2,1,0:T(8,128)(2,1)S(1)}, bf16[3,256,4096]{2,1,0:T(8,128)(2,1)S(1)}) custom-call(bf16[32,4096]{1,0:T(8,128)(2,1)S(1)} %copy-done, bf16[32,4096]{1,0:T(8,128)(2,1)S(1)} %collective-permute-done.after.refs_1_, ...), custom_call_target="tpu_custom_call" | custom-call | flops 1610612736 | bytes 8388608 | tf_op jit(solution)/shard_map/hidden_first/pallas_call | solution.py:286
  21.5 0.0 collective-permute-done.2.refs_5_.refs_2_
  21.5 0.3 collective-permute-start.5
  21.8 4.3 %hidden_second.1 = (f32[3,128,256]{2,1,0:T(8,128)S(1)}, bf16[3,256,4096]{2,1,0:T(8,128)(2,1)S(1)}) custom-call(bf16[128,4096]{1,0:T(8,128)(2,1)S(1)} %get-tuple-element.29.refs_0_, bf16[6,256,4096]{2,1,0:T(8,128)(2,1)S(1)} %get-tuple-element.24.refs_4_.refs_1_, bf16[5,256,4096]{2,1,0:T(8,128)(2,1)S(1)} %load_up.1.refs_5_.refs_2_, ...), custom_call_target="tpu_custom_call" | custom-call | flops 1610612736 | bytes 6291456 | tf_op jit(solution)/shard_map/hidden_second/pallas_call | solution.py:309
  26.2 0.0 collective-permute-done.1.refs_1_
  26.2 0.0 collective-permute-done.5.refs_3_
  26.2 4.0 %scores.1 = (f32[4,4,128]{2,1,0:T(4,128)S(1)}, f32[32,128]{1,0:T(8,128)S(1)}, f32[32,128]{1,0:T(8,128)S(1)}) custom-call(bf16[32,4224]{1,0:T(8,128)(2,1)S(1)} %get-tuple-element.21.refs_0_, bf16[32,4224]{1,0:T(8,128)(2,1)S(1)} %collective-permute-done.1.refs_1_, bf16[32,4224]{1,0:T(8,128)(2,1)S(1)} %collective-permute-done.2.refs_5_.refs_2_, ...), custom_call_target="tpu_custom_call" | custom-call | flops 1610612736 | tf_op jit(solution)/shard_map/scores/pallas_call | solution.py:324
  30.2 6.2 %all_to_all.10.parts = f32[4,4,128]{2,1,0:T(4,128)S(1)} all-to-all(f32[4,4,128]{2,1,0:T(4,128)S(1)} %get-tuple-element.34), channel_id=1, replica_groups=mesh['dp'=4,'expert'=8] {'dp'}, dimensions={0} | all-to-all | bytes 16384 | tf_op jit(solution)/shard_map/all_to_all | solution.py:343
  36.3 12.2 %all_to_all.11.blocks = f32[8,4,128]{2,1,0:T(4,128)S(1)} all-to-all(f32[8,4,128]{2,1,0:T(4,128)S(1)} %add_parts.1), channel_id=1, replica_groups=mesh['dp'=4,'expert'=8] {'expert'}, dimensions={0} | all-to-all | bytes 32768 | tf_op jit(solution)/shard_map/all_to_all | solution.py:352
  48.5 0.9 %gradient.1 = (f32[32,32]{1,0:T(8,128)}, f32[32,1024]{1,0:T(8,128)}) custom-call(f32[8,4,128]{2,1,0:T(4,128)S(1)} %all_to_all.11.blocks, f32[32,128]{1,0:T(8,128)S(1)} %get-tuple-element.35.probs_ref, f32[32,128]{1,0:T(8,128)S(1)} %get-tuple-element.36.chosen_ref, bf16[128,1024]{1,0:T(8,128)(2,1)S(1)} %get-tuple-element.37.mine), custom_call_target="tpu_custom_call" | custom-call | tf_op jit(solution)/shard_map/gradient/pallas_call | solution.py:354
  (1 shorter events, 0.0 us)
Async XLA Ops:
  0.6 3.1 %collective-permute-start = (bf16[32,4096]{1,0:T(8,128)(2,1)}, bf16[32,4096]{1,0:T(8,128)(2,1)S(1)}, u32[]{:S(2)}, u32[]{:S(2)}) collective-permute-start(bf16[32,4096]{1,0:T(8,128)(2,1)} %refs_0_.1), channel_id=1, source_target_pairs={{0,8},{8,0},{16,24},{24,16},{1,9},{9,1},{17,25},{25,17},{2,10},{10... | collective-permute-start | bytes 786440 | tf_op jit(solution)/shard_map/ppermute | solution.py:198
  1.1 9.7 %collective-permute-start.3 = (bf16[32,4096]{1,0:T(8,128)(2,1)}, bf16[32,4096]{1,0:T(8,128)(2,1)S(1)}, u32[]{:S(2)}, u32[]{:S(2)}) collective-permute-start(bf16[32,4096]{1,0:T(8,128)(2,1)} %refs_0_.1), channel_id=1, source_target_pairs={{0,16},{8,24},{16,0},{24,8},{1,17},{9,25},{17,1},{25,9},{2,18},{10... | collective-permute-start | bytes 786440 | tf_op jit(solution)/shard_map/ppermute | solution.py:198
  8.6 8.4 %copy-start = (bf16[32,4096]{1,0:T(8,128)(2,1)S(1)}, bf16[32,4096]{1,0:T(8,128)(2,1)}, u32[]{:S(2)}) copy-start(bf16[32,4096]{1,0:T(8,128)(2,1)} %refs_0_.1) | copy-start | bytes 786436
  10.9 6.1 %collective-permute-start.4 = (bf16[32,4096]{1,0:T(8,128)(2,1)S(1)}, bf16[32,4096]{1,0:T(8,128)(2,1)S(1)}, u32[]{:S(2)}, u32[]{:S(2)}) collective-permute-start(bf16[32,4096]{1,0:T(8,128)(2,1)S(1)} %collective-permute-done.3.after.refs_2_), channel_id=1, source_target_pairs={{0,8},{8,0},{16,24},{24,16},{1,9},{9,1},{17,25},{25,17},{2,10},{10... | collective-permute-start | bytes 786440 | tf_op jit(solution)/shard_map/ppermute | solution.py:198
  10.9 10.6 %collective-permute-start.2 = (bf16[32,4224]{1,0:T(8,128)(2,1)S(1)}, bf16[32,4224]{1,0:T(8,128)(2,1)S(1)}, u32[]{:S(2)}, u32[]{:S(2)}) collective-permute-start(bf16[32,4224]{1,0:T(8,128)(2,1)S(1)} %get-tuple-element.21.refs_0_), channel_id=1, source_target_pairs={{0,16},{8,24},{16,0},{24,8},{1,17},{9,25},{17,1},{25,9},{2,18},{10... | collective-permute-start | bytes 811016 | tf_op jit(solution)/shard_map/ppermute | solution.py:198
  12.6 13.6 %collective-permute-start.1 = (bf16[32,4224]{1,0:T(8,128)(2,1)S(1)}, bf16[32,4224]{1,0:T(8,128)(2,1)S(1)}, u32[]{:S(2)}, u32[]{:S(2)}) collective-permute-start(bf16[32,4224]{1,0:T(8,128)(2,1)S(1)} %get-tuple-element.21.refs_0_), channel_id=1, source_target_pairs={{0,8},{8,0},{16,24},{24,16},{1,9},{9,1},{17,25},{25,17},{2,10},{10... | collective-permute-start | bytes 811016 | tf_op jit(solution)/shard_map/ppermute | solution.py:198
  21.5 4.7 %collective-permute-start.5 = (bf16[32,4224]{1,0:T(8,128)(2,1)S(1)}, bf16[32,4224]{1,0:T(8,128)(2,1)S(1)}, u32[]{:S(2)}, u32[]{:S(2)}) collective-permute-start(bf16[32,4224]{1,0:T(8,128)(2,1)S(1)} %collective-permute-done.2.refs_5_.refs_2_), channel_id=1, source_target_pairs={{0,8},{8,0},{16,24},{24,16},{1,9},{9,1},{17,25},{25,17},{2,10},{10... | collective-permute-start | bytes 811016 | tf_op jit(solution)/shard_map/ppermute | solution.py:198

commit v3 on v2

v3 whole, which is shorter than its diff:
```python
import functools

import jax
import jax.numpy as jnp
from jax import lax
from jax.experimental import pallas as pl
from jax.experimental.pallas import tpu as pltpu
from jax.sharding import PartitionSpec as P

CORES = 2


def dot_rows(a, b):
    return lax.dot_general(a, b, (((1,), (1,)), ((), ())), preferred_element_type=jnp.float32)


def stream_dots(rows, jobs, accs, finish):
    if not accs:
        for number, weights in enumerate(jobs):
            finish(number, [dot_rows(rows[...], weight[...]) for weight in weights])
        return
    edge = jobs[0][0].shape[0]
    order = [(number, step) for number in range(len(jobs)) for step in range(jobs[0][0].shape[1] // edge)]

    def push(at):
        number, step = order[at]
        for unit, weight in enumerate(jobs[number]):
            part = weight[:, step * edge : (step + 1) * edge]
            pltpu.matmul_push_rhs(part, at % 2, unit, transpose=True)

    def pop(number):
        finish(number, [pltpu.matmul_pop(acc) for acc in accs[number % 2][: len(jobs[number])]])

    push(0)
    for at, (number, step) in enumerate(order):
        if at + 1 < len(order):
            push(at + 1)
        for acc in accs[number % 2][: len(jobs[number])]:
            pltpu.matmul_acc_lhs(acc, rows[:, step * edge : (step + 1) * edge], load_staged_rhs=at % 2)
        if step == 1 and number > 0:
            pop(number - 1)
    pop(len(jobs) - 1)


def with_accs(kernel, shapes):
    if not shapes:
        return kernel

    def body(*refs):
        pl.run_scoped(lambda *accs: kernel(*refs, accs=(accs[:2], accs[2:])), *shapes)

    return body


def place_rows(pieces, distances, rows):
    me = lax.axis_index("dp")
    tok_dev = pieces[0].shape[0]
    for piece, distance in zip(pieces, distances):
        start = pl.multiple_of(jnp.bitwise_xor(me, distance) * tok_dev, tok_dev)
        rows[pl.ds(start, tok_dev), :] = piece[...]


def start_loads(plan, sources, nears, sems):
    copies, number = [], 0
    for (first, last), source, near in zip(plan, sources, nears):
        for chunk in range(first, last):
            copies.append(pltpu.make_async_copy(source.at[chunk], near.at[chunk - first], sems.at[number]))
            number += 1
    for copy in copies:
        copy.start()
    return copies


def pack_load_kernel(plan, logits, routes, cotangent, gate, up, after, packed, gate_near, up_near, *scratch):
    logits_near, routes_near, columns, pack_sems, sems = scratch
    model_width = cotangent.shape[1]
    copies = [
        pltpu.make_async_copy(logits, logits_near, pack_sems.at[0]),
        pltpu.make_async_copy(routes, routes_near, pack_sems.at[1]),
        pltpu.make_async_copy(cotangent, packed.at[:, :model_width], pack_sems.at[2]),
    ]
    for copy in copies:
        copy.start()
    loads = start_loads(plan, [gate, up], [gate_near, up_near], sems)
    columns[...] = jnp.zeros(columns.shape, jnp.float32)
    copies[0].wait()
    left = logits_near[...]
    experts_all = left.shape[1]
    for term in range(3):
        rounded = left.astype(jnp.bfloat16).astype(jnp.float32)
        columns[:, term * experts_all : (term + 1) * experts_all] = rounded
        left = left - rounded
    copies[1].wait()
    columns[:, 3 * experts_all : 3 * experts_all + routes.shape[0]] = routes_near[...].astype(jnp.float32).T
    packed[:, model_width:] = columns[...].astype(jnp.bfloat16)
    copies[2].wait()
    for copy in loads:
        copy.wait()


def find_chunk(parts, chunk):
    for first, buffer in reversed(parts):
        if chunk >= first:
            return buffer.at[chunk - first]


def gated(dots):
    gate_pre, up_pre = dots
    return gate_pre / (1.0 + jnp.exp(-gate_pre)) * up_pre


def first_hidden_kernel(distances, plan, *refs, accs=()):
    count = len(distances)
    pieces, refs = refs[:count], refs[count:]
    gate, up, up_far, down_far, hidden, mine, rows, up_near, down_near, sems, mine_sem = refs
    loads = start_loads(plan, [up_far, down_far], [up_near, down_near], sems)
    place_rows(pieces, distances, rows)
    width = mine.shape[1]
    start = pl.multiple_of(lax.axis_index("dp") * width, width)
    own = pltpu.make_async_copy(rows.at[:, pl.ds(start, width)], mine, mine_sem)
    own.start()
    jobs = [[gate.at[chunk], up.at[chunk]] for chunk in range(hidden.shape[0])]

    def finish(number, dots):
        hidden[number] = gated(dots)

    stream_dots(rows, jobs, accs, finish)
    own.wait()
    for copy in loads:
        copy.wait()


def second_hidden_kernel(plan, rows, gate, up, down_far, after, hidden, down_near, sems, accs=()):
    loads = start_loads(plan, [down_far], [down_near], sems)
    first = gate.shape[0] - hidden.shape[0]
    jobs = [[gate.at[first + chunk], up.at[chunk]] for chunk in range(hidden.shape[0])]

    def finish(number, dots):
        hidden[number] = gated(dots)

    stream_dots(rows, jobs, accs, finish)
    for copy in loads:
        copy.wait()


def score_kernel(distances, top, down_starts, *refs, accs=()):
    count = len(distances)
    pieces, refs = refs[:count], refs[count:]
    hidden_0, hidden_1, down_0, down_1, partial, probs, chosen, rows, total = refs
    model_width = down_0.shape[2]
    experts_all = probs.shape[0]
    place_rows(pieces, distances, rows)
    local_experts, _, unit = total.shape
    half = hidden_0.shape[0]
    chunks = half + hidden_1.shape[0]
    per_chunk = down_0.shape[1] // unit
    per_expert = chunks * per_chunk // local_experts
    hidden_parts = [(0, hidden_0), (half, hidden_1)]
    down_parts = list(zip(down_starts, (down_0, down_1)))
    jobs = [
        [find_chunk(down_parts, chunk) for chunk in range(first, min(first + 2, chunks))]
        for first in range(0, chunks, 2)
    ]
    sums = [None] * local_experts

    def routing():
        packed = rows[:, model_width:].astype(jnp.float32).T
        terms = [packed[term * experts_all : (term + 1) * experts_all] for term in range(3)]
        logits = terms[0] + terms[1] + terms[2]
        raised = jnp.exp(logits - jnp.max(logits, axis=0, keepdims=True))
        probs[...] = raised / jnp.sum(raised, axis=0, keepdims=True)
        number = lax.broadcasted_iota(jnp.int32, logits.shape, 0).astype(jnp.float32)
        named = jnp.zeros(logits.shape, jnp.float32)
        for slot in range(3 * experts_all, 3 * experts_all + top):
            named = named + (packed[slot : slot + 1] == number).astype(jnp.float32)
        chosen[...] = named

    def finish(number, dots):
        if number == 0:
            routing()
        for side, paired in enumerate(dots):
            chunk = 2 * number + side
            product = find_chunk(hidden_parts, chunk)[...] * paired
            for part in range(per_chunk):
                expert = (chunk * per_chunk + part) // per_expert
                term = product[:, part * unit : (part + 1) * unit]
                sums[expert] = term if sums[expert] is None else sums[expert] + term

    stream_dots(rows.at[:, :model_width], jobs, accs, finish)
    for expert in range(local_experts):
        total[expert] = sums[expert]
    lines = [jnp.sum(total[expert].T, axis=0, keepdims=True) for expert in range(local_experts)]
    partial[...] = jnp.concatenate(lines, axis=0)


def joined(distance, held, other):
    second = jnp.bitwise_and(lax.axis_index("expert"), distance) != 0
    return jnp.concatenate([jnp.where(second, other, held), jnp.where(second, held, other)], axis=0)


def join_kernel(distance, held, other, both):
    both[...] = joined(distance, held[...], other[...])


def gradient_kernel(distance, held, other, probs_ref, chosen_ref, mine, logit_grad, router_grad, grads):
    scores = joined(distance, held[...], other[...])
    probs, chosen = probs_ref[...], chosen_ref[...]
    mass = jnp.sum(probs * chosen, axis=0, keepdims=True)
    weighted = jnp.sum(probs * chosen * scores, axis=0, keepdims=True)
    prob_grad = scores / mass - chosen * weighted / (mass * mass)
    grad = probs * (prob_grad - jnp.sum(probs * prob_grad, axis=0, keepdims=True))
    router_grad[...] = jnp.dot(grad.astype(jnp.bfloat16), mine[...], preferred_element_type=jnp.float32)
    grads[...] = grad.T
    tok_dev = logit_grad.shape[0]
    logit_grad[...] = grads[pl.ds(pl.multiple_of(lax.axis_index("dp") * tok_dev, tok_dev), tok_dev), :]


def swap(value, axis, distance):
    return lax.ppermute(value, axis, [(index, index ^ distance) for index in range(lax.axis_size(axis))])


def per_device(tokens, cotangent, logits, routes, gate_weight, up_weight, down_weight):
    data_count = lax.axis_size("dp")
    expert_count = lax.axis_size("expert")
    tok_dev, model_width = tokens.shape
    local_experts, ff_dev = gate_weight.shape[:2]
    total_tokens = tok_dev * data_count
    experts_all = local_experts * expert_count
    top = routes.shape[1]
    unit = 128 if ff_dev % 128 == 0 else ff_dev
    units = local_experts * ff_dev // unit
    chunk_rows = unit * (2 if unit == 128 and units % 2 == 0 else 1)
    chunks = local_experts * ff_dev // chunk_rows
    extra = -(-(3 * experts_all + top) // 128) * 128
    chips = data_count // CORES
    distances = [chip * CORES + core for chip in range(chips) for core in range(CORES)]
    half = chunks // 2
    down_cut = max(1, chunks // 6)

    vmem = pl.BlockSpec(memory_space=pltpu.VMEM)
    hbm = pl.BlockSpec(memory_space=pltpu.HBM)
    anywhere = pl.BlockSpec(memory_space=pl.ANY)
    row_bytes = total_tokens * model_width * 2

    def keep_far(value):
        return pltpu.with_memory_space_constraint(value, pltpu.HBM)

    def near(first, last):
        return pltpu.VMEM((last - first, chunk_rows, model_width), jnp.bfloat16)

    def cost(loads, dots):
        return pl.CostEstimate(flops=dots, bytes_accessed=loads, transcendentals=0)

    def scoped(size):
        return pltpu.CompilerParams(vmem_limit_bytes=size + (2 << 20))

    edge = pltpu.get_tpu_info().mxu_column_size
    accs = []
    if chunk_rows == edge and model_width % edge == 0 and total_tokens <= 512:
        accs = [pltpu.ACC(number % 2)((total_tokens, edge), jnp.float32) for number in range(4)]
    cut = (chunks, chunk_rows, model_width)
    gate, up, down = (keep_far(weight.reshape(cut)) for weight in (gate_weight, up_weight, down_weight))

    tokens_beside = swap(tokens, "dp", 1)
    tokens_far = [swap(tokens, "dp", chip * CORES) for chip in range(1, chips)]
    plan = [(0, chunks), (0, half)]
    loads = chunks + half
    packed, gate_near, up_0 = pl.pallas_call(
        functools.partial(pack_load_kernel, plan),
        out_shape=(
            jax.ShapeDtypeStruct((tok_dev, model_width + extra), jnp.bfloat16),
            near(*plan[0]),
            near(*plan[1]),
        ),
        in_specs=[hbm] * 5 + [anywhere],
        out_specs=(vmem,) * 3,
        scratch_shapes=[
            pltpu.VMEM((tok_dev, experts_all), jnp.float32),
            pltpu.VMEM((top, tok_dev), jnp.int32),
            pltpu.VMEM((tok_dev, extra), jnp.float32),
            pltpu.SemaphoreType.DMA((3,)),
            pltpu.SemaphoreType.DMA((loads,)),
        ],
        compiler_params=scoped(0),
        cost_estimate=cost(loads, 0),
        name="load_pack",
    )(keep_far(logits), keep_far(routes.T), keep_far(cotangent), gate, up, tokens_beside)
    packed_far = [swap(packed, "dp", chip * CORES) for chip in range(1, chips)]
    packed_beside = swap(packed, "dp", 1)

    tokens_far, gate_near, up_0 = lax.optimization_barrier((tokens_far, gate_near, up_0))
    token_pieces = [tokens, tokens_beside]
    for far in tokens_far:
        token_pieces += [far, swap(far, "dp", 1)]

    plan = [(half, chunks), (0, down_cut)]
    loads = sum(last - first for first, last in plan)
    hidden_0, mine, rows, up_1, down_0 = pl.pallas_call(
        with_accs(functools.partial(first_hidden_kernel, distances, plan), accs),
        out_shape=(
            jax.ShapeDtypeStruct((half, total_tokens, chunk_rows), jnp.float32),
            jax.ShapeDtypeStruct((total_tokens, model_width // data_count), jnp.bfloat16),
            jax.ShapeDtypeStruct((total_tokens, model_width), jnp.bfloat16),
            near(*plan[0]),
            near(*plan[1]),
        ),
        in_specs=[vmem] * (data_count + 2) + [hbm] * 2,
        out_specs=(vmem,) * 5,
        scratch_shapes=[pltpu.SemaphoreType.DMA((loads,)), pltpu.SemaphoreType.DMA],
        compiler_params=scoped(0),
        cost_estimate=cost(loads, 2 * half),
        name="hidden_first",
    )(*token_pieces, gate_near, up_0, up, down)

    packed_far, hidden_0, rows = lax.optimization_barrier((packed_far, hidden_0, rows))
    packed_pieces = [packed, packed_beside]
    for far in packed_far:
        packed_pieces += [far, swap(far, "dp", 1)]

    plan = [(down_cut, chunks)]
    hidden_1, down_1 = pl.pallas_call(
        with_accs(functools.partial(second_hidden_kernel, plan), accs),
        out_shape=(
            jax.ShapeDtypeStruct((chunks - half, total_tokens, chunk_rows), jnp.float32),
            near(*plan[0]),
        ),
        in_specs=[vmem] * 3 + [hbm, anywhere],
        out_specs=(vmem, vmem),
        scratch_shapes=[pltpu.SemaphoreType.DMA((chunks - down_cut,))],
        compiler_params=scoped(0),
        cost_estimate=cost(chunks - down_cut, 2 * (chunks - half)),
        name="hidden_second",
    )(rows, gate_near, up_1, down, packed_far[0])

    table = jax.ShapeDtypeStruct((experts_all, total_tokens), jnp.float32)
    partial, probs, chosen = pl.pallas_call(
        with_accs(functools.partial(score_kernel, distances, top, (0, down_cut)), accs),
        out_shape=(
            jax.ShapeDtypeStruct((local_experts, total_tokens), jnp.float32),
            table,
            table,
        ),
        in_specs=[vmem] * (data_count + 4),
        out_specs=(vmem, vmem, vmem),
        scratch_shapes=[
            pltpu.VMEM((total_tokens, model_width + extra), jnp.bfloat16),
            pltpu.VMEM((local_experts, total_tokens, unit), jnp.float32),
        ]
       ,
        compiler_params=scoped(2 * row_bytes),
        cost_estimate=cost(0, chunks),
        name="scores",
    )(*packed_pieces, hidden_0, hidden_1, down_0, down_1)

    scores = partial
    distance = 1
    while distance < data_count:
        scores = scores + swap(scores, "dp", distance)
        distance *= 2
    distance = 1
    while 2 * distance < expert_count:
        rows_held = distance * local_experts
        scores = pl.pallas_call(
            functools.partial(join_kernel, distance),
            out_shape=jax.ShapeDtypeStruct((2 * rows_held, total_tokens), jnp.float32),
            in_specs=[vmem] * 2,
            out_specs=vmem,
            compiler_params=scoped(0),
            cost_estimate=cost(1, 1),
            name="join_scores",
        )(scores, swap(scores, "expert", distance))
        distance *= 2
    others = swap(scores, "expert", distance)

    logit_grad, router_grad = pl.pallas_call(
        functools.partial(gradient_kernel, distance),
        out_shape=(
            jax.ShapeDtypeStruct((tok_dev, experts_all), jnp.float32),
            jax.ShapeDtypeStruct((experts_all, model_width // data_count), jnp.float32),
        ),
        in_specs=[vmem] * 5,
        out_specs=(vmem, vmem),
        scratch_shapes=[pltpu.VMEM((total_tokens, experts_all), jnp.float32)],
        compiler_params=scoped(4 << 20),
        name="gradient",
    )(scores, others, probs, chosen, mine)
    return logit_grad, router_grad.T


def solution(mesh):
    placed = (
        P("dp", None),
        P("dp", None),
        P("dp", None),
        P("dp", None),
        P("expert", "dp", None),
        P("expert", "dp", None),
        P("expert", "dp", None),
    )
    mapped = jax.shard_map(
        per_device,
        mesh=mesh,
        in_specs=placed,
        out_specs=(P("dp", None), P("dp", None)),
        check_vma=False,
    )

    def run(*args):
        with jax.sharding.use_abstract_mesh(mesh.abstract_mesh):
            return mapped(*args)

    return run
```

time: 49.5 us -> 45.2 us (0.913)
  blocking collectives: 18.3 us -> 0 us
  waiting for transfers between devices: 2.25 us -> 10.4 us
  starting transfers between devices: 5.45 us -> 13.6 us
  Pallas kernels: 22.6 us -> 20.4 us
    all_to_all x2 -> x0, blocking collectives: 18.3 us -> none  [the longest x1 12.2 us: per_device(): lax.all_to_all(summed, 'expert', split_axis=0, concat_axis=0, tiled=True)]
    ppermute x6 -> x11, waiting for transfers between devices: 2.25 us -> 10.4 us  [swap(): lax.ppermute(value, axis, [(index, index ^ distance) for index in range(l...]
    ppermute x6 -> x11, starting transfers between devices: 5.45 us -> 13.6 us  [swap(): lax.ppermute(value, axis, [(index, index ^ distance) for index in range(l...]
    pallas_call x6, Pallas kernels: 18.1 us -> 15.9 us  [the longest x1 6.68 us: per_device(): pl.pallas_call(functools.partial(pack_load_kernel, plan), out_shape=(jax....]
  transfers between devices with their start and end apart: 6 -> 11, of which waited for: 1 -> 7; matrix products, arithmetic and copies ran while one was open for 0% -> 0% of each run, Pallas kernels for 36% -> 34%
where the time goes in v3:
time: 45.2 us; the launch traced here: 45 us
  Pallas kernels  20.4 us (45%)
  starting transfers between devices  13.6 us (30%)
  waiting for transfers between devices  10.4 us (23%)
  between operations  0.69 us (2%)
    ppermute x11, starting transfers between devices, swap(): lax.ppermute(value, axis, [(index, index ^ distance) for index in range(l...  13.6 us
    ppermute x11, waiting for transfers between devices, swap(): lax.ppermute(value, axis, [(index, index ^ distance) for index in range(l...  10.4 us
    pallas_call x1, Pallas kernels, per_device(): pl.pallas_call(functools.partial(pack_load_kernel, plan), out_shape=(jax....  6.68 us
    pallas_call x1, Pallas kernels, per_device(): pl.pallas_call(with_accs(functools.partial(first_hidden_kernel, distances...  4.46 us
    pallas_call x1, Pallas kernels, per_device(): pl.pallas_call(with_accs(functools.partial(second_hidden_kernel, plan), a...  4.36 us
    pallas_call x1, Pallas kernels, per_device(): pl.pallas_call(with_accs(functools.partial(score_kernel, distances, top,...  3.99 us
  transfers between devices with their start and end apart: 11, of which 7 were waited for; matrix products, arithmetic and copies ran while one was open for 0% of the time, Pallas kernels for 34%

profile of v3, /device:TPU:0, one launch (start us, length us, event | category | flops | bytes accessed | tf_op | source)
XLA Modules:
  0.0 45.0 jit_solution(13647968799596307338)
XLA Ops:
  0.6 0.5 %collective-permute-start = (bf16[32,4096]{1,0:T(8,128)(2,1)}, bf16[32,4096]{1,0:T(8,128)(2,1)S(1)}, u32[]{:S(2)}, u32[]{:S(2)}) collective-permute-start(bf16[32,4096]{1,0:T(8,128)(2,1)} %refs_0_.1), channel_id=1, source_target_pairs={{0,8},{8,0},{16,24},{24,16},{1,9},{9,1},{17,25},{25,17},{2,10},{10... | collective-permute-start | bytes 786440 | tf_op jit(solution)/shard_map/ppermute | solution.py:219
  1.1 2.6 %collective-permute-start.3 = (bf16[32,4096]{1,0:T(8,128)(2,1)}, bf16[32,4096]{1,0:T(8,128)(2,1)S(1)}, u32[]{:S(2)}, u32[]{:S(2)}) collective-permute-start(bf16[32,4096]{1,0:T(8,128)(2,1)} %refs_0_.1), channel_id=1, source_target_pairs={{0,16},{8,24},{16,0},{24,8},{1,17},{9,25},{17,1},{25,9},{2,18},{10... | collective-permute-start | bytes 786440 | tf_op jit(solution)/shard_map/ppermute | solution.py:219
  3.7 0.0 collective-permute-done.after.refs_1_
  3.7 6.7 %load_pack.1 = (bf16[32,4224]{1,0:T(8,128)(2,1)S(1)}, bf16[6,256,4096]{2,1,0:T(8,128)(2,1)S(1)}, bf16[3,256,4096]{2,1,0:T(8,128)(2,1)S(1)}) custom-call(f32[32,32]{1,0:T(8,128)} %logits.1, s32[8,32]{1,0:T(8,128)} %bitcast.10, bf16[32,4096]{1,0:T(8,128)(2,1)} %cotangent.1, bf16[6,256,4096]{2,1,0:T(8,128)(2,1)} %bitcast.9, bf16[6,256,4096]{2,1,0:T(8,128)(2,1)} %bitcast.5, ...), custom_call_target="tpu_custom_call" | custom-call | bytes 9 | tf_op jit(solution)/shard_map/load_pack/pallas_call | solution.py:268
  10.4 1.7 %collective-permute-start.2 = (bf16[32,4224]{1,0:T(8,128)(2,1)S(1)}, bf16[32,4224]{1,0:T(8,128)(2,1)S(1)}, u32[]{:S(2)}, u32[]{:S(2)}) collective-permute-start(bf16[32,4224]{1,0:T(8,128)(2,1)S(1)} %get-tuple-element.23.refs_0_), channel_id=1, source_target_pairs={{0,16},{8,24},{16,0},{24,8},{1,17},{9,25},{17,1},{25,9},{2,18},{10... | collective-permute-start | bytes 811016 | tf_op jit(solution)/shard_map/ppermute | solution.py:219
  12.2 0.0 collective-permute-start.4
  12.2 0.5 %collective-permute-start.1 = (bf16[32,4224]{1,0:T(8,128)(2,1)S(1)}, bf16[32,4224]{1,0:T(8,128)(2,1)S(1)}, u32[]{:S(2)}, u32[]{:S(2)}) collective-permute-start(bf16[32,4224]{1,0:T(8,128)(2,1)S(1)} %get-tuple-element.23.refs_0_), channel_id=1, source_target_pairs={{0,8},{8,0},{16,24},{24,16},{1,9},{9,1},{17,25},{25,17},{2,10},{10... | collective-permute-start | bytes 811016 | tf_op jit(solution)/shard_map/ppermute | solution.py:219
  12.7 1.0 %collective-permute-done.4.refs_3_ = bf16[32,4096]{1,0:T(8,128)(2,1)S(1)} collective-permute-done((bf16[32,4096]{1,0:T(8,128)(2,1)S(1)}, bf16[32,4096]{1,0:T(8,128)(2,1)S(1)}, u32[]{:S(2)}, u32[]{:S(2)}) %collective-permute-start.4) | collective-permute-done | bytes 262176 | tf_op jit(solution)/shard_map/ppermute | solution.py:219
  13.7 4.5 %hidden_first.1 = (f32[3,128,256]{2,1,0:T(8,128)S(1)}, bf16[128,1024]{1,0:T(8,128)(2,1)S(1)}, bf16[128,4096]{1,0:T(8,128)(2,1)S(1)}, bf16[3,256,4096]{2,1,0:T(8,128)(2,1)S(1)}, bf16[1,256,4096]{2,1,0:T(8,128)(2,1)S(1)}) custom-call(bf16[32,4096]{1,0:T(8,128)(2,1)S(1)} %copy-done, bf16[32,4096]{1,0:T(8,128)(2,1)S(1)} %collective-permute-done.after.refs_1_, ...), custom_call_target="tpu_custom_call" | custom-call | flops 6 | bytes 4 | tf_op jit(solution)/shard_map/hidden_first/pallas_call | solution.py:298
  18.2 0.9 %collective-permute-done.2.refs_4_.refs_2_ = bf16[32,4224]{1,0:T(8,128)(2,1)S(1)} collective-permute-done((bf16[32,4224]{1,0:T(8,128)(2,1)S(1)}, bf16[32,4224]{1,0:T(8,128)(2,1)S(1)}, u32[]{:S(2)}, u32[]{:S(2)}) %collective-permute-start.2) | collective-permute-done | bytes 270368 | tf_op jit(solution)/shard_map/ppermute | solution.py:219
  19.1 4.4 %hidden_second.1 = (f32[3,128,256]{2,1,0:T(8,128)S(1)}, bf16[5,256,4096]{2,1,0:T(8,128)(2,1)S(1)}) custom-call(bf16[128,4096]{1,0:T(8,128)(2,1)S(1)} %get-tuple-element.33.refs_0_, bf16[6,256,4096]{2,1,0:T(8,128)(2,1)S(1)} %get-tuple-element.27.refs_4_.refs_1_, bf16[3,256,4096]{2,1,0:T(8,128)(2,1)S(1)} %get-tuple-element.34.refs_2_, ...), custom_call_target="tpu_custom_call" | custom-call | flops 6 | bytes 5 | tf_op jit(solution)/shard_map/hidden_second/pallas_call | solution.py:321
  23.4 0.0 collective-permute-done.1.refs_1_
  23.5 4.0 %scores.1 = (f32[4,128]{1,0:T(4,128)S(1)}, f32[32,128]{1,0:T(8,128)S(1)}, f32[32,128]{1,0:T(8,128)S(1)}) custom-call(bf16[32,4224]{1,0:T(8,128)(2,1)S(1)} %get-tuple-element.23.refs_0_, bf16[32,4224]{1,0:T(8,128)(2,1)S(1)} %collective-permute-done.1.refs_1_, bf16[32,4224]{1,0:T(8,128)(2,1)S(1)} %collective-permute-done.2.refs_4_.refs_2_, ...), custom_call_target="tpu_custom_call" | custom-call | flops 6 | tf_op jit(solution)/shard_map/scores/pallas_call | solution.py:336
  27.4 0.6 %collective-permute-start.6 = (f32[4,128]{1,0:T(4,128)S(1)}, f32[4,128]{1,0:T(4,128)S(1)}, u32[]{:S(2)}, u32[]{:S(2)}) collective-permute-start(f32[4,128]{1,0:T(4,128)S(1)} %get-tuple-element.38), channel_id=1, source_target_pairs={{0,8},{8,0},{16,24},{24,16},{1,9},{9,1},{17,25},{25,17},{2,10},{10... | collective-permute-start | bytes 6152 | tf_op jit(solution)/shard_map/ppermute | solution.py:219
  28.0 0.8 %collective-permute-done.6 = f32[4,128]{1,0:T(4,128)S(1)} collective-permute-done((f32[4,128]{1,0:T(4,128)S(1)}, f32[4,128]{1,0:T(4,128)S(1)}, u32[]{:S(2)}, u32[]{:S(2)}) %collective-permute-start.6) | collective-permute-done | bytes 2080 | tf_op jit(solution)/shard_map/ppermute | solution.py:219
  28.8 1.6 %collective-permute-start.7 = (f32[4,128]{1,0:T(4,128)S(1)}, f32[4,128]{1,0:T(4,128)S(1)}, u32[]{:S(2)}, u32[]{:S(2)}) collective-permute-start(f32[4,128]{1,0:T(4,128)S(1)} %add.6), channel_id=1, source_target_pairs={{0,16},{8,24},{16,0},{24,8},{1,17},{9,25},{17,1},{25,9},{2,18},{10... | collective-permute-start | bytes 6152 | tf_op jit(solution)/shard_map/ppermute | solution.py:219
  30.5 1.9 %collective-permute-done.7 = f32[4,128]{1,0:T(4,128)S(1)} collective-permute-done((f32[4,128]{1,0:T(4,128)S(1)}, f32[4,128]{1,0:T(4,128)S(1)}, u32[]{:S(2)}, u32[]{:S(2)}) %collective-permute-start.7) | collective-permute-done | bytes 2080 | tf_op jit(solution)/shard_map/ppermute | solution.py:219
  32.4 1.6 %collective-permute-start.8 = (f32[4,128]{1,0:T(4,128)S(1)}, f32[4,128]{1,0:T(4,128)S(1)}, u32[]{:S(2)}, u32[]{:S(2)}) collective-permute-start(f32[4,128]{1,0:T(4,128)S(1)} %add.7.held), channel_id=1, source_target_pairs={{0,1},{1,0},{2,3},{3,2},{4,5},{5,4},{6,7},{7,6},{8,9},{9,8},{10,11... | collective-permute-start | bytes 6152 | tf_op jit(solution)/shard_map/ppermute | solution.py:219
  34.0 2.0 %collective-permute-done.8.other = f32[4,128]{1,0:T(4,128)S(1)} collective-permute-done((f32[4,128]{1,0:T(4,128)S(1)}, f32[4,128]{1,0:T(4,128)S(1)}, u32[]{:S(2)}, u32[]{:S(2)}) %collective-permute-start.8) | collective-permute-done | bytes 2080 | tf_op jit(solution)/shard_map/ppermute | solution.py:219
  36.0 1.7 %collective-permute-start.9 = (f32[8,128]{1,0:T(8,128)S(1)}, f32[8,128]{1,0:T(8,128)S(1)}, u32[]{:S(2)}, u32[]{:S(2)}) collective-permute-start(f32[8,128]{1,0:T(8,128)S(1)} %join_scores.2.held), channel_id=1, source_target_pairs={{0,2},{1,3},{2,0},{3,1},{4,6},{5,7},{6,4},{7,5},{8,10},{9,11},{10,... | collective-permute-start | bytes 12296 | tf_op jit(solution)/shard_map/ppermute | solution.py:219
  37.7 1.9 %collective-permute-done.9.other = f32[8,128]{1,0:T(8,128)S(1)} collective-permute-done((f32[8,128]{1,0:T(8,128)S(1)}, f32[8,128]{1,0:T(8,128)S(1)}, u32[]{:S(2)}, u32[]{:S(2)}) %collective-permute-start.9) | collective-permute-done | bytes 4128 | tf_op jit(solution)/shard_map/ppermute | solution.py:219
  39.6 2.7 %collective-permute-start.10 = (f32[16,128]{1,0:T(8,128)S(1)}, f32[16,128]{1,0:T(8,128)S(1)}, u32[]{:S(2)}, u32[]{:S(2)}) collective-permute-start(f32[16,128]{1,0:T(8,128)S(1)} %join_scores.3.held), channel_id=1, source_target_pairs={{0,4},{1,5},{2,6},{3,7},{4,0},{5,1},{6,2},{7,3},{8,12},{9,13},{10,... | collective-permute-start | bytes 24584 | tf_op jit(solution)/shard_map/ppermute | solution.py:219
  42.3 1.8 %collective-permute-done.10.other = f32[16,128]{1,0:T(8,128)S(1)} collective-permute-done((f32[16,128]{1,0:T(8,128)S(1)}, f32[16,128]{1,0:T(8,128)S(1)}, u32[]{:S(2)}, u32[]{:S(2)}) %collective-permute-start.10) | collective-permute-done | bytes 8224 | tf_op jit(solution)/shard_map/ppermute | solution.py:219
  44.2 0.8 %gradient.1 = (f32[32,32]{1,0:T(8,128)}, f32[32,1024]{1,0:T(8,128)}) custom-call(f32[16,128]{1,0:T(8,128)S(1)} %join_scores.3.held, f32[16,128]{1,0:T(8,128)S(1)} %collective-permute-done.10.other, f32[32,128]{1,0:T(8,128)S(1)} %get-tuple-element.39.probs_ref, f32[32,128]{1,0:T(8,128)S(1)} %get-tuple-element.40.chosen_ref, ...), custom_call_target="tpu_custom_call" | custom-call | tf_op jit(solution)/shard_map/gradient/pallas_call | solution.py:375
  (9 shorter events, 0.0 us)
Async XLA Ops:
  0.6 3.1 %collective-permute-start = (bf16[32,4096]{1,0:T(8,128)(2,1)}, bf16[32,4096]{1,0:T(8,128)(2,1)S(1)}, u32[]{:S(2)}, u32[]{:S(2)}) collective-permute-start(bf16[32,4096]{1,0:T(8,128)(2,1)} %refs_0_.1), channel_id=1, source_target_pairs={{0,8},{8,0},{16,24},{24,16},{1,9},{9,1},{17,25},{25,17},{2,10},{10... | collective-permute-start | bytes 786440 | tf_op jit(solution)/shard_map/ppermute | solution.py:219
  1.1 11.0 %collective-permute-start.3 = (bf16[32,4096]{1,0:T(8,128)(2,1)}, bf16[32,4096]{1,0:T(8,128)(2,1)S(1)}, u32[]{:S(2)}, u32[]{:S(2)}) collective-permute-start(bf16[32,4096]{1,0:T(8,128)(2,1)} %refs_0_.1), channel_id=1, source_target_pairs={{0,16},{8,24},{16,0},{24,8},{1,17},{9,25},{17,1},{25,9},{2,18},{10... | collective-permute-start | bytes 786440 | tf_op jit(solution)/shard_map/ppermute | solution.py:219
  3.7 10.0 %copy-start = (bf16[32,4096]{1,0:T(8,128)(2,1)S(1)}, bf16[32,4096]{1,0:T(8,128)(2,1)}, u32[]{:S(2)}) copy-start(bf16[32,4096]{1,0:T(8,128)(2,1)} %refs_0_.1) | copy-start | bytes 786436
  10.4 8.6 %collective-permute-start.2 = (bf16[32,4224]{1,0:T(8,128)(2,1)S(1)}, bf16[32,4224]{1,0:T(8,128)(2,1)S(1)}, u32[]{:S(2)}, u32[]{:S(2)}) collective-permute-start(bf16[32,4224]{1,0:T(8,128)(2,1)S(1)} %get-tuple-element.23.refs_0_), channel_id=1, source_target_pairs={{0,16},{8,24},{16,0},{24,8},{1,17},{9,25},{17,1},{25,9},{2,18},{10... | collective-permute-start | bytes 811016 | tf_op jit(solution)/shard_map/ppermute | solution.py:219
  12.2 1.5 %collective-permute-start.4 = (bf16[32,4096]{1,0:T(8,128)(2,1)S(1)}, bf16[32,4096]{1,0:T(8,128)(2,1)S(1)}, u32[]{:S(2)}, u32[]{:S(2)}) collective-permute-start(bf16[32,4096]{1,0:T(8,128)(2,1)S(1)} %collective-permute-done.3.refs_2_), channel_id=1, source_target_pairs={{0,8},{8,0},{16,24},{24,16},{1,9},{9,1},{17,25},{25,17},{2,10},{10... | collective-permute-start | bytes 786440 | tf_op jit(solution)/shard_map/ppermute | solution.py:219
  12.2 11.3 %collective-permute-start.1 = (bf16[32,4224]{1,0:T(8,128)(2,1)S(1)}, bf16[32,4224]{1,0:T(8,128)(2,1)S(1)}, u32[]{:S(2)}, u32[]{:S(2)}) collective-permute-start(bf16[32,4224]{1,0:T(8,128)(2,1)S(1)} %get-tuple-element.23.refs_0_), channel_id=1, source_target_pairs={{0,8},{8,0},{16,24},{24,16},{1,9},{9,1},{17,25},{25,17},{2,10},{10... | collective-permute-start | bytes 811016 | tf_op jit(solution)/shard_map/ppermute | solution.py:219
  19.1 4.4 %collective-permute-start.5 = (bf16[32,4224]{1,0:T(8,128)(2,1)S(1)}, bf16[32,4224]{1,0:T(8,128)(2,1)S(1)}, u32[]{:S(2)}, u32[]{:S(2)}) collective-permute-start(bf16[32,4224]{1,0:T(8,128)(2,1)S(1)} %collective-permute-done.2.refs_4_.refs_2_), channel_id=1, source_target_pairs={{0,8},{8,0},{16,24},{24,16},{1,9},{9,1},{17,25},{25,17},{2,10},{10... | collective-permute-start | bytes 811016 | tf_op jit(solution)/shard_map/ppermute | solution.py:219
  27.4 1.4 %collective-permute-start.6 = (f32[4,128]{1,0:T(4,128)S(1)}, f32[4,128]{1,0:T(4,128)S(1)}, u32[]{:S(2)}, u32[]{:S(2)}) collective-permute-start(f32[4,128]{1,0:T(4,128)S(1)} %get-tuple-element.38), channel_id=1, source_target_pairs={{0,8},{8,0},{16,24},{24,16},{1,9},{9,1},{17,25},{25,17},{2,10},{10... | collective-permute-start | bytes 6152 | tf_op jit(solution)/shard_map/ppermute | solution.py:219
  28.8 3.6 %collective-permute-start.7 = (f32[4,128]{1,0:T(4,128)S(1)}, f32[4,128]{1,0:T(4,128)S(1)}, u32[]{:S(2)}, u32[]{:S(2)}) collective-permute-start(f32[4,128]{1,0:T(4,128)S(1)} %add.6), channel_id=1, source_target_pairs={{0,16},{8,24},{16,0},{24,8},{1,17},{9,25},{17,1},{25,9},{2,18},{10... | collective-permute-start | bytes 6152 | tf_op jit(solution)/shard_map/ppermute | solution.py:219
  32.4 3.6 %collective-permute-start.8 = (f32[4,128]{1,0:T(4,128)S(1)}, f32[4,128]{1,0:T(4,128)S(1)}, u32[]{:S(2)}, u32[]{:S(2)}) collective-permute-start(f32[4,128]{1,0:T(4,128)S(1)} %add.7.held), channel_id=1, source_target_pairs={{0,1},{1,0},{2,3},{3,2},{4,5},{5,4},{6,7},{7,6},{8,9},{9,8},{10,11... | collective-permute-start | bytes 6152 | tf_op jit(solution)/shard_map/ppermute | solution.py:219
  36.0 3.6 %collective-permute-start.9 = (f32[8,128]{1,0:T(8,128)S(1)}, f32[8,128]{1,0:T(8,128)S(1)}, u32[]{:S(2)}, u32[]{:S(2)}) collective-permute-start(f32[8,128]{1,0:T(8,128)S(1)} %join_scores.2.held), channel_id=1, source_target_pairs={{0,2},{1,3},{2,0},{3,1},{4,6},{5,7},{6,4},{7,5},{8,10},{9,11},{10,... | collective-permute-start | bytes 12296 | tf_op jit(solution)/shard_map/ppermute | solution.py:219
  39.6 4.5 %collective-permute-start.10 = (f32[16,128]{1,0:T(8,128)S(1)}, f32[16,128]{1,0:T(8,128)S(1)}, u32[]{:S(2)}, u32[]{:S(2)}) collective-permute-start(f32[16,128]{1,0:T(8,128)S(1)} %join_scores.3.held), channel_id=1, source_target_pairs={{0,4},{1,5},{2,6},{3,7},{4,0},{5,1},{6,2},{7,3},{8,12},{9,13},{10,... | collective-permute-start | bytes 24584 | tf_op jit(solution)/shard_map/ppermute | solution.py:219

commit v4 on v3

v4 whole, which is shorter than its diff:
```python
import functools

import jax
import jax.numpy as jnp
from jax import lax
from jax.experimental import pallas as pl
from jax.experimental.pallas import tpu as pltpu
from jax.sharding import PartitionSpec as P

CORES = 2


def dot_rows(a, b):
    return lax.dot_general(a, b, (((1,), (1,)), ((), ())), preferred_element_type=jnp.float32)


def stream_dots(rows, lanes, accs, finish):
    places = len(lanes[0])
    if not accs:
        for place in range(places):
            finish(place, [dot_rows(lane[place][...], rows[...]) for lane in lanes])
        return
    total_tokens, edge = rows.shape[0], accs[0][0].shape[1]
    steps = rows.shape[1] // edge

    def push(step):
        part = rows[:, step * edge : (step + 1) * edge]
        both = jnp.concatenate([part] * (edge // total_tokens), axis=0)
        for unit in range(len(lanes)):
            pltpu.matmul_push_rhs(both, step % 2, unit, transpose=True)

    push(0)
    for step in range(steps):
        for place in range(places):
            for lane, acc in zip(lanes, accs):
                part = lane[place][:, step * edge : (step + 1) * edge]
                pltpu.matmul_acc_lhs(acc[place], part, load_staged_rhs=step % 2 if place == 0 else None)
            if place == 0 and step + 1 < steps:
                push(step + 1)
    for place in range(places):
        finish(place, [pltpu.matmul_pop(acc[place])[:, :total_tokens] for acc in accs])


def with_accs(kernel, shapes):
    if not shapes:
        return kernel
    half = len(shapes) // 2

    def body(*refs):
        pl.run_scoped(lambda *accs: kernel(*refs, accs=(accs[:half], accs[half:])), *shapes)

    return body


def place_rows(pieces, distances, rows):
    me = lax.axis_index("dp")
    tok_dev = pieces[0].shape[0]
    for piece, distance in zip(pieces, distances):
        start = pl.multiple_of(jnp.bitwise_xor(me, distance) * tok_dev, tok_dev)
        rows[pl.ds(start, tok_dev), :] = piece[...]


def start_loads(plan, sources, nears, sems):
    copies, number = [], 0
    for (first, last), source, near in zip(plan, sources, nears):
        for chunk in range(first, last):
            copies.append(pltpu.make_async_copy(source.at[chunk], near.at[chunk - first], sems.at[number]))
            number += 1
    for copy in copies:
        copy.start()
    return copies


def pack_kernel(logits, routes, cotangent, packed, logits_near, routes_near, columns, sems):
    model_width = cotangent.shape[1]
    copies = [
        pltpu.make_async_copy(logits, logits_near, sems.at[0]),
        pltpu.make_async_copy(routes, routes_near, sems.at[1]),
        pltpu.make_async_copy(cotangent, packed.at[:, :model_width], sems.at[2]),
    ]
    for copy in copies:
        copy.start()
    columns[...] = jnp.zeros(columns.shape, jnp.float32)
    copies[0].wait()
    left = logits_near[...]
    experts_all = left.shape[1]
    for term in range(3):
        rounded = left.astype(jnp.bfloat16).astype(jnp.float32)
        columns[:, term * experts_all : (term + 1) * experts_all] = rounded
        left = left - rounded
    copies[1].wait()
    columns[:, 3 * experts_all : 3 * experts_all + routes.shape[0]] = routes_near[...].astype(jnp.float32).T
    packed[:, model_width:] = columns[...].astype(jnp.bfloat16)
    copies[2].wait()


def load_kernel(plan, gate, up, after, gate_near, up_near, sems):
    for copy in start_loads(plan, [gate, up], [gate_near, up_near], sems):
        copy.wait()


def blocks_of(buffers, unit):
    return [
        buffer.at[chunk, first : first + unit]
        for buffer in buffers
        for chunk in range(buffer.shape[0])
        for first in range(0, buffer.shape[1], unit)
    ]


def gated(dots):
    gate_pre, up_pre = dots
    return gate_pre / (1.0 + jnp.exp(-gate_pre)) * up_pre


def first_hidden_kernel(distances, plan, *refs, accs=()):
    count = len(distances)
    pieces, refs = refs[:count], refs[count:]
    gate, up, up_far, down_far, hidden, mine, rows, up_near, down_near, sems, mine_sem = refs
    loads = start_loads(plan, [up_far, down_far], [up_near, down_near], sems)
    place_rows(pieces, distances, rows)
    width = mine.shape[1]
    start = pl.multiple_of(lax.axis_index("dp") * width, width)
    own = pltpu.make_async_copy(rows.at[:, pl.ds(start, width)], mine, mine_sem)
    own.start()
    places, unit = hidden.shape[:2]
    lanes = [blocks_of([gate], unit)[:places], blocks_of([up], unit)]

    def finish(place, dots):
        hidden[place] = gated(dots)

    stream_dots(rows, lanes, accs, finish)
    own.wait()
    for copy in loads:
        copy.wait()


def second_hidden_kernel(plan, rows, gate, up, down_far, after, hidden, down_near, sems, accs=()):
    loads = start_loads(plan, [down_far], [down_near], sems)
    places, unit = hidden.shape[:2]
    lanes = [blocks_of([gate], unit)[-places:], blocks_of([up], unit)]

    def finish(place, dots):
        hidden[place] = gated(dots)

    stream_dots(rows, lanes, accs, finish)
    for copy in loads:
        copy.wait()


def score_kernel(distances, top, *refs, accs=()):
    count = len(distances)
    pieces, refs = refs[:count], refs[count:]
    hidden_0, hidden_1, down_0, down_1, partial, probs, chosen, rows = refs
    model_width = down_0.shape[2]
    experts_all = probs.shape[0]
    place_rows(pieces, distances, rows)
    local_experts = partial.shape[1]
    unit = hidden_0.shape[1]
    blocks = blocks_of([down_0, down_1], unit)
    places = len(blocks) // 2
    per_expert = len(blocks) // local_experts
    sums = [None] * local_experts

    def routing():
        packed = rows[:, model_width:].astype(jnp.float32).T
        terms = [packed[term * experts_all : (term + 1) * experts_all] for term in range(3)]
        logits = terms[0] + terms[1] + terms[2]
        raised = jnp.exp(logits - jnp.max(logits, axis=0, keepdims=True))
        probs[...] = raised / jnp.sum(raised, axis=0, keepdims=True)
        number = lax.broadcasted_iota(jnp.int32, logits.shape, 0).astype(jnp.float32)
        named = jnp.zeros(logits.shape, jnp.float32)
        for slot in range(3 * experts_all, 3 * experts_all + top):
            named = named + (packed[slot : slot + 1] == number).astype(jnp.float32)
        chosen[...] = named

    def finish(place, dots):
        for held, block, paired in zip((hidden_0, hidden_1), (place, places + place), dots):
            product = held[place] * paired
            expert = block // per_expert
            sums[expert] = product if sums[expert] is None else sums[expert] + product

    routing()
    stream_dots(rows.at[:, :model_width], [blocks[:places], blocks[places:]], accs, finish)
    lines = [jnp.sum(term, axis=0, keepdims=True) for term in sums]
    partial[...] = jnp.broadcast_to(jnp.concatenate(lines, axis=0)[None], partial.shape)


def gradient_kernel(data_count, blocks, probs_ref, chosen_ref, mine, logit_grad, router_grad, grads):
    experts_all, total_tokens = probs_ref.shape
    scores = jnp.sum(blocks[...].reshape((data_count, experts_all, total_tokens)), axis=0)
    probs, chosen = probs_ref[...], chosen_ref[...]
    mass = jnp.sum(probs * chosen, axis=0, keepdims=True)
    weighted = jnp.sum(probs * chosen * scores, axis=0, keepdims=True)
    prob_grad = scores / mass - chosen * weighted / (mass * mass)
    grad = probs * (prob_grad - jnp.sum(probs * prob_grad, axis=0, keepdims=True))
    router_grad[...] = jnp.dot(grad.astype(jnp.bfloat16), mine[...], preferred_element_type=jnp.float32)
    grads[...] = grad.T
    tok_dev = logit_grad.shape[0]
    logit_grad[...] = grads[pl.ds(pl.multiple_of(lax.axis_index("dp") * tok_dev, tok_dev), tok_dev), :]


def swap(value, axis, distance):
    return lax.ppermute(value, axis, [(index, index ^ distance) for index in range(lax.axis_size(axis))])


def per_device(tokens, cotangent, logits, routes, gate_weight, up_weight, down_weight):
    data_count = lax.axis_size("dp")
    expert_count = lax.axis_size("expert")
    tok_dev, model_width = tokens.shape
    local_experts, ff_dev = gate_weight.shape[:2]
    total_tokens = tok_dev * data_count
    experts_all = local_experts * expert_count
    top = routes.shape[1]
    unit = 128 if ff_dev % 128 == 0 else ff_dev
    units = local_experts * ff_dev // unit
    chunk_rows = unit * (2 if unit == 128 and units % 2 == 0 else 1)
    chunks = local_experts * ff_dev // chunk_rows
    extra = -(-(3 * experts_all + top) // 128) * 128
    chips = data_count // CORES
    distances = [chip * CORES + core for chip in range(chips) for core in range(CORES)]
    half = chunks // 2
    down_cut = max(1, chunks // 6)

    vmem = pl.BlockSpec(memory_space=pltpu.VMEM)
    hbm = pl.BlockSpec(memory_space=pltpu.HBM)
    anywhere = pl.BlockSpec(memory_space=pl.ANY)
    row_bytes = total_tokens * model_width * 2

    def keep_far(value):
        return pltpu.with_memory_space_constraint(value, pltpu.HBM)

    def near(first, last):
        return pltpu.VMEM((last - first, chunk_rows, model_width), jnp.bfloat16)

    def roomy():
        return scoped(0 if accs else 2 * row_bytes)

    def cost(loads, dots):
        return pl.CostEstimate(flops=dots, bytes_accessed=loads, transcendentals=0)

    def scoped(size):
        return pltpu.CompilerParams(vmem_limit_bytes=size + (2 << 20))

    edge = pltpu.get_tpu_info().mxu_column_size
    accs = []
    places = half * chunk_rows // unit
    if edge == 2 * total_tokens and model_width % edge == 0 and 2 * half == chunks and places * unit <= 1024:
        accs = [pltpu.ACC(number)((unit, edge), jnp.float32) for number in range(2) for _ in range(places)]
    cut = (chunks, chunk_rows, model_width)
    gate, up, down = (keep_far(weight.reshape(cut)) for weight in (gate_weight, up_weight, down_weight))

    tokens_beside = swap(tokens, "dp", 1)
    tokens_far = [swap(tokens, "dp", chip * CORES) for chip in range(1, chips)]
    packed = pl.pallas_call(
        pack_kernel,
        out_shape=jax.ShapeDtypeStruct((tok_dev, model_width + extra), jnp.bfloat16),
        in_specs=[hbm] * 3,
        out_specs=vmem,
        scratch_shapes=[
            pltpu.VMEM((tok_dev, experts_all), jnp.float32),
            pltpu.VMEM((top, tok_dev), jnp.int32),
            pltpu.VMEM((tok_dev, extra), jnp.float32),
            pltpu.SemaphoreType.DMA((3,)),
        ],
        compiler_params=scoped(0),
        cost_estimate=cost(1, 0),
        name="pack",
    )(keep_far(logits), keep_far(routes.T), keep_far(cotangent))
    packed_far = [swap(packed, "dp", chip * CORES) for chip in range(1, chips)]
    packed_beside = swap(packed, "dp", 1)
    plan = [(0, chunks), (0, half)]
    gate_near, up_0 = pl.pallas_call(
        functools.partial(load_kernel, plan),
        out_shape=(near(*plan[0]), near(*plan[1])),
        in_specs=[hbm, hbm, anywhere],
        out_specs=(vmem, vmem),
        scratch_shapes=[pltpu.SemaphoreType.DMA((chunks + half,))],
        compiler_params=scoped(0),
        cost_estimate=cost(chunks + half, 0),
        name="load",
    )(gate, up, packed)

    tokens_far, gate_near, up_0 = lax.optimization_barrier((tokens_far, gate_near, up_0))
    token_pieces = [tokens, tokens_beside]
    for far in tokens_far:
        token_pieces += [far, swap(far, "dp", 1)]

    plan = [(half, chunks), (0, down_cut)]
    loads = sum(last - first for first, last in plan)
    hidden_0, mine, rows, up_1, down_0 = pl.pallas_call(
        with_accs(functools.partial(first_hidden_kernel, distances, plan), accs),
        out_shape=(
            jax.ShapeDtypeStruct((places, unit, total_tokens), jnp.float32),
            jax.ShapeDtypeStruct((total_tokens, model_width // data_count), jnp.bfloat16),
            jax.ShapeDtypeStruct((total_tokens, model_width), jnp.bfloat16),
            near(*plan[0]),
            near(*plan[1]),
        ),
        in_specs=[vmem] * (data_count + 2) + [hbm] * 2,
        out_specs=(vmem,) * 5,
        scratch_shapes=[pltpu.SemaphoreType.DMA((loads,)), pltpu.SemaphoreType.DMA],
        compiler_params=roomy(),
        cost_estimate=cost(loads, 2 * half),
        name="hidden_first",
    )(*token_pieces, gate_near, up_0, up, down)

    packed_far, hidden_0, rows = lax.optimization_barrier((packed_far, hidden_0, rows))
    packed_pieces = [packed, packed_beside]
    for far in packed_far:
        packed_pieces += [far, swap(far, "dp", 1)]

    plan = [(down_cut, chunks)]
    hidden_1, down_1 = pl.pallas_call(
        with_accs(functools.partial(second_hidden_kernel, plan), accs),
        out_shape=(
            jax.ShapeDtypeStruct((units - places, unit, total_tokens), jnp.float32),
            near(*plan[0]),
        ),
        in_specs=[vmem] * 3 + [hbm, anywhere],
        out_specs=(vmem, vmem),
        scratch_shapes=[pltpu.SemaphoreType.DMA((chunks - down_cut,))],
        compiler_params=roomy(),
        cost_estimate=cost(chunks - down_cut, 2 * (chunks - half)),
        name="hidden_second",
    )(rows, gate_near, up_1, down, packed_far[0])

    table = jax.ShapeDtypeStruct((experts_all, total_tokens), jnp.float32)
    partial, probs, chosen = pl.pallas_call(
        with_accs(functools.partial(score_kernel, distances, top), accs),
        out_shape=(
            jax.ShapeDtypeStruct((data_count * expert_count, local_experts, total_tokens), jnp.float32),
            table,
            table,
        ),
        in_specs=[vmem] * (data_count + 4),
        out_specs=(vmem, vmem, vmem),
        scratch_shapes=[
            pltpu.VMEM((total_tokens, model_width + extra), jnp.bfloat16),
        ]
       ,
        compiler_params=scoped(2 * row_bytes),
        cost_estimate=cost(0, chunks),
        name="scores",
    )(*packed_pieces, hidden_0, hidden_1, down_0, down_1)

    score_blocks = lax.all_to_all(partial, ("dp", "expert"), split_axis=0, concat_axis=0, tiled=True)

    logit_grad, router_grad = pl.pallas_call(
        functools.partial(gradient_kernel, data_count),
        out_shape=(
            jax.ShapeDtypeStruct((tok_dev, experts_all), jnp.float32),
            jax.ShapeDtypeStruct((experts_all, model_width // data_count), jnp.float32),
        ),
        in_specs=[vmem] * 4,
        out_specs=(vmem, vmem),
        scratch_shapes=[pltpu.VMEM((total_tokens, experts_all), jnp.float32)],
        compiler_params=scoped(4 << 20),
        name="gradient",
    )(score_blocks, probs, chosen, mine)
    return logit_grad, router_grad.T


def solution(mesh):
    placed = (
        P("dp", None),
        P("dp", None),
        P("dp", None),
        P("dp", None),
        P("expert", "dp", None),
        P("expert", "dp", None),
        P("expert", "dp", None),
    )
    mapped = jax.shard_map(
        per_device,
        mesh=mesh,
        in_specs=placed,
        out_specs=(P("dp", None), P("dp", None)),
        check_vma=False,
    )

    def run(*args):
        with jax.sharding.use_abstract_mesh(mesh.abstract_mesh):
            return mapped(*args)

    return run
```

time: 45.2 us -> 41.1 us (0.909)
  blocking collectives: 0 us -> 13.4 us
  starting transfers between devices: 13.6 us -> 4.25 us
  waiting for transfers between devices: 10.4 us -> 1.09 us
  Pallas kernels: 20.4 us -> 21.4 us
    all_to_all x0 -> x1, blocking collectives: none -> 13.4 us  [per_device(): lax.all_to_all(partial, ('dp', 'expert'), split_axis=0, concat_axis=0, ti...]
    ppermute x11 -> x6, waiting for transfers between devices: 10.4 us -> 1.09 us  [swap(): lax.ppermute(value, axis, [(index, index ^ distance) for index in range(l...]
    ppermute x11 -> x6, starting transfers between devices: 13.6 us -> 4.25 us  [swap(): lax.ppermute(value, axis, [(index, index ^ distance) for index in range(l...]
    pallas_call x1, Pallas kernels: 4.36 us -> 5.81 us  [per_device(): pl.pallas_call(with_accs(functools.partial(second_hidden_kernel, plan), a...]
    pallas_call x1, Pallas kernels: 4.46 us -> 3.61 us  [per_device(): pl.pallas_call(with_accs(functools.partial(first_hidden_kernel, distances...]
    pallas_call x5 -> x4, Pallas kernels: 11.5 us -> 12 us  [the longest x1 6.56 us: per_device(): pl.pallas_call(functools.partial(load_kernel, plan), out_shape=(near(*pla...]
  transfers between devices with their start and end apart: 11 -> 6, of which waited for: 7 -> 1; matrix products, arithmetic and copies ran while one was open for 0% -> 0% of each run, Pallas kernels for 34% -> 42%
where the time goes in v4:
time: 41.1 us; the launch traced here: 40.8 us
  Pallas kernels  21.4 us (52%)
  blocking collectives  13.4 us (33%)
  starting transfers between devices  4.25 us (10%)
  waiting for transfers between devices  1.09 us (3%)
  between operations  0.72 us (2%)
    all_to_all x1, blocking collectives, per_device(): lax.all_to_all(partial, ('dp', 'expert'), split_axis=0, concat_axis=0, ti...  13.4 us
    pallas_call x1, Pallas kernels, per_device(): pl.pallas_call(functools.partial(load_kernel, plan), out_shape=(near(*pla...  6.56 us
    pallas_call x1, Pallas kernels, per_device(): pl.pallas_call(with_accs(functools.partial(second_hidden_kernel, plan), a...  5.81 us
    ppermute x6, starting transfers between devices, swap(): lax.ppermute(value, axis, [(index, index ^ distance) for index in range(l...  4.25 us
    pallas_call x1, Pallas kernels, per_device(): pl.pallas_call(with_accs(functools.partial(first_hidden_kernel, distances...  3.61 us
    pallas_call x1, Pallas kernels, per_device(): pl.pallas_call(with_accs(functools.partial(score_kernel, distances, top),...  3.55 us
    ppermute x6, waiting for transfers between devices, swap(): lax.ppermute(value, axis, [(index, index ^ distance) for index in range(l...  1.09 us
    pallas_call x1, Pallas kernels, per_device(): pl.pallas_call(pack_kernel, out_shape=jax.ShapeDtypeStruct((tok_dev, mode...  1.01 us
  transfers between devices with their start and end apart: 6, of which 1 were waited for; matrix products, arithmetic and copies ran while one was open for 0% of the time, Pallas kernels for 42%

profile of v4, /device:TPU:0, one launch (start us, length us, event | category | flops | bytes accessed | tf_op | source)
XLA Modules:
  0.0 40.8 jit_solution(3455127898009779561)
XLA Ops:
  0.6 3.0 %collective-permute-start.3 = (bf16[32,4096]{1,0:T(8,128)(2,1)}, bf16[32,4096]{1,0:T(8,128)(2,1)S(1)}, u32[]{:S(2)}, u32[]{:S(2)}) collective-permute-start(bf16[32,4096]{1,0:T(8,128)(2,1)} %refs_0_.1), channel_id=1, source_target_pairs={{0,16},{8,24},{16,0},{24,8},{1,17},{9,25},{17,1},{25,9},{2,18},{10... | collective-permute-start | bytes 786440 | tf_op jit(solution)/shard_map/ppermute | solution.py:204
  3.7 1.0 %pack.1.after.refs_0_ = bf16[32,4224]{1,0:T(8,128)(2,1)S(1)} custom-call(f32[32,32]{1,0:T(8,128)} %logits.1, s32[8,32]{1,0:T(8,128)} %bitcast.10, bf16[32,4096]{1,0:T(8,128)(2,1)} %cotangent.1), custom_call_target="tpu_custom_call" | custom-call | bytes 1 | tf_op jit(solution)/shard_map/pack/pallas_call | solution.py:255
  4.7 0.1 collective-permute-start.1
  4.8 0.1 collective-permute-start.2
  4.8 0.0 copy-start
  4.8 6.6 %load.1 = (bf16[6,256,4096]{2,1,0:T(8,128)(2,1)S(1)}, bf16[3,256,4096]{2,1,0:T(8,128)(2,1)S(1)}) custom-call(bf16[6,256,4096]{2,1,0:T(8,128)(2,1)} %bitcast.9, bf16[6,256,4096]{2,1,0:T(8,128)(2,1)} %bitcast.5, bf16[32,4224]{1,0:T(8,128)(2,1)S(1)} %pack.1.after.refs_0_), custom_call_target="tpu_custom_call" | custom-call | bytes 9 | tf_op jit(solution)/shard_map/load/pallas_call | solution.py:273
  11.4 0.0 collective-permute-done.3.refs_2_
  11.4 0.5 %collective-permute-start.4 = (bf16[32,4096]{1,0:T(8,128)(2,1)S(1)}, bf16[32,4096]{1,0:T(8,128)(2,1)S(1)}, u32[]{:S(2)}, u32[]{:S(2)}) collective-permute-start(bf16[32,4096]{1,0:T(8,128)(2,1)S(1)} %collective-permute-done.3.refs_2_), channel_id=1, source_target_pairs={{0,8},{8,0},{16,24},{24,16},{1,9},{9,1},{17,25},{25,17},{2,10},{10... | collective-permute-start | bytes 786440 | tf_op jit(solution)/shard_map/ppermute | solution.py:204
  12.0 0.1 collective-permute-start
  12.1 0.0 collective-permute-done.2.refs_1_
  12.1 1.1 %collective-permute-done.4.refs_3_ = bf16[32,4096]{1,0:T(8,128)(2,1)S(1)} collective-permute-done((bf16[32,4096]{1,0:T(8,128)(2,1)S(1)}, bf16[32,4096]{1,0:T(8,128)(2,1)S(1)}, u32[]{:S(2)}, u32[]{:S(2)}) %collective-permute-start.4) | collective-permute-done | bytes 262176 | tf_op jit(solution)/shard_map/ppermute | solution.py:204
  13.1 0.0 copy-done
  13.1 3.6 %hidden_first.1 = (f32[6,128,128]{2,1,0:T(8,128)S(1)}, bf16[128,1024]{1,0:T(8,128)(2,1)S(1)}, bf16[128,4096]{1,0:T(8,128)(2,1)S(1)}, bf16[3,256,4096]{2,1,0:T(8,128)(2,1)S(1)}, bf16[1,256,4096]{2,1,0:T(8,128)(2,1)S(1)}) custom-call(bf16[32,4096]{1,0:T(8,128)(2,1)S(1)} %copy-done, bf16[32,4096]{1,0:T(8,128)(2,1)S(1)} %collective-permute-done.2.refs_1_, ...), custom_call_target="tpu_custom_call" | custom-call | flops 6 | bytes 4 | tf_op jit(solution)/shard_map/hidden_first/pallas_call | solution.py:291
  16.8 0.0 collective-permute-done.1.refs_4_.refs_2_
  16.8 0.4 %collective-permute-start.5 = (bf16[32,4224]{1,0:T(8,128)(2,1)S(1)}, bf16[32,4224]{1,0:T(8,128)(2,1)S(1)}, u32[]{:S(2)}, u32[]{:S(2)}) collective-permute-start(bf16[32,4224]{1,0:T(8,128)(2,1)S(1)} %collective-permute-done.1.refs_4_.refs_2_), channel_id=1, source_target_pairs={{0,8},{8,0},{16,24},{24,16},{1,9},{9,1},{17,25},{25,17},{2,10},{10... | collective-permute-start | bytes 811016 | tf_op jit(solution)/shard_map/ppermute | solution.py:204
  17.2 5.8 %hidden_second.1 = (f32[6,128,128]{2,1,0:T(8,128)S(1)}, bf16[5,256,4096]{2,1,0:T(8,128)(2,1)S(1)}) custom-call(bf16[128,4096]{1,0:T(8,128)(2,1)S(1)} %get-tuple-element.31.refs_0_, bf16[6,256,4096]{2,1,0:T(8,128)(2,1)S(1)} %get-tuple-element.25.refs_4_.refs_1_, bf16[3,256,4096]{2,1,0:T(8,128)(2,1)S(1)} %get-tuple-element.32.refs_2_, ...), custom_call_target="tpu_custom_call" | custom-call | flops 6 | bytes 5 | tf_op jit(solution)/shard_map/hidden_second/pallas_call | solution.py:314
  23.0 0.0 collective-permute-done.refs_1_
  23.0 0.0 collective-permute-done.5.refs_3_
  23.1 3.6 %scores.1 = (f32[32,4,128]{2,1,0:T(4,128)S(1)}, f32[32,128]{1,0:T(8,128)S(1)}, f32[32,128]{1,0:T(8,128)S(1)}) custom-call(bf16[32,4224]{1,0:T(8,128)(2,1)S(1)} %pack.1.after.refs_0_, bf16[32,4224]{1,0:T(8,128)(2,1)S(1)} %collective-permute-done.refs_1_, bf16[32,4224]{1,0:T(8,128)(2,1)S(1)} %collective-permute-done.1.refs_4_.refs_2_, ...), custom_call_target="tpu_custom_call" | custom-call | flops 6 | tf_op jit(solution)/shard_map/scores/pallas_call | solution.py:329
  26.6 13.4 %all_to_all.5.blocks = f32[32,4,128]{2,1,0:T(4,128)S(1)} all-to-all(f32[32,4,128]{2,1,0:T(4,128)S(1)} %get-tuple-element.36), channel_id=1, replica_groups=mesh['dp'=4,'expert'=8] {'dp','expert'}, dimensions={0} | all-to-all | bytes 131072 | tf_op jit(solution)/shard_map/all_to_all | solution.py:347
  40.0 0.8 %gradient.1 = (f32[32,32]{1,0:T(8,128)}, f32[32,1024]{1,0:T(8,128)}) custom-call(f32[32,4,128]{2,1,0:T(4,128)S(1)} %all_to_all.5.blocks, f32[32,128]{1,0:T(8,128)S(1)} %get-tuple-element.37.probs_ref, f32[32,128]{1,0:T(8,128)S(1)} %get-tuple-element.38.chosen_ref, bf16[128,1024]{1,0:T(8,128)(2,1)S(1)} %get-tuple-element.39.mine), custom_call_target="tpu_custom_call" | custom-call | tf_op jit(solution)/shard_map/gradient/pallas_call | solution.py:349
Async XLA Ops:
  0.6 10.8 %collective-permute-start.3 = (bf16[32,4096]{1,0:T(8,128)(2,1)}, bf16[32,4096]{1,0:T(8,128)(2,1)S(1)}, u32[]{:S(2)}, u32[]{:S(2)}) collective-permute-start(bf16[32,4096]{1,0:T(8,128)(2,1)} %refs_0_.1), channel_id=1, source_target_pairs={{0,16},{8,24},{16,0},{24,8},{1,17},{9,25},{17,1},{25,9},{2,18},{10... | collective-permute-start | bytes 786440 | tf_op jit(solution)/shard_map/ppermute | solution.py:204
  4.7 12.1 %collective-permute-start.1 = (bf16[32,4224]{1,0:T(8,128)(2,1)S(1)}, bf16[32,4224]{1,0:T(8,128)(2,1)S(1)}, u32[]{:S(2)}, u32[]{:S(2)}) collective-permute-start(bf16[32,4224]{1,0:T(8,128)(2,1)S(1)} %pack.1.after.refs_0_), channel_id=1, source_target_pairs={{0,16},{8,24},{16,0},{24,8},{1,17},{9,25},{17,1},{25,9},{2,18},{10... | collective-permute-start | bytes 811016 | tf_op jit(solution)/shard_map/ppermute | solution.py:204
  4.8 7.3 %collective-permute-start.2 = (bf16[32,4096]{1,0:T(8,128)(2,1)}, bf16[32,4096]{1,0:T(8,128)(2,1)S(1)}, u32[]{:S(2)}, u32[]{:S(2)}) collective-permute-start(bf16[32,4096]{1,0:T(8,128)(2,1)} %refs_0_.1), channel_id=1, source_target_pairs={{0,8},{8,0},{16,24},{24,16},{1,9},{9,1},{17,25},{25,17},{2,10},{10... | collective-permute-start | bytes 786440 | tf_op jit(solution)/shard_map/ppermute | solution.py:204
  4.8 8.3 %copy-start = (bf16[32,4096]{1,0:T(8,128)(2,1)S(1)}, bf16[32,4096]{1,0:T(8,128)(2,1)}, u32[]{:S(2)}) copy-start(bf16[32,4096]{1,0:T(8,128)(2,1)} %refs_0_.1) | copy-start | bytes 786436
  11.4 1.7 %collective-permute-start.4 = (bf16[32,4096]{1,0:T(8,128)(2,1)S(1)}, bf16[32,4096]{1,0:T(8,128)(2,1)S(1)}, u32[]{:S(2)}, u32[]{:S(2)}) collective-permute-start(bf16[32,4096]{1,0:T(8,128)(2,1)S(1)} %collective-permute-done.3.refs_2_), channel_id=1, source_target_pairs={{0,8},{8,0},{16,24},{24,16},{1,9},{9,1},{17,25},{25,17},{2,10},{10... | collective-permute-start | bytes 786440 | tf_op jit(solution)/shard_map/ppermute | solution.py:204
  12.0 11.1 %collective-permute-start = (bf16[32,4224]{1,0:T(8,128)(2,1)S(1)}, bf16[32,4224]{1,0:T(8,128)(2,1)S(1)}, u32[]{:S(2)}, u32[]{:S(2)}) collective-permute-start(bf16[32,4224]{1,0:T(8,128)(2,1)S(1)} %pack.1.after.refs_0_), channel_id=1, source_target_pairs={{0,8},{8,0},{16,24},{24,16},{1,9},{9,1},{17,25},{25,17},{2,10},{10... | collective-permute-start | bytes 811016 | tf_op jit(solution)/shard_map/ppermute | solution.py:204
  16.8 6.3 %collective-permute-start.5 = (bf16[32,4224]{1,0:T(8,128)(2,1)S(1)}, bf16[32,4224]{1,0:T(8,128)(2,1)S(1)}, u32[]{:S(2)}, u32[]{:S(2)}) collective-permute-start(bf16[32,4224]{1,0:T(8,128)(2,1)S(1)} %collective-permute-done.1.refs_4_.refs_2_), channel_id=1, source_target_pairs={{0,8},{8,0},{16,24},{24,16},{1,9},{9,1},{17,25},{25,17},{2,10},{10... | collective-permute-start | bytes 811016 | tf_op jit(solution)/shard_map/ppermute | solution.py:204

commit v5 on v4

--- a/solution.py
+++ b/solution.py
@@ -71,7 +71,8 @@
     return copies
 
 
-def pack_kernel(logits, routes, cotangent, packed, logits_near, routes_near, columns, sems):
+def pack_load_kernel(plan, logits, routes, cotangent, gate, packed, gate_near, *scratch):
+    logits_near, routes_near, columns, sems, load_sems = scratch
     model_width = cotangent.shape[1]
     copies = [
         pltpu.make_async_copy(logits, logits_near, sems.at[0]),
@@ -80,6 +81,7 @@
     ]
     for copy in copies:
         copy.start()
+    loads = start_loads(plan, [gate], [gate_near], load_sems)
     columns[...] = jnp.zeros(columns.shape, jnp.float32)
     copies[0].wait()
     left = logits_near[...]
@@ -92,10 +94,14 @@
     columns[:, 3 * experts_all : 3 * experts_all + routes.shape[0]] = routes_near[...].astype(jnp.float32).T
     packed[:, model_width:] = columns[...].astype(jnp.bfloat16)
     copies[2].wait()
-
-
-def load_kernel(plan, gate, up, after, gate_near, up_near, sems):
-    for copy in start_loads(plan, [gate, up], [gate_near, up_near], sems):
+    for copy in loads:
+        copy.wait()
+
+
+def load_kernel(plan, *refs):
+    count = len(plan)
+    sources, nears, sems = refs[:count], refs[count + 1 : 2 * count + 1], refs[-1]
+    for copy in start_loads(plan, sources, nears, sems):
         copy.wait()
 
 
@@ -116,7 +122,7 @@
 def first_hidden_kernel(distances, plan, *refs, accs=()):
     count = len(distances)
     pieces, refs = refs[:count], refs[count:]
-    gate, up, up_far, down_far, hidden, mine, rows, up_near, down_near, sems, mine_sem = refs
+    gate_0, gate_1, up, up_far, down_far, after, hidden, mine, rows, up_near, down_near, sems, mine_sem = refs
     loads = start_loads(plan, [up_far, down_far], [up_near, down_near], sems)
     place_rows(pieces, distances, rows)
     width = mine.shape[1]
@@ -124,7 +130,7 @@
     own = pltpu.make_async_copy(rows.at[:, pl.ds(start, width)], mine, mine_sem)
     own.start()
     places, unit = hidden.shape[:2]
-    lanes = [blocks_of([gate], unit)[:places], blocks_of([up], unit)]
+    lanes = [blocks_of([gate_0, gate_1], unit)[:places], blocks_of([up], unit)]
 
     def finish(place, dots):
         hidden[place] = gated(dots)
@@ -135,10 +141,10 @@
         copy.wait()
 
 
-def second_hidden_kernel(plan, rows, gate, up, down_far, after, hidden, down_near, sems, accs=()):
+def second_hidden_kernel(plan, rows, gate, up_1, up_2, down_far, after, hidden, down_near, sems, accs=()):
     loads = start_loads(plan, [down_far], [down_near], sems)
     places, unit = hidden.shape[:2]
-    lanes = [blocks_of([gate], unit)[-places:], blocks_of([up], unit)]
+    lanes = [blocks_of([gate], unit)[-places:], blocks_of([up_1, up_2], unit)]
 
     def finish(place, dots):
         hidden[place] = gated(dots)
@@ -158,6 +164,7 @@
     local_experts = partial.shape[1]
     unit = hidden_0.shape[1]
     blocks = blocks_of([down_0, down_1], unit)
+    hidden = [held.at[place] for held in (hidden_0, hidden_1) for place in range(held.shape[0])]
     places = len(blocks) // 2
     per_expert = len(blocks) // local_experts
     sums = [None] * local_experts
@@ -175,8 +182,8 @@
         chosen[...] = named
 
     def finish(place, dots):
-        for held, block, paired in zip((hidden_0, hidden_1), (place, places + place), dots):
-            product = held[place] * paired
+        for block, paired in zip((place, places + place), dots):
+            product = hidden[block][...] * paired
             expert = block // per_expert
             sums[expert] = product if sums[expert] is None else sums[expert] + product
 
@@ -219,8 +226,8 @@
     extra = -(-(3 * experts_all + top) // 128) * 128
     chips = data_count // CORES
     distances = [chip * CORES + core for chip in range(chips) for core in range(CORES)]
-    half = chunks // 2
-    down_cut = max(1, chunks // 6)
+    gate_cut = chunks // 2
+    first = 2 * chunks // 3
 
     vmem = pl.BlockSpec(memory_space=pltpu.VMEM)
     hbm = pl.BlockSpec(memory_space=pltpu.HBM)
@@ -234,7 +241,7 @@
         return pltpu.VMEM((last - first, chunk_rows, model_width), jnp.bfloat16)
 
     def roomy():
-        return scoped(0 if accs else 2 * row_bytes)
+        return scoped(0 if accs(1) else 2 * row_bytes)
 
     def cost(loads, dots):
         return pl.CostEstimate(flops=dots, bytes_accessed=loads, transcendentals=0)
@@ -244,52 +251,62 @@
 
     edge = pltpu.get_tpu_info().mxu_column_size
     accs = []
-    places = half * chunk_rows // unit
-    if edge == 2 * total_tokens and model_width % edge == 0 and 2 * half == chunks and places * unit <= 1024:
-        accs = [pltpu.ACC(number)((unit, edge), jnp.float32) for number in range(2) for _ in range(places)]
+    places = first * chunk_rows // unit
+
+    def accs(count):
+        if edge != 2 * total_tokens or model_width % edge != 0 or units % 2 != 0 or count * unit > 1024:
+            return []
+        return [pltpu.ACC(number)((unit, edge), jnp.float32) for number in range(2) for _ in range(count)]
+
+    def load(parts, after, name):
+        plan = [(begin, end) for _, begin, end in parts]
+        count = sum(end - begin for begin, end in plan)
+        return pl.pallas_call(
+            functools.partial(load_kernel, plan),
+            out_shape=[near(*part) for part in plan],
+            in_specs=[hbm] * len(plan) + [anywhere],
+            out_specs=[vmem] * len(plan),
+            scratch_shapes=[pltpu.SemaphoreType.DMA((count,))],
+            compiler_params=scoped(0),
+            cost_estimate=cost(count, 0),
+            name=name,
+        )(*(source for source, _, _ in parts), after)
+
     cut = (chunks, chunk_rows, model_width)
     gate, up, down = (keep_far(weight.reshape(cut)) for weight in (gate_weight, up_weight, down_weight))
 
     tokens_beside = swap(tokens, "dp", 1)
     tokens_far = [swap(tokens, "dp", chip * CORES) for chip in range(1, chips)]
-    packed = pl.pallas_call(
-        pack_kernel,
-        out_shape=jax.ShapeDtypeStruct((tok_dev, model_width + extra), jnp.bfloat16),
-        in_specs=[hbm] * 3,
-        out_specs=vmem,
+    plan = [(0, gate_cut)]
+    packed, gate_0 = pl.pallas_call(
+        functools.partial(pack_load_kernel, plan),
+        out_shape=(jax.ShapeDtypeStruct((tok_dev, model_width + extra), jnp.bfloat16), near(*plan[0])),
+        in_specs=[hbm] * 4,
+        out_specs=(vmem, vmem),
         scratch_shapes=[
             pltpu.VMEM((tok_dev, experts_all), jnp.float32),
             pltpu.VMEM((top, tok_dev), jnp.int32),
             pltpu.VMEM((tok_dev, extra), jnp.float32),
             pltpu.SemaphoreType.DMA((3,)),
+            pltpu.SemaphoreType.DMA((gate_cut,)),
         ],
         compiler_params=scoped(0),
-        cost_estimate=cost(1, 0),
-        name="pack",
-    )(keep_far(logits), keep_far(routes.T), keep_far(cotangent))
+        cost_estimate=cost(gate_cut, 0),
+        name="load_pack",
+    )(keep_far(logits), keep_far(routes.T), keep_far(cotangent), gate)
     packed_far = [swap(packed, "dp", chip * CORES) for chip in range(1, chips)]
     packed_beside = swap(packed, "dp", 1)
-    plan = [(0, chunks), (0, half)]
-    gate_near, up_0 = pl.pallas_call(
-        functools.partial(load_kernel, plan),
-        out_shape=(near(*plan[0]), near(*plan[1])),
-        in_specs=[hbm, hbm, anywhere],
-        out_specs=(vmem, vmem),
-        scratch_shapes=[pltpu.SemaphoreType.DMA((chunks + half,))],
-        compiler_params=scoped(0),
-        cost_estimate=cost(chunks + half, 0),
-        name="load",
-    )(gate, up, packed)
-
-    tokens_far, gate_near, up_0 = lax.optimization_barrier((tokens_far, gate_near, up_0))
+    gate_1, up_0 = load([(gate, gate_cut, chunks), (up, 0, first)], packed, "load_second")
+    tokens_far, gate_1, up_0 = lax.optimization_barrier((tokens_far, gate_1, up_0))
     token_pieces = [tokens, tokens_beside]
     for far in tokens_far:
         token_pieces += [far, swap(far, "dp", 1)]
-
-    plan = [(half, chunks), (0, down_cut)]
+    (up_1,) = load([(up, first, first + 1)], tokens_far[0], "load_third")
+
+    plan = [(first + 1, chunks), (0, first)]
     loads = sum(last - first for first, last in plan)
-    hidden_0, mine, rows, up_1, down_0 = pl.pallas_call(
-        with_accs(functools.partial(first_hidden_kernel, distances, plan), accs),
+    hidden_0, mine, rows, up_2, down_0 = pl.pallas_call(
+        with_accs(functools.partial(first_hidden_kernel, distances, plan), accs(places)),
         out_shape=(
             jax.ShapeDtypeStruct((places, unit, total_tokens), jnp.float32),
             jax.ShapeDtypeStruct((total_tokens, model_width // data_count), jnp.bfloat16),
@@ -297,37 +314,37 @@
             near(*plan[0]),
             near(*plan[1]),
         ),
-        in_specs=[vmem] * (data_count + 2) + [hbm] * 2,
+        in_specs=[vmem] * (data_count + 3) + [hbm] * 2 + [anywhere],
         out_specs=(vmem,) * 5,
         scratch_shapes=[pltpu.SemaphoreType.DMA((loads,)), pltpu.SemaphoreType.DMA],
         compiler_params=roomy(),
-        cost_estimate=cost(loads, 2 * half),
+        cost_estimate=cost(loads, 2 * first),
         name="hidden_first",
-    )(*token_pieces, gate_near, up_0, up, down)
+    )(*token_pieces, gate_0, gate_1, up_0, up, down, up_1)
 
     packed_far, hidden_0, rows = lax.optimization_barrier((packed_far, hidden_0, rows))
     packed_pieces = [packed, packed_beside]
     for far in packed_far:
         packed_pieces += [far, swap(far, "dp", 1)]
 
-    plan = [(down_cut, chunks)]
+    plan = [(first, chunks)]
     hidden_1, down_1 = pl.pallas_call(
-        with_accs(functools.partial(second_hidden_kernel, plan), accs),
+        with_accs(functools.partial(second_hidden_kernel, plan), accs(units - places)),
         out_shape=(
             jax.ShapeDtypeStruct((units - places, unit, total_tokens), jnp.float32),
             near(*plan[0]),
         ),
-        in_specs=[vmem] * 3 + [hbm, anywhere],
+        in_specs=[vmem] * 4 + [hbm, anywhere],
         out_specs=(vmem, vmem),
-        scratch_shapes=[pltpu.SemaphoreType.DMA((chunks - down_cut,))],
+        scratch_shapes=[pltpu.SemaphoreType.DMA((chunks - first,))],
         compiler_params=roomy(),
-        cost_estimate=cost(chunks - down_cut, 2 * (chunks - half)),
+        cost_estimate=cost(chunks - first, 2 * (chunks - first)),
         name="hidden_second",
-    )(rows, gate_near, up_1, down, packed_far[0])
+    )(rows, gate_1, up_1, up_2, down, packed_far[0])
 
     table = jax.ShapeDtypeStruct((experts_all, total_tokens), jnp.float32)
     partial, probs, chosen = pl.pallas_call(
-        with_accs(functools.partial(score_kernel, distances, top), accs),
+        with_accs(functools.partial(score_kernel, distances, top), accs(units // 2)),
         out_shape=(
             jax.ShapeDtypeStruct((data_count * expert_count, local_experts, total_tokens), jnp.float32),
             table,

time: 41.1 us -> 41.8 us (1.017)
  Pallas kernels: 21.4 us -> 23.2 us
  waiting for transfers between devices: 1.09 us -> 0.02 us
    pallas_call x2 -> x3, Pallas kernels: 7.57 us -> 9.94 us  [the longest x2 6.92 us: load(): pl.pallas_call(functools.partial(load_kernel, plan), out_shape=[near(*par...]
    pallas_call x1, Pallas kernels: 5.81 us -> 4.16 us  [per_device(): pl.pallas_call(with_accs(functools.partial(second_hidden_kernel, plan), a...]
    pallas_call x1, Pallas kernels: 3.61 us -> 4.7 us  [per_device(): pl.pallas_call(with_accs(functools.partial(first_hidden_kernel, distances...]
    ppermute x6, waiting for transfers between devices: 1.09 us -> 0.02 us  [swap(): lax.ppermute(value, axis, [(index, index ^ distance) for index in range(l...]
  transfers between devices with their start and end apart: 6 -> 6, of which waited for: 1 -> 0; matrix products, arithmetic and copies ran while one was open for 0% -> 0% of each run, Pallas kernels for 42% -> 45%
where the time goes in v5:
time: 41.8 us; the launch traced here: 41.6 us
  Pallas kernels  23.2 us (56%)
  blocking collectives  13.4 us (32%)
  starting transfers between devices  4.31 us (10%)
  between operations  0.75 us (2%)
    all_to_all x1, blocking collectives, per_device(): lax.all_to_all(partial, ('dp', 'expert'), split_axis=0, concat_axis=0, ti...  13.4 us
    pallas_call x2, Pallas kernels, load(): pl.pallas_call(functools.partial(load_kernel, plan), out_shape=[near(*par...  6.92 us
    pallas_call x1, Pallas kernels, per_device(): pl.pallas_call(with_accs(functools.partial(first_hidden_kernel, distances...  4.7 us
    ppermute x6, starting transfers between devices, swap(): lax.ppermute(value, axis, [(index, index ^ distance) for index in range(l...  4.31 us
    pallas_call x1, Pallas kernels, per_device(): pl.pallas_call(with_accs(functools.partial(second_hidden_kernel, plan), a...  4.16 us
    pallas_call x1, Pallas kernels, per_device(): pl.pallas_call(with_accs(functools.partial(score_kernel, distances, top),...  3.55 us
    pallas_call x1, Pallas kernels, per_device(): pl.pallas_call(functools.partial(pack_load_kernel, plan), out_shape=(jax....  3.02 us
    pallas_call x1, Pallas kernels, per_device(): pl.pallas_call(functools.partial(gradient_kernel, data_count), out_shape=...  0.85 us
  transfers between devices with their start and end apart: 6, of which 0 were waited for; matrix products, arithmetic and copies ran while one was open for 0% of the time, Pallas kernels for 45%

profile of v5, /device:TPU:0, one launch (start us, length us, event | category | flops | bytes accessed | tf_op | source)
XLA Modules:
  0.0 41.6 jit_solution(2007760363898869858)
XLA Ops:
  0.6 0.0 copy-start
  0.6 3.0 %collective-permute-start.3 = (bf16[32,4096]{1,0:T(8,128)(2,1)}, bf16[32,4096]{1,0:T(8,128)(2,1)S(1)}, u32[]{:S(2)}, u32[]{:S(2)}) collective-permute-start(bf16[32,4096]{1,0:T(8,128)(2,1)} %refs_0_.1), channel_id=1, source_target_pairs={{0,16},{8,24},{16,0},{24,8},{1,17},{9,25},{17,1},{25,9},{2,18},{10... | collective-permute-start | bytes 786440 | tf_op jit(solution)/shard_map/ppermute | solution.py:211
  3.7 3.0 %load_pack.1 = (bf16[32,4224]{1,0:T(8,128)(2,1)S(1)}, bf16[3,256,4096]{2,1,0:T(8,128)(2,1)S(1)}) custom-call(f32[32,32]{1,0:T(8,128)} %logits.1, s32[8,32]{1,0:T(8,128)} %bitcast.12, bf16[32,4096]{1,0:T(8,128)(2,1)} %cotangent.1, bf16[6,256,4096]{2,1,0:T(8,128)(2,1)} %bitcast.8), custom_call_target="tpu_custom_call" | custom-call | bytes 3 | tf_op jit(solution)/shard_map/load_pack/pallas_call | solution.py:281
  6.7 0.1 collective-permute-start.1
  6.8 0.0 copy-done
  6.8 0.1 collective-permute-start.2
  6.9 5.3 %load_second.1 = (bf16[3,256,4096]{2,1,0:T(8,128)(2,1)S(1)}, bf16[4,256,4096]{2,1,0:T(8,128)(2,1)S(1)}) custom-call(bf16[6,256,4096]{2,1,0:T(8,128)(2,1)} %bitcast.9, bf16[6,256,4096]{2,1,0:T(8,128)(2,1)} %bitcast.5, bf16[32,4224]{1,0:T(8,128)(2,1)S(1)} %get-tuple-element.24.refs_2_.refs_0_), custom_call_target="tpu_custom_call" | custom-call | bytes 7 | tf_op jit(solution)/shard_map/load_second/pallas_call | solution.py:264
  12.2 0.0 collective-permute-done.3.refs_1_.refs_2_
  12.2 0.6 %collective-permute-start.4 = (bf16[32,4096]{1,0:T(8,128)(2,1)S(1)}, bf16[32,4096]{1,0:T(8,128)(2,1)S(1)}, u32[]{:S(2)}, u32[]{:S(2)}) collective-permute-start(bf16[32,4096]{1,0:T(8,128)(2,1)S(1)} %collective-permute-done.3.refs_1_.refs_2_), channel_id=1, source_target_pairs={{0,8},{8,0},{16,24},{24,16},{1,9},{9,1},{17,25},{25,17},{2,10},{10... | collective-permute-start | bytes 786440 | tf_op jit(solution)/shard_map/ppermute | solution.py:211
  12.8 0.1 collective-permute-start
  12.8 1.6 %load_third.1.refs_9_.refs_2_ = bf16[1,256,4096]{2,1,0:T(8,128)(2,1)S(1)} custom-call(bf16[6,256,4096]{2,1,0:T(8,128)(2,1)} %bitcast.6, bf16[32,4096]{1,0:T(8,128)(2,1)S(1)} %collective-permute-done.3.refs_1_.refs_2_), custom_call_target="tpu_custom_call" | custom-call | bytes 1 | tf_op jit(solution)/shard_map/load_third/pallas_call | solution.py:264
  14.5 0.0 collective-permute-done.2.refs_1_
  14.5 0.0 collective-permute-done.4.refs_3_
  14.5 4.7 %hidden_first.1 = (f32[8,128,128]{2,1,0:T(8,128)S(1)}, bf16[128,1024]{1,0:T(8,128)(2,1)S(1)}, bf16[128,4096]{1,0:T(8,128)(2,1)S(1)}, bf16[1,256,4096]{2,1,0:T(8,128)(2,1)S(1)}, bf16[4,256,4096]{2,1,0:T(8,128)(2,1)S(1)}) custom-call(bf16[32,4096]{1,0:T(8,128)(2,1)S(1)} %copy-done, bf16[32,4096]{1,0:T(8,128)(2,1)S(1)} %collective-permute-done.2.refs_1_, ...), custom_call_target="tpu_custom_call" | custom-call | flops 8 | bytes 5 | tf_op jit(solution)/shard_map/hidden_first/pallas_call | solution.py:308
  19.2 0.0 collective-permute-done.1.refs_5_.refs_2_
  19.2 0.5 %collective-permute-start.5 = (bf16[32,4224]{1,0:T(8,128)(2,1)S(1)}, bf16[32,4224]{1,0:T(8,128)(2,1)S(1)}, u32[]{:S(2)}, u32[]{:S(2)}) collective-permute-start(bf16[32,4224]{1,0:T(8,128)(2,1)S(1)} %collective-permute-done.1.refs_5_.refs_2_), channel_id=1, source_target_pairs={{0,8},{8,0},{16,24},{24,16},{1,9},{9,1},{17,25},{25,17},{2,10},{10... | collective-permute-start | bytes 811016 | tf_op jit(solution)/shard_map/ppermute | solution.py:211
  19.7 4.2 %hidden_second.1 = (f32[4,128,128]{2,1,0:T(8,128)S(1)}, bf16[2,256,4096]{2,1,0:T(8,128)(2,1)S(1)}) custom-call(bf16[128,4096]{1,0:T(8,128)(2,1)S(1)} %get-tuple-element.35.refs_0_, bf16[3,256,4096]{2,1,0:T(8,128)(2,1)S(1)} %get-tuple-element.29.refs_5_.refs_1_, bf16[1,256,4096]{2,1,0:T(8,128)(2,1)S(1)} %load_third.1.refs_9_.refs_2_, ...), custom_call_target="tpu_custom_call" | custom-call | flops 4 | bytes 2 | tf_op jit(solution)/shard_map/hidden_second/pallas_call | solution.py:331
  23.9 0.0 collective-permute-done.refs_1_
  23.9 0.0 collective-permute-done.5.refs_3_
  23.9 3.6 %scores.1 = (f32[32,4,128]{2,1,0:T(4,128)S(1)}, f32[32,128]{1,0:T(8,128)S(1)}, f32[32,128]{1,0:T(8,128)S(1)}) custom-call(bf16[32,4224]{1,0:T(8,128)(2,1)S(1)} %get-tuple-element.24.refs_2_.refs_0_, bf16[32,4224]{1,0:T(8,128)(2,1)S(1)} %collective-permute-done.refs_1_, bf16[32,4224]{1,0:T(8,128)(2,1)S(1)} %collective-permute-done.1.refs_5_.refs_2_, ...), custom_call_target="tpu_custom_call" | custom-call | flops 6 | tf_op jit(solution)/shard_map/scores/pallas_call | solution.py:346
  27.4 13.4 %all_to_all.5.blocks = f32[32,4,128]{2,1,0:T(4,128)S(1)} all-to-all(f32[32,4,128]{2,1,0:T(4,128)S(1)} %get-tuple-element.40), channel_id=1, replica_groups=mesh['dp'=4,'expert'=8] {'dp','expert'}, dimensions={0} | all-to-all | bytes 131072 | tf_op jit(solution)/shard_map/all_to_all | solution.py:364
  40.8 0.8 %gradient.1 = (f32[32,32]{1,0:T(8,128)}, f32[32,1024]{1,0:T(8,128)}) custom-call(f32[32,4,128]{2,1,0:T(4,128)S(1)} %all_to_all.5.blocks, f32[32,128]{1,0:T(8,128)S(1)} %get-tuple-element.41.probs_ref, f32[32,128]{1,0:T(8,128)S(1)} %get-tuple-element.42.chosen_ref, bf16[128,1024]{1,0:T(8,128)(2,1)S(1)} %get-tuple-element.43.mine), custom_call_target="tpu_custom_call" | custom-call | tf_op jit(solution)/shard_map/gradient/pallas_call | solution.py:366
Async XLA Ops:
  0.6 6.2 %copy-start = (bf16[32,4096]{1,0:T(8,128)(2,1)S(1)}, bf16[32,4096]{1,0:T(8,128)(2,1)}, u32[]{:S(2)}) copy-start(bf16[32,4096]{1,0:T(8,128)(2,1)} %refs_0_.1) | copy-start | bytes 786436
  0.6 11.6 %collective-permute-start.3 = (bf16[32,4096]{1,0:T(8,128)(2,1)}, bf16[32,4096]{1,0:T(8,128)(2,1)S(1)}, u32[]{:S(2)}, u32[]{:S(2)}) collective-permute-start(bf16[32,4096]{1,0:T(8,128)(2,1)} %refs_0_.1), channel_id=1, source_target_pairs={{0,16},{8,24},{16,0},{24,8},{1,17},{9,25},{17,1},{25,9},{2,18},{10... | collective-permute-start | bytes 786440 | tf_op jit(solution)/shard_map/ppermute | solution.py:211
  6.7 12.5 %collective-permute-start.1 = (bf16[32,4224]{1,0:T(8,128)(2,1)S(1)}, bf16[32,4224]{1,0:T(8,128)(2,1)S(1)}, u32[]{:S(2)}, u32[]{:S(2)}) collective-permute-start(bf16[32,4224]{1,0:T(8,128)(2,1)S(1)} %get-tuple-element.24.refs_2_.refs_0_), channel_id=1, source_target_pairs={{0,16},{8,24},{16,0},{24,8},{1,17},{9,25},{17,1},{25,9},{2,18},{10... | collective-permute-start | bytes 811016 | tf_op jit(solution)/shard_map/ppermute | solution.py:211
  6.8 7.7 %collective-permute-start.2 = (bf16[32,4096]{1,0:T(8,128)(2,1)S(1)}, bf16[32,4096]{1,0:T(8,128)(2,1)S(1)}, u32[]{:S(2)}, u32[]{:S(2)}) collective-permute-start(bf16[32,4096]{1,0:T(8,128)(2,1)S(1)} %copy-done), channel_id=1, source_target_pairs={{0,8},{8,0},{16,24},{24,16},{1,9},{9,1},{17,25},{25,17},{2,10},{10... | collective-permute-start | bytes 786440 | tf_op jit(solution)/shard_map/ppermute | solution.py:211
  12.2 2.3 %collective-permute-start.4 = (bf16[32,4096]{1,0:T(8,128)(2,1)S(1)}, bf16[32,4096]{1,0:T(8,128)(2,1)S(1)}, u32[]{:S(2)}, u32[]{:S(2)}) collective-permute-start(bf16[32,4096]{1,0:T(8,128)(2,1)S(1)} %collective-permute-done.3.refs_1_.refs_2_), channel_id=1, source_target_pairs={{0,8},{8,0},{16,24},{24,16},{1,9},{9,1},{17,25},{25,17},{2,10},{10... | collective-permute-start | bytes 786440 | tf_op jit(solution)/shard_map/ppermute | solution.py:211
  12.8 11.1 %collective-permute-start = (bf16[32,4224]{1,0:T(8,128)(2,1)S(1)}, bf16[32,4224]{1,0:T(8,128)(2,1)S(1)}, u32[]{:S(2)}, u32[]{:S(2)}) collective-permute-start(bf16[32,4224]{1,0:T(8,128)(2,1)S(1)} %get-tuple-element.24.refs_2_.refs_0_), channel_id=1, source_target_pairs={{0,8},{8,0},{16,24},{24,16},{1,9},{9,1},{17,25},{25,17},{2,10},{10... | collective-permute-start | bytes 811016 | tf_op jit(solution)/shard_map/ppermute | solution.py:211
  19.2 4.7 %collective-permute-start.5 = (bf16[32,4224]{1,0:T(8,128)(2,1)S(1)}, bf16[32,4224]{1,0:T(8,128)(2,1)S(1)}, u32[]{:S(2)}, u32[]{:S(2)}) collective-permute-start(bf16[32,4224]{1,0:T(8,128)(2,1)S(1)} %collective-permute-done.1.refs_5_.refs_2_), channel_id=1, source_target_pairs={{0,8},{8,0},{16,24},{24,16},{1,9},{9,1},{17,25},{25,17},{2,10},{10... | collective-permute-start | bytes 811016 | tf_op jit(solution)/shard_map/ppermute | solution.py:211

commit v6 on v4

v6 whole, which is shorter than its diff:
```python
import functools

import jax
import jax.numpy as jnp
from jax import lax
from jax.experimental import pallas as pl
from jax.experimental.pallas import tpu as pltpu
from jax.sharding import PartitionSpec as P

CORES = 2


def dot_rows(a, b):
    return lax.dot_general(a, b, (((1,), (1,)), ((), ())), preferred_element_type=jnp.float32)


def stream_dots(rows, lanes, size, accs, ready, finish):
    groups = [range(first, first + size) for first in range(0, len(lanes[0]), size)]

    def dots_of(number, place):
        if not accs:
            return [dot_rows(lane[place][...], rows[...]) for lane in lanes]
        at = number % 2 * size + place % size
        return [pltpu.matmul_pop(acc[at])[:, : rows.shape[0]] for acc in accs]

    def read(number):
        for place in groups[number]:
            finish(place, dots_of(number, place))

    if not accs:
        for number in range(len(groups)):
            ready(number)
            read(number)
        return
    edge = accs[0][0].shape[1]
    steps = rows.shape[1] // edge

    def push(turn):
        first = turn % steps * edge
        both = jnp.concatenate([rows[:, first : first + edge]] * (edge // rows.shape[0]), axis=0)
        for unit in range(len(lanes)):
            pltpu.matmul_push_rhs(both, turn % 2, unit, transpose=True)

    push(0)
    for turn in range(len(groups) * steps):
        number, step = divmod(turn, steps)
        if step == 0:
            ready(number)
        for place in groups[number]:
            for lane, acc in zip(lanes, accs):
                part = lane[place][:, step * edge : (step + 1) * edge]
                staged = turn % 2 if place == groups[number][0] else None
                pltpu.matmul_acc_lhs(acc[number % 2 * size + place % size], part, load_staged_rhs=staged)
            if place == groups[number][0] and turn + 1 < len(groups) * steps:
                push(turn + 1)
        if step == 0 and number > 0:
            read(number - 1)
    read(len(groups) - 1)


def with_accs(kernel, shapes):
    if not shapes:
        return kernel
    half = len(shapes) // 2

    def body(*refs):
        pl.run_scoped(lambda *accs: kernel(*refs, accs=(accs[:half], accs[half:])), *shapes)

    return body


def place_rows(pieces, distances, rows):
    me = lax.axis_index("dp")
    tok_dev = pieces[0].shape[0]
    for piece, distance in zip(pieces, distances):
        start = pl.multiple_of(jnp.bitwise_xor(me, distance) * tok_dev, tok_dev)
        rows[pl.ds(start, tok_dev), :] = piece[...]


def start_loads(plan, sources, nears, sems):
    copies, number = [], 0
    for (first, last), source, near in zip(plan, sources, nears):
        for chunk in range(first, last):
            copies.append(pltpu.make_async_copy(source.at[chunk], near.at[chunk - first], sems.at[number]))
            number += 1
    for copy in copies:
        copy.start()
    return copies


def load_pack_kernel(plan, logits, routes, cotangent, gate, up, packed, gate_near, up_near, *scratch):
    logits_near, routes_near, columns, sems, load_sems = scratch
    model_width = cotangent.shape[1]
    copies = [
        pltpu.make_async_copy(logits, logits_near, sems.at[0]),
        pltpu.make_async_copy(routes, routes_near, sems.at[1]),
        pltpu.make_async_copy(cotangent, packed.at[:, :model_width], sems.at[2]),
    ]
    for copy in copies:
        copy.start()
    loads = start_loads(plan, [gate, up], [gate_near, up_near], load_sems)
    columns[...] = jnp.zeros(columns.shape, jnp.float32)
    copies[0].wait()
    left = logits_near[...]
    experts_all = left.shape[1]
    for term in range(3):
        rounded = left.astype(jnp.bfloat16).astype(jnp.float32)
        columns[:, term * experts_all : (term + 1) * experts_all] = rounded
        left = left - rounded
    copies[1].wait()
    columns[:, 3 * experts_all : 3 * experts_all + routes.shape[0]] = routes_near[...].astype(jnp.float32).T
    packed[:, model_width:] = columns[...].astype(jnp.bfloat16)
    copies[2].wait()
    for copy in loads:
        copy.wait()


def blocks_of(buffers, unit):
    return [
        buffer.at[chunk, first : first + unit]
        for buffer in buffers
        for chunk in range(buffer.shape[0])
        for first in range(0, buffer.shape[1], unit)
    ]


def gated(dots):
    gate_pre, up_pre = dots
    return gate_pre / (1.0 + jnp.exp(-gate_pre)) * up_pre


def hidden_kernel(distances, plan, size, *refs, accs=()):
    count = len(distances)
    pieces, refs = refs[:count], refs[count:]
    gate, up_near, up_far, down_far, hidden, mine, down_near, rows, up_late, sems, mine_sem = refs
    loads = start_loads(plan, [up_far, down_far], [up_late, down_near], sems)
    late = up_late.shape[0]
    place_rows(pieces, distances, rows)
    width = mine.shape[1]
    start = pl.multiple_of(lax.axis_index("dp") * width, width)
    own = pltpu.make_async_copy(rows.at[:, pl.ds(start, width)], mine, mine_sem)
    own.start()
    places, unit = hidden.shape[:2]
    lanes = [blocks_of([gate], unit), blocks_of([up_near, up_late], unit)]
    per_chunk = places // gate.shape[0]
    waited = [0]

    def ready(group):
        needed = -(-(group + 1) * size // per_chunk) - up_near.shape[0]
        while waited[0] < min(needed, late):
            loads[waited[0]].wait()
            waited[0] += 1

    def finish(place, dots):
        gate_pre, up_pre = dots
        hidden[place] = gate_pre / (1.0 + jnp.exp(-gate_pre)) * up_pre

    stream_dots(rows, lanes, size, accs, ready, finish)
    own.wait()
    for copy in loads[late:]:
        copy.wait()


def score_kernel(distances, plan, top, *refs, accs=()):
    count = len(distances)
    pieces, refs = refs[:count], refs[count:]
    hidden, down_near, down_far, partial, probs, chosen, rows, down_late, sems = refs
    loads = start_loads(plan, [down_far], [down_late], sems)
    model_width = down_far.shape[2]
    experts_all = probs.shape[0]
    place_rows(pieces, distances, rows)
    local_experts = partial.shape[1]
    blocks = blocks_of([down_near, down_late], hidden.shape[1])
    per_expert = len(blocks) // local_experts
    size = len(blocks) // 4
    order = [
        [group * 2 * size + lane * size + place for group in range(2) for place in range(size)] for lane in range(2)
    ]
    sums = [None] * local_experts

    def routing():
        packed = rows[:, model_width:].astype(jnp.float32).T
        terms = [packed[term * experts_all : (term + 1) * experts_all] for term in range(3)]
        logits = terms[0] + terms[1] + terms[2]
        raised = jnp.exp(logits - jnp.max(logits, axis=0, keepdims=True))
        probs[...] = raised / jnp.sum(raised, axis=0, keepdims=True)
        number = lax.broadcasted_iota(jnp.int32, logits.shape, 0).astype(jnp.float32)
        named = jnp.zeros(logits.shape, jnp.float32)
        for slot in range(3 * experts_all, 3 * experts_all + top):
            named = named + (packed[slot : slot + 1] == number).astype(jnp.float32)
        chosen[...] = named

    def ready(group):
        if group == 1:
            for copy in loads:
                copy.wait()

    def finish(place, dots):
        for lane, paired in zip(order, dots):
            block = lane[place]
            product = hidden[block] * paired
            expert = block // per_expert
            sums[expert] = product if sums[expert] is None else sums[expert] + product

    routing()
    lanes = [[blocks[block] for block in lane] for lane in order]
    stream_dots(rows.at[:, :model_width], lanes, size, accs, ready, finish)
    lines = [jnp.sum(term, axis=0, keepdims=True) for term in sums]
    partial[...] = jnp.broadcast_to(jnp.concatenate(lines, axis=0)[None], partial.shape)


def gradient_kernel(data_count, blocks, probs_ref, chosen_ref, mine, logit_grad, router_grad, grads):
    experts_all, total_tokens = probs_ref.shape
    scores = jnp.sum(blocks[...].reshape((data_count, experts_all, total_tokens)), axis=0)
    probs, chosen = probs_ref[...], chosen_ref[...]
    mass = jnp.sum(probs * chosen, axis=0, keepdims=True)
    weighted = jnp.sum(probs * chosen * scores, axis=0, keepdims=True)
    prob_grad = scores / mass - chosen * weighted / (mass * mass)
    grad = probs * (prob_grad - jnp.sum(probs * prob_grad, axis=0, keepdims=True))
    router_grad[...] = jnp.dot(grad.astype(jnp.bfloat16), mine[...], preferred_element_type=jnp.float32)
    grads[...] = grad.T
    tok_dev = logit_grad.shape[0]
    logit_grad[...] = grads[pl.ds(pl.multiple_of(lax.axis_index("dp") * tok_dev, tok_dev), tok_dev), :]


def swap(value, axis, distance):
    return lax.ppermute(value, axis, [(index, index ^ distance) for index in range(lax.axis_size(axis))])


def per_device(tokens, cotangent, logits, routes, gate_weight, up_weight, down_weight):
    data_count = lax.axis_size("dp")
    expert_count = lax.axis_size("expert")
    tok_dev, model_width = tokens.shape
    local_experts, ff_dev = gate_weight.shape[:2]
    total_tokens = tok_dev * data_count
    experts_all = local_experts * expert_count
    top = routes.shape[1]
    unit = 128 if ff_dev % 128 == 0 else ff_dev
    units = local_experts * ff_dev // unit
    chunk_rows = unit * (2 if unit == 128 and units % 2 == 0 else 1)
    chunks = local_experts * ff_dev // chunk_rows
    extra = -(-(3 * experts_all + top) // 128) * 128
    chips = data_count // CORES
    distances = [chip * CORES + core for chip in range(chips) for core in range(CORES)]
    up_cut = chunks // 2
    down_cut = 2 * chunks // 3

    vmem = pl.BlockSpec(memory_space=pltpu.VMEM)
    hbm = pl.BlockSpec(memory_space=pltpu.HBM)
    anywhere = pl.BlockSpec(memory_space=pl.ANY)
    row_bytes = total_tokens * model_width * 2

    def keep_far(value):
        return pltpu.with_memory_space_constraint(value, pltpu.HBM)

    def near(first, last):
        return pltpu.VMEM((last - first, chunk_rows, model_width), jnp.bfloat16)

    def cost(loads, dots):
        return pl.CostEstimate(flops=dots, bytes_accessed=loads, transcendentals=0)

    def scoped(size):
        return pltpu.CompilerParams(vmem_limit_bytes=size + (2 << 20))

    edge = pltpu.get_tpu_info().mxu_column_size
    accs = []
    size = units // 3 if units % 3 == 0 else 1

    def accs(count):
        if edge != 2 * total_tokens or model_width % edge != 0 or 2 * count * unit > 1024 or units % 12 != 0:
            return []
        return [pltpu.ACC(number)((unit, edge), jnp.float32) for number in range(2) for _ in range(2 * count)]

    cut = (chunks, chunk_rows, model_width)
    gate, up, down = (keep_far(weight.reshape(cut)) for weight in (gate_weight, up_weight, down_weight))

    tokens_beside = swap(tokens, "dp", 1)
    tokens_far = [swap(tokens, "dp", chip * CORES) for chip in range(1, chips)]
    plan = [(0, chunks), (0, up_cut)]
    packed, gate_near, up_near = pl.pallas_call(
        functools.partial(load_pack_kernel, plan),
        out_shape=(
            jax.ShapeDtypeStruct((tok_dev, model_width + extra), jnp.bfloat16),
            near(*plan[0]),
            near(*plan[1]),
        ),
        in_specs=[hbm] * 5,
        out_specs=(vmem,) * 3,
        scratch_shapes=[
            pltpu.VMEM((tok_dev, experts_all), jnp.float32),
            pltpu.VMEM((top, tok_dev), jnp.int32),
            pltpu.VMEM((tok_dev, extra), jnp.float32),
            pltpu.SemaphoreType.DMA((3,)),
            pltpu.SemaphoreType.DMA((chunks + up_cut,)),
        ],
        compiler_params=scoped(0),
        cost_estimate=cost(chunks + up_cut, 0),
        name="load_pack",
    )(keep_far(logits), keep_far(routes.T), keep_far(cotangent), gate, up)
    packed_far = [swap(packed, "dp", chip * CORES) for chip in range(1, chips)]
    packed_beside = swap(packed, "dp", 1)
    tokens_far, gate_near, up_near = lax.optimization_barrier((tokens_far, gate_near, up_near))
    token_pieces = [tokens, tokens_beside]
    for far in tokens_far:
        token_pieces += [far, swap(far, "dp", 1)]
    plan = [(up_cut, chunks), (0, down_cut)]
    loads = chunks - up_cut + down_cut
    hidden, mine, down_near = pl.pallas_call(
        with_accs(functools.partial(hidden_kernel, distances, plan, size), accs(size)),
        out_shape=(
            jax.ShapeDtypeStruct((units, unit, total_tokens), jnp.float32),
            jax.ShapeDtypeStruct((total_tokens, model_width // data_count), jnp.bfloat16),
            near(*plan[1]),
        ),
        in_specs=[vmem] * (data_count + 2) + [hbm] * 2,
        out_specs=(vmem,) * 3,
        scratch_shapes=[
            pltpu.VMEM((total_tokens, model_width), jnp.bfloat16),
            near(*plan[0]),
            pltpu.SemaphoreType.DMA((loads,)),
            pltpu.SemaphoreType.DMA,
        ],
        compiler_params=scoped((chunks - up_cut) * cut[1] * cut[2] * 2 + (1 if accs(size) else 3) * row_bytes),
        cost_estimate=cost(loads, 2 * chunks),
        name="hidden",
    )(*token_pieces, gate_near, up_near, up, down)

    packed_far, hidden = lax.optimization_barrier((packed_far, hidden))
    packed_pieces = [packed, packed_beside]
    for far in packed_far:
        packed_pieces += [far, swap(far, "dp", 1)]

    plan = [(down_cut, chunks)]
    table = jax.ShapeDtypeStruct((experts_all, total_tokens), jnp.float32)
    partial, probs, chosen = pl.pallas_call(
        with_accs(functools.partial(score_kernel, distances, plan, top), accs(units // 4)),
        out_shape=(
            jax.ShapeDtypeStruct((data_count * expert_count, local_experts, total_tokens), jnp.float32),
            table,
            table,
        ),
        in_specs=[vmem] * (data_count + 2) + [hbm],
        out_specs=(vmem, vmem, vmem),
        scratch_shapes=[
            pltpu.VMEM((total_tokens, model_width + extra), jnp.bfloat16),
            near(*plan[0]),
            pltpu.SemaphoreType.DMA((chunks - down_cut,)),
        ],
        compiler_params=scoped((chunks - down_cut) * cut[1] * cut[2] * 2 + 3 * row_bytes),
        cost_estimate=cost(chunks - down_cut, chunks),
        name="scores",
    )(*packed_pieces, hidden, down_near, down)

    score_blocks = lax.all_to_all(partial, ("dp", "expert"), split_axis=0, concat_axis=0, tiled=True)

    logit_grad, router_grad = pl.pallas_call(
        functools.partial(gradient_kernel, data_count),
        out_shape=(
            jax.ShapeDtypeStruct((tok_dev, experts_all), jnp.float32),
            jax.ShapeDtypeStruct((experts_all, model_width // data_count), jnp.float32),
        ),
        in_specs=[vmem] * 4,
        out_specs=(vmem, vmem),
        scratch_shapes=[pltpu.VMEM((total_tokens, experts_all), jnp.float32)],
        compiler_params=scoped(4 << 20),
        name="gradient",
    )(score_blocks, probs, chosen, mine)
    return logit_grad, router_grad.T


def solution(mesh):
    placed = (
        P("dp", None),
        P("dp", None),
        P("dp", None),
        P("dp", None),
        P("expert", "dp", None),
        P("expert", "dp", None),
        P("expert", "dp", None),
    )
    mapped = jax.shard_map(
        per_device,
        mesh=mesh,
        in_specs=placed,
        out_specs=(P("dp", None), P("dp", None)),
        check_vma=False,
    )

    def run(*args):
        with jax.sharding.use_abstract_mesh(mesh.abstract_mesh):
            return mapped(*args)

    return run
```

time: 41.1 us -> 39.4 us (0.959)
  Pallas kernels: 21.4 us -> 18.5 us
  waiting for transfers between devices: 1.09 us -> 2.72 us
    pallas_call x5 -> x3, Pallas kernels: 20.5 us -> 17.7 us  [the longest x1 6.91 us: per_device(): pl.pallas_call(with_accs(functools.partial(hidden_kernel, distances, plan...]
    ppermute x6, waiting for transfers between devices: 1.09 us -> 2.72 us  [swap(): lax.ppermute(value, axis, [(index, index ^ distance) for index in range(l...]
  transfers between devices with their start and end apart: 6 -> 6, of which waited for: 1 -> 3; matrix products, arithmetic and copies ran while one was open for 0% -> 0% of each run, Pallas kernels for 42% -> 35%
where the time goes in v6:
time: 39.4 us; the launch traced here: 39.3 us
  Pallas kernels  18.5 us (47%)
  blocking collectives  13.4 us (34%)
  starting transfers between devices  3.97 us (10%)
  waiting for transfers between devices  2.72 us (7%)
  between operations  0.68 us (2%)
    all_to_all x1, blocking collectives, per_device(): lax.all_to_all(partial, ('dp', 'expert'), split_axis=0, concat_axis=0, ti...  13.4 us
    pallas_call x1, Pallas kernels, per_device(): pl.pallas_call(with_accs(functools.partial(hidden_kernel, distances, plan...  6.91 us
    pallas_call x1, Pallas kernels, per_device(): pl.pallas_call(functools.partial(load_pack_kernel, plan), out_shape=(jax....  6.68 us
    pallas_call x1, Pallas kernels, per_device(): pl.pallas_call(with_accs(functools.partial(score_kernel, distances, plan,...  4.08 us
    ppermute x6, starting transfers between devices, swap(): lax.ppermute(value, axis, [(index, index ^ distance) for index in range(l...  3.97 us
    ppermute x6, waiting for transfers between devices, swap(): lax.ppermute(value, axis, [(index, index ^ distance) for index in range(l...  2.72 us
    pallas_call x1, Pallas kernels, per_device(): pl.pallas_call(functools.partial(gradient_kernel, data_count), out_shape=...  0.85 us
  transfers between devices with their start and end apart: 6, of which 3 were waited for; matrix products, arithmetic and copies ran while one was open for 0% of the time, Pallas kernels for 35%

profile of v6, /device:TPU:0, one launch (start us, length us, event | category | flops | bytes accessed | tf_op | source)
XLA Modules:
  0.0 39.3 jit_solution(5563129856483582552)
XLA Ops:
  0.6 3.0 %collective-permute-start.3 = (bf16[32,4096]{1,0:T(8,128)(2,1)}, bf16[32,4096]{1,0:T(8,128)(2,1)S(1)}, u32[]{:S(2)}, u32[]{:S(2)}) collective-permute-start(bf16[32,4096]{1,0:T(8,128)(2,1)} %refs_0_.1), channel_id=1, source_target_pairs={{0,16},{8,24},{16,0},{24,8},{1,17},{9,25},{17,1},{25,9},{2,18},{10... | collective-permute-start | bytes 786440 | tf_op jit(solution)/shard_map/ppermute | solution.py:227
  3.7 0.0 copy-start
  3.7 6.7 %load_pack.1 = (bf16[32,4224]{1,0:T(8,128)(2,1)S(1)}, bf16[6,256,4096]{2,1,0:T(8,128)(2,1)S(1)}, bf16[3,256,4096]{2,1,0:T(8,128)(2,1)S(1)}) custom-call(f32[32,32]{1,0:T(8,128)} %logits.1, s32[8,32]{1,0:T(8,128)} %bitcast.10, bf16[32,4096]{1,0:T(8,128)(2,1)} %cotangent.1, bf16[6,256,4096]{2,1,0:T(8,128)(2,1)} %bitcast.9, bf16[6,256,4096]{2,1,0:T(8,128)(2,1)} %bitcast.5), custom_call_target="tpu_custom_call" | custom-call | bytes 9 | tf_op jit(solution)/shard_map/load_pack/pallas_call | solution.py:280
  10.4 0.1 collective-permute-start.1
  10.4 0.0 copy-done
  10.4 0.1 collective-permute-start.2
  10.5 0.0 collective-permute-done.3.refs_2_
  10.5 0.5 %collective-permute-start.4 = (bf16[32,4096]{1,0:T(8,128)(2,1)S(1)}, bf16[32,4096]{1,0:T(8,128)(2,1)S(1)}, u32[]{:S(2)}, u32[]{:S(2)}) collective-permute-start(bf16[32,4096]{1,0:T(8,128)(2,1)S(1)} %collective-permute-done.3.refs_2_), channel_id=1, source_target_pairs={{0,8},{8,0},{16,24},{24,16},{1,9},{9,1},{17,25},{25,17},{2,10},{10... | collective-permute-start | bytes 786440 | tf_op jit(solution)/shard_map/ppermute | solution.py:227
  11.0 0.1 collective-permute-start
  11.1 0.9 %collective-permute-done.2.refs_1_ = bf16[32,4096]{1,0:T(8,128)(2,1)S(1)} collective-permute-done((bf16[32,4096]{1,0:T(8,128)(2,1)S(1)}, bf16[32,4096]{1,0:T(8,128)(2,1)S(1)}, u32[]{:S(2)}, u32[]{:S(2)}) %collective-permute-start.2) | collective-permute-done | bytes 262176 | tf_op jit(solution)/shard_map/ppermute | solution.py:227
  12.0 0.4 collective-permute-done.4.refs_3_
  12.4 6.9 %hidden.1 = (f32[12,128,128]{2,1,0:T(8,128)S(1)}, bf16[128,1024]{1,0:T(8,128)(2,1)S(1)}, bf16[4,256,4096]{2,1,0:T(8,128)(2,1)S(1)}) custom-call(bf16[32,4096]{1,0:T(8,128)(2,1)S(1)} %copy-done, bf16[32,4096]{1,0:T(8,128)(2,1)S(1)} %collective-permute-done.2.refs_1_, bf16[32,4096]{1,0:T(8,128)(2,1)S(1)} %collective-permute-done.3.refs_2_, ...), custom_call_target="tpu_custom_call" | custom-call | flops 12 | bytes 7 | tf_op jit(solution)/shard_map/hidden/pallas_call | solution.py:308
  19.3 0.0 collective-permute-done.1.refs_2_
  19.4 0.2 collective-permute-start.5
  19.6 0.0 collective-permute-done.refs_1_
  19.6 1.4 %collective-permute-done.5.refs_3_ = bf16[32,4224]{1,0:T(8,128)(2,1)S(1)} collective-permute-done((bf16[32,4224]{1,0:T(8,128)(2,1)S(1)}, bf16[32,4224]{1,0:T(8,128)(2,1)S(1)}, u32[]{:S(2)}, u32[]{:S(2)}) %collective-permute-start.5) | collective-permute-done | bytes 270368 | tf_op jit(solution)/shard_map/ppermute | solution.py:227
  21.0 4.1 %scores.1 = (f32[32,4,128]{2,1,0:T(4,128)S(1)}, f32[32,128]{1,0:T(8,128)S(1)}, f32[32,128]{1,0:T(8,128)S(1)}) custom-call(bf16[32,4224]{1,0:T(8,128)(2,1)S(1)} %get-tuple-element.18.refs_0_, bf16[32,4224]{1,0:T(8,128)(2,1)S(1)} %collective-permute-done.refs_1_, bf16[32,4224]{1,0:T(8,128)(2,1)S(1)} %collective-permute-done.1.refs_2_, ...), custom_call_target="tpu_custom_call" | custom-call | flops 6 | bytes 2 | tf_op jit(solution)/shard_map/scores/pallas_call | solution.py:335
  25.1 13.4 %all_to_all.5.blocks = f32[32,4,128]{2,1,0:T(4,128)S(1)} all-to-all(f32[32,4,128]{2,1,0:T(4,128)S(1)} %get-tuple-element.28), channel_id=1, replica_groups=mesh['dp'=4,'expert'=8] {'dp','expert'}, dimensions={0} | all-to-all | bytes 131072 | tf_op jit(solution)/shard_map/all_to_all | solution.py:354
  38.4 0.8 %gradient.1 = (f32[32,32]{1,0:T(8,128)}, f32[32,1024]{1,0:T(8,128)}) custom-call(f32[32,4,128]{2,1,0:T(4,128)S(1)} %all_to_all.5.blocks, f32[32,128]{1,0:T(8,128)S(1)} %get-tuple-element.29.probs_ref, f32[32,128]{1,0:T(8,128)S(1)} %get-tuple-element.30.chosen_ref, bf16[128,1024]{1,0:T(8,128)(2,1)S(1)} %get-tuple-element.31.mine), custom_call_target="tpu_custom_call" | custom-call | tf_op jit(solution)/shard_map/gradient/pallas_call | solution.py:356
Async XLA Ops:
  0.6 9.9 %collective-permute-start.3 = (bf16[32,4096]{1,0:T(8,128)(2,1)}, bf16[32,4096]{1,0:T(8,128)(2,1)S(1)}, u32[]{:S(2)}, u32[]{:S(2)}) collective-permute-start(bf16[32,4096]{1,0:T(8,128)(2,1)} %refs_0_.1), channel_id=1, source_target_pairs={{0,16},{8,24},{16,0},{24,8},{1,17},{9,25},{17,1},{25,9},{2,18},{10... | collective-permute-start | bytes 786440 | tf_op jit(solution)/shard_map/ppermute | solution.py:227
  3.7 6.8 %copy-start = (bf16[32,4096]{1,0:T(8,128)(2,1)S(1)}, bf16[32,4096]{1,0:T(8,128)(2,1)}, u32[]{:S(2)}) copy-start(bf16[32,4096]{1,0:T(8,128)(2,1)} %refs_0_.1) | copy-start | bytes 786436
  10.4 9.0 %collective-permute-start.1 = (bf16[32,4224]{1,0:T(8,128)(2,1)S(1)}, bf16[32,4224]{1,0:T(8,128)(2,1)S(1)}, u32[]{:S(2)}, u32[]{:S(2)}) collective-permute-start(bf16[32,4224]{1,0:T(8,128)(2,1)S(1)} %get-tuple-element.18.refs_0_), channel_id=1, source_target_pairs={{0,16},{8,24},{16,0},{24,8},{1,17},{9,25},{17,1},{25,9},{2,18},{10... | collective-permute-start | bytes 811016 | tf_op jit(solution)/shard_map/ppermute | solution.py:227
  10.4 1.6 %collective-permute-start.2 = (bf16[32,4096]{1,0:T(8,128)(2,1)S(1)}, bf16[32,4096]{1,0:T(8,128)(2,1)S(1)}, u32[]{:S(2)}, u32[]{:S(2)}) collective-permute-start(bf16[32,4096]{1,0:T(8,128)(2,1)S(1)} %copy-done), channel_id=1, source_target_pairs={{0,8},{8,0},{16,24},{24,16},{1,9},{9,1},{17,25},{25,17},{2,10},{10... | collective-permute-start | bytes 786440 | tf_op jit(solution)/shard_map/ppermute | solution.py:227
  10.5 1.9 %collective-permute-start.4 = (bf16[32,4096]{1,0:T(8,128)(2,1)S(1)}, bf16[32,4096]{1,0:T(8,128)(2,1)S(1)}, u32[]{:S(2)}, u32[]{:S(2)}) collective-permute-start(bf16[32,4096]{1,0:T(8,128)(2,1)S(1)} %collective-permute-done.3.refs_2_), channel_id=1, source_target_pairs={{0,8},{8,0},{16,24},{24,16},{1,9},{9,1},{17,25},{25,17},{2,10},{10... | collective-permute-start | bytes 786440 | tf_op jit(solution)/shard_map/ppermute | solution.py:227
  11.0 8.5 %collective-permute-start = (bf16[32,4224]{1,0:T(8,128)(2,1)S(1)}, bf16[32,4224]{1,0:T(8,128)(2,1)S(1)}, u32[]{:S(2)}, u32[]{:S(2)}) collective-permute-start(bf16[32,4224]{1,0:T(8,128)(2,1)S(1)} %get-tuple-element.18.refs_0_), channel_id=1, source_target_pairs={{0,8},{8,0},{16,24},{24,16},{1,9},{9,1},{17,25},{25,17},{2,10},{10... | collective-permute-start | bytes 811016 | tf_op jit(solution)/shard_map/ppermute | solution.py:227
  19.4 1.6 %collective-permute-start.5 = (bf16[32,4224]{1,0:T(8,128)(2,1)S(1)}, bf16[32,4224]{1,0:T(8,128)(2,1)S(1)}, u32[]{:S(2)}, u32[]{:S(2)}) collective-permute-start(bf16[32,4224]{1,0:T(8,128)(2,1)S(1)} %collective-permute-done.1.refs_2_), channel_id=1, source_target_pairs={{0,8},{8,0},{16,24},{24,16},{1,9},{9,1},{17,25},{25,17},{2,10},{10... | collective-permute-start | bytes 811016 | tf_op jit(solution)/shard_map/ppermute | solution.py:227

commit v7 on v6

--- a/solution.py
+++ b/solution.py
@@ -88,8 +88,14 @@
     return copies
 
 
-def load_pack_kernel(plan, logits, routes, cotangent, gate, up, packed, gate_near, up_near, *scratch):
-    logits_near, routes_near, columns, sems, load_sems = scratch
+def load_kernel(plan, *refs):
+    count = len(plan)
+    sources, nears, sems = refs[:count], refs[count + 1 : 2 * count + 1], refs[-1]
+    for copy in start_loads(plan, sources, nears, sems):
+        copy.wait()
+
+
+def pack_kernel(logits, routes, cotangent, packed, logits_near, routes_near, columns, sems):
     model_width = cotangent.shape[1]
     copies = [
         pltpu.make_async_copy(logits, logits_near, sems.at[0]),
@@ -98,7 +104,6 @@
     ]
     for copy in copies:
         copy.start()
-    loads = start_loads(plan, [gate, up], [gate_near, up_near], load_sems)
     columns[...] = jnp.zeros(columns.shape, jnp.float32)
     copies[0].wait()
     left = logits_near[...]
@@ -111,8 +116,6 @@
     columns[:, 3 * experts_all : 3 * experts_all + routes.shape[0]] = routes_near[...].astype(jnp.float32).T
     packed[:, model_width:] = columns[...].astype(jnp.bfloat16)
     copies[2].wait()
-    for copy in loads:
-        copy.wait()
 
 
 def blocks_of(buffers, unit):
@@ -129,48 +132,63 @@
     return gate_pre / (1.0 + jnp.exp(-gate_pre)) * up_pre
 
 
-def hidden_kernel(distances, plan, size, *refs, accs=()):
+def stream_hidden(rows, lanes, size, accs, ready, hidden):
+    def finish(place, dots):
+        gate_pre, up_pre = dots
+        hidden[place] = gate_pre / (1.0 + jnp.exp(-gate_pre)) * up_pre
+
+    stream_dots(rows, lanes, size, accs, ready, finish)
+
+
+def first_hidden_kernel(distances, plan, size, *refs, accs=()):
     count = len(distances)
     pieces, refs = refs[:count], refs[count:]
-    gate, up_near, up_far, down_far, hidden, mine, down_near, rows, up_late, sems, mine_sem = refs
-    loads = start_loads(plan, [up_far, down_far], [up_late, down_near], sems)
-    late = up_late.shape[0]
+    gate, up, up_far, gate_far, hidden, mine, gate_late, up_late, rows, up_mid, sems, mine_sem = refs
+    loads = start_loads(plan, [up_far, gate_far, up_far], [up_mid, gate_late, up_late], sems)
     place_rows(pieces, distances, rows)
     width = mine.shape[1]
     start = pl.multiple_of(lax.axis_index("dp") * width, width)
     own = pltpu.make_async_copy(rows.at[:, pl.ds(start, width)], mine, mine_sem)
     own.start()
-    places, unit = hidden.shape[:2]
-    lanes = [blocks_of([gate], unit), blocks_of([up_near, up_late], unit)]
-    per_chunk = places // gate.shape[0]
-    waited = [0]
+    unit = hidden.shape[1]
+    waited = up_mid.shape[0]
 
     def ready(group):
-        needed = -(-(group + 1) * size // per_chunk) - up_near.shape[0]
-        while waited[0] < min(needed, late):
-            loads[waited[0]].wait()
-            waited[0] += 1
-
-    def finish(place, dots):
-        gate_pre, up_pre = dots
-        hidden[place] = gate_pre / (1.0 + jnp.exp(-gate_pre)) * up_pre
-
-    stream_dots(rows, lanes, size, accs, ready, finish)
+        if group == 1:
+            for copy in loads[:waited]:
+                copy.wait()
+
+    lanes = [blocks_of([gate], unit), blocks_of([up, up_mid], unit)]
+    stream_hidden(rows, lanes, size, accs, ready, hidden)
     own.wait()
-    for copy in loads[late:]:
+    for copy in loads[waited:]:
+        copy.wait()
+
+
+def second_hidden_kernel(distances, plan, size, *refs, accs=()):
+    count = len(distances)
+    pieces, refs = refs[:count], refs[count:]
+    gate, up, down_far, after, hidden, down_near, rows, sems = refs
+    loads = start_loads(plan, [down_far], [down_near], sems)
+    place_rows(pieces, distances, rows)
+    unit = hidden.shape[1]
+    lanes = [blocks_of([gate], unit), blocks_of([up], unit)]
+    stream_hidden(rows, lanes, size, accs, lambda group: None, hidden)
+    for copy in loads:
         copy.wait()
 
 
 def score_kernel(distances, plan, top, *refs, accs=()):
     count = len(distances)
     pieces, refs = refs[:count], refs[count:]
-    hidden, down_near, down_far, partial, probs, chosen, rows, down_late, sems = refs
+    hidden_0, hidden_1, down_near, down_far, partial, probs, chosen, rows, down_late, sems = refs
     loads = start_loads(plan, [down_far], [down_late], sems)
     model_width = down_far.shape[2]
     experts_all = probs.shape[0]
     place_rows(pieces, distances, rows)
     local_experts = partial.shape[1]
-    blocks = blocks_of([down_near, down_late], hidden.shape[1])
+    blocks = blocks_of([down_near, down_late], hidden_0.shape[1])
+    hidden = [held.at[place] for held in (hidden_0, hidden_1) for place in range(held.shape[0])]
     per_expert = len(blocks) // local_experts
     size = len(blocks) // 4
     order = [
@@ -196,13 +214,14 @@
                 copy.wait()
 
     def finish(place, dots):
+        if place == 0:
+            routing()
         for lane, paired in zip(order, dots):
             block = lane[place]
-            product = hidden[block] * paired
+            product = hidden[block][...] * paired
             expert = block // per_expert
             sums[expert] = product if sums[expert] is None else sums[expert] + product
 
-    routing()
     lanes = [[blocks[block] for block in lane] for lane in order]
     stream_dots(rows.at[:, :model_width], lanes, size, accs, ready, finish)
     lines = [jnp.sum(term, axis=0, keepdims=True) for term in sums]
@@ -242,8 +261,8 @@
     extra = -(-(3 * experts_all + top) // 128) * 128
     chips = data_count // CORES
     distances = [chip * CORES + core for chip in range(chips) for core in range(CORES)]
-    up_cut = chunks // 2
-    down_cut = 2 * chunks // 3
+    first = 2 * chunks // 3
+    down_cut = chunks // 2
 
     vmem = pl.BlockSpec(memory_space=pltpu.VMEM)
     hbm = pl.BlockSpec(memory_space=pltpu.HBM)
@@ -276,56 +295,76 @@
 
     tokens_beside = swap(tokens, "dp", 1)
     tokens_far = [swap(tokens, "dp", chip * CORES) for chip in range(1, chips)]
-    plan = [(0, chunks), (0, up_cut)]
-    packed, gate_near, up_near = pl.pallas_call(
-        functools.partial(load_pack_kernel, plan),
-        out_shape=(
-            jax.ShapeDtypeStruct((tok_dev, model_width + extra), jnp.bfloat16),
-            near(*plan[0]),
-            near(*plan[1]),
-        ),
-        in_specs=[hbm] * 5,
-        out_specs=(vmem,) * 3,
+    packed = pl.pallas_call(
+        pack_kernel,
+        out_shape=jax.ShapeDtypeStruct((tok_dev, model_width + extra), jnp.bfloat16),
+        in_specs=[hbm] * 3,
+        out_specs=vmem,
         scratch_shapes=[
             pltpu.VMEM((tok_dev, experts_all), jnp.float32),
             pltpu.VMEM((top, tok_dev), jnp.int32),
             pltpu.VMEM((tok_dev, extra), jnp.float32),
             pltpu.SemaphoreType.DMA((3,)),
-            pltpu.SemaphoreType.DMA((chunks + up_cut,)),
         ],
         compiler_params=scoped(0),
-        cost_estimate=cost(chunks + up_cut, 0),
-        name="load_pack",
-    )(keep_far(logits), keep_far(routes.T), keep_far(cotangent), gate, up)
+        cost_estimate=cost(1, 0),
+        name="pack",
+    )(keep_far(logits), keep_far(routes.T), keep_far(cotangent))
     packed_far = [swap(packed, "dp", chip * CORES) for chip in range(1, chips)]
     packed_beside = swap(packed, "dp", 1)
+    plan = [(0, first), (0, first - 1)]
+    gate_near, up_near = pl.pallas_call(
+        functools.partial(load_kernel, plan),
+        out_shape=[near(*part) for part in plan],
+        in_specs=[hbm, hbm, anywhere],
+        out_specs=[vmem, vmem],
+        scratch_shapes=[pltpu.SemaphoreType.DMA((2 * first - 1,))],
+        compiler_params=scoped(0),
+        cost_estimate=cost(2 * first - 1, 0),
+        name="load",
+    )(gate, up, packed)
     tokens_far, gate_near, up_near = lax.optimization_barrier((tokens_far, gate_near, up_near))
     token_pieces = [tokens, tokens_beside]
     for far in tokens_far:
         token_pieces += [far, swap(far, "dp", 1)]
-    plan = [(up_cut, chunks), (0, down_cut)]
-    loads = chunks - up_cut + down_cut
-    hidden, mine, down_near = pl.pallas_call(
-        with_accs(functools.partial(hidden_kernel, distances, plan, size), accs(size)),
+    plan = [(first - 1, first), (first, chunks), (first, chunks)]
+    loads = 1 + 2 * (chunks - first)
+    places = units * first // chunks
+    rows_scratch = pltpu.VMEM((total_tokens, model_width), jnp.bfloat16)
+    hidden_0, mine, gate_late, up_late = pl.pallas_call(
+        with_accs(functools.partial(first_hidden_kernel, distances, plan, size), accs(size)),
         out_shape=(
-            jax.ShapeDtypeStruct((units, unit, total_tokens), jnp.float32),
+            jax.ShapeDtypeStruct((places, unit, total_tokens), jnp.float32),
             jax.ShapeDtypeStruct((total_tokens, model_width // data_count), jnp.bfloat16),
             near(*plan[1]),
+            near(*plan[2]),
         ),
         in_specs=[vmem] * (data_count + 2) + [hbm] * 2,
-        out_specs=(vmem,) * 3,
+        out_specs=(vmem,) * 4,
         scratch_shapes=[
-            pltpu.VMEM((total_tokens, model_width), jnp.bfloat16),
+            rows_scratch,
             near(*plan[0]),
             pltpu.SemaphoreType.DMA((loads,)),
             pltpu.SemaphoreType.DMA,
         ],
-        compiler_params=scoped((chunks - up_cut) * cut[1] * cut[2] * 2 + (1 if accs(size) else 3) * row_bytes),
-        cost_estimate=cost(loads, 2 * chunks),
-        name="hidden",
-    )(*token_pieces, gate_near, up_near, up, down)
-
-    packed_far, hidden = lax.optimization_barrier((packed_far, hidden))
+        compiler_params=scoped(cut[1] * cut[2] * 2 + (1 if accs(size) else 3) * row_bytes),
+        cost_estimate=cost(loads, 2 * first),
+        name="hidden_first",
+    )(*token_pieces, gate_near, up_near, up, gate)
+
+    packed_far, hidden_0 = lax.optimization_barrier((packed_far, hidden_0))
+    plan = [(0, down_cut)]
+    hidden_1, down_near = pl.pallas_call(
+        with_accs(functools.partial(second_hidden_kernel, distances, plan, size), accs(size)),
+        out_shape=(jax.ShapeDtypeStruct((units - places, unit, total_tokens), jnp.float32), near(*plan[0])),
+        in_specs=[vmem] * (data_count + 2) + [hbm, anywhere],
+        out_specs=(vmem, vmem),
+        scratch_shapes=[rows_scratch, pltpu.SemaphoreType.DMA((down_cut,))],
+        compiler_params=scoped((1 if accs(size) else 3) * row_bytes),
+        cost_estimate=cost(down_cut, 2 * (chunks - first)),
+        name="hidden_second",
+    )(*token_pieces, gate_late, up_late, down, packed_far[0])
+
     packed_pieces = [packed, packed_beside]
     for far in packed_far:
         packed_pieces += [far, swap(far, "dp", 1)]
@@ -339,7 +378,7 @@
             table,
             table,
         ),
-        in_specs=[vmem] * (data_count + 2) + [hbm],
+        in_specs=[vmem] * (data_count + 3) + [hbm],
         out_specs=(vmem, vmem, vmem),
         scratch_shapes=[
             pltpu.VMEM((total_tokens, model_width + extra), jnp.bfloat16),
@@ -349,7 +388,7 @@
         compiler_params=scoped((chunks - down_cut) * cut[1] * cut[2] * 2 + 3 * row_bytes),
         cost_estimate=cost(chunks - down_cut, chunks),
         name="scores",
-    )(*packed_pieces, hidden, down_near, down)
+    )(*packed_pieces, hidden_0, hidden_1, down_near, down)
 
     score_blocks = lax.all_to_all(partial, ("dp", "expert"), split_axis=0, concat_axis=0, tiled=True)
 

time: 39.4 us -> 40.8 us (1.036)
  Pallas kernels: 18.5 us -> 20.6 us
  waiting for transfers between devices: 2.72 us -> 1.83 us
    pallas_call x2 -> x4, Pallas kernels: 13.6 us -> 15 us  [the longest x1 5.35 us: per_device(): pl.pallas_call(functools.partial(load_kernel, plan), out_shape=[near(*par...]
    ppermute x6, waiting for transfers between devices: 2.72 us -> 1.83 us  [swap(): lax.ppermute(value, axis, [(index, index ^ distance) for index in range(l...]
    pallas_call x1, Pallas kernels: 4.08 us -> 4.74 us  [per_device(): pl.pallas_call(with_accs(functools.partial(score_kernel, distances, plan,...]
  transfers between devices with their start and end apart: 6 -> 6, of which waited for: 3 -> 2; matrix products, arithmetic and copies ran while one was open for 0% -> 0% of each run, Pallas kernels for 35% -> 37%
where the time goes in v7:
time: 40.8 us; the launch traced here: 40.5 us
  Pallas kernels  20.6 us (50%)
  blocking collectives  13.5 us (33%)
  starting transfers between devices  3.89 us (10%)
  waiting for transfers between devices  1.83 us (4%)
  between operations  0.71 us (2%)
    all_to_all x1, blocking collectives, per_device(): lax.all_to_all(partial, ('dp', 'expert'), split_axis=0, concat_axis=0, ti...  13.5 us
    pallas_call x1, Pallas kernels, per_device(): pl.pallas_call(functools.partial(load_kernel, plan), out_shape=[near(*par...  5.35 us
    pallas_call x1, Pallas kernels, per_device(): pl.pallas_call(with_accs(functools.partial(score_kernel, distances, plan,...  4.74 us
    pallas_call x1, Pallas kernels, per_device(): pl.pallas_call(with_accs(functools.partial(first_hidden_kernel, distances...  4.72 us
    pallas_call x1, Pallas kernels, per_device(): pl.pallas_call(with_accs(functools.partial(second_hidden_kernel, distance...  3.91 us
    ppermute x6, starting transfers between devices, swap(): lax.ppermute(value, axis, [(index, index ^ distance) for index in range(l...  3.89 us
    ppermute x6, waiting for transfers between devices, swap(): lax.ppermute(value, axis, [(index, index ^ distance) for index in range(l...  1.83 us
    pallas_call x1, Pallas kernels, per_device(): pl.pallas_call(pack_kernel, out_shape=jax.ShapeDtypeStruct((tok_dev, mode...  1.01 us
  transfers between devices with their start and end apart: 6, of which 2 were waited for; matrix products, arithmetic and copies ran while one was open for 0% of the time, Pallas kernels for 37%

profile of v7, /device:TPU:0, one launch (start us, length us, event | category | flops | bytes accessed | tf_op | source)
XLA Modules:
  0.0 40.5 jit_solution(8737950980416232110)
XLA Ops:
  0.6 3.0 %collective-permute-start.3 = (bf16[32,4096]{1,0:T(8,128)(2,1)}, bf16[32,4096]{1,0:T(8,128)(2,1)S(1)}, u32[]{:S(2)}, u32[]{:S(2)}) collective-permute-start(bf16[32,4096]{1,0:T(8,128)(2,1)} %refs_0_.3), channel_id=1, source_target_pairs={{0,16},{8,24},{16,0},{24,8},{1,17},{9,25},{17,1},{25,9},{2,18},{10... | collective-permute-start | bytes 786440 | tf_op jit(solution)/shard_map/ppermute | solution.py:246
  3.7 1.0 %pack.1.refs_2_.refs_0_ = bf16[32,4224]{1,0:T(8,128)(2,1)S(1)} custom-call(f32[32,32]{1,0:T(8,128)} %logits.1, s32[8,32]{1,0:T(8,128)} %bitcast.11, bf16[32,4096]{1,0:T(8,128)(2,1)} %cotangent.1), custom_call_target="tpu_custom_call" | custom-call | bytes 1 | tf_op jit(solution)/shard_map/pack/pallas_call | solution.py:298
  4.7 0.1 collective-permute-start.1
  4.8 0.1 collective-permute-start.2
  4.8 0.0 copy-start
  4.8 5.4 %load.1 = (bf16[4,256,4096]{2,1,0:T(8,128)(2,1)S(1)}, bf16[3,256,4096]{2,1,0:T(8,128)(2,1)S(1)}) custom-call(bf16[6,256,4096]{2,1,0:T(8,128)(2,1)} %bitcast.7, bf16[6,256,4096]{2,1,0:T(8,128)(2,1)} %bitcast.9, bf16[32,4224]{1,0:T(8,128)(2,1)S(1)} %pack.1.refs_2_.refs_0_), custom_call_target="tpu_custom_call" | custom-call | bytes 7 | tf_op jit(solution)/shard_map/load/pallas_call | solution.py:316
  10.2 0.8 %collective-permute-done.3.refs_2_ = bf16[32,4096]{1,0:T(8,128)(2,1)S(1)} collective-permute-done((bf16[32,4096]{1,0:T(8,128)(2,1)}, bf16[32,4096]{1,0:T(8,128)(2,1)S(1)}, u32[]{:S(2)}, u32[]{:S(2)}) %collective-permute-start.3) | collective-permute-done | bytes 262176 | tf_op jit(solution)/shard_map/ppermute | solution.py:246
  11.0 0.0 collective-permute-start.4
  11.0 0.5 %collective-permute-start = (bf16[32,4224]{1,0:T(8,128)(2,1)S(1)}, bf16[32,4224]{1,0:T(8,128)(2,1)S(1)}, u32[]{:S(2)}, u32[]{:S(2)}) collective-permute-start(bf16[32,4224]{1,0:T(8,128)(2,1)S(1)} %pack.1.refs_2_.refs_0_), channel_id=1, source_target_pairs={{0,8},{8,0},{16,24},{24,16},{1,9},{9,1},{17,25},{25,17},{2,10},{10... | collective-permute-start | bytes 811016 | tf_op jit(solution)/shard_map/ppermute | solution.py:246
  11.5 0.0 collective-permute-done.2.refs_1_
  11.5 1.0 %collective-permute-done.4.refs_3_ = bf16[32,4096]{1,0:T(8,128)(2,1)S(1)} collective-permute-done((bf16[32,4096]{1,0:T(8,128)(2,1)S(1)}, bf16[32,4096]{1,0:T(8,128)(2,1)S(1)}, u32[]{:S(2)}, u32[]{:S(2)}) %collective-permute-start.4) | collective-permute-done | bytes 262176 | tf_op jit(solution)/shard_map/ppermute | solution.py:246
  12.5 0.0 copy-done
  12.5 4.7 %hidden_first.1 = (f32[8,128,128]{2,1,0:T(8,128)S(1)}, bf16[128,1024]{1,0:T(8,128)(2,1)S(1)}, bf16[2,256,4096]{2,1,0:T(8,128)(2,1)S(1)}, bf16[2,256,4096]{2,1,0:T(8,128)(2,1)S(1)}) custom-call(bf16[32,4096]{1,0:T(8,128)(2,1)S(1)} %copy-done, bf16[32,4096]{1,0:T(8,128)(2,1)S(1)} %collective-permute-done.2.refs_1_, ...), custom_call_target="tpu_custom_call" | custom-call | flops 8 | bytes 5 | tf_op jit(solution)/shard_map/hidden_first/pallas_call | solution.py:334
  17.3 0.0 collective-permute-done.1.refs_7_.refs_2_
  17.3 0.2 collective-permute-start.5
  17.5 3.9 %hidden_second.1 = (f32[4,128,128]{2,1,0:T(8,128)S(1)}, bf16[3,256,4096]{2,1,0:T(8,128)(2,1)S(1)}) custom-call(bf16[32,4096]{1,0:T(8,128)(2,1)S(1)} %copy-done, bf16[32,4096]{1,0:T(8,128)(2,1)S(1)} %collective-permute-done.2.refs_1_, bf16[32,4096]{1,0:T(8,128)(2,1)S(1)} %collective-permute-done.3.refs_2_, ...), custom_call_target="tpu_custom_call" | custom-call | flops 4 | bytes 3 | tf_op jit(solution)/shard_map/hidden_second/pallas_call | solution.py:357
  21.4 0.0 collective-permute-done.refs_1_
  21.4 0.0 collective-permute-done.5.refs_3_
  21.4 4.7 %scores.1 = (f32[32,4,128]{2,1,0:T(4,128)S(1)}, f32[32,128]{1,0:T(8,128)S(1)}, f32[32,128]{1,0:T(8,128)S(1)}) custom-call(bf16[32,4224]{1,0:T(8,128)(2,1)S(1)} %pack.1.refs_2_.refs_0_, bf16[32,4224]{1,0:T(8,128)(2,1)S(1)} %collective-permute-done.refs_1_, bf16[32,4224]{1,0:T(8,128)(2,1)S(1)} %collective-permute-done.1.refs_7_.refs_2_, ...), custom_call_target="tpu_custom_call" | custom-call | flops 6 | bytes 3 | tf_op jit(solution)/shard_map/scores/pallas_call | solution.py:374
  26.2 13.5 %all_to_all.5.blocks = f32[32,4,128]{2,1,0:T(4,128)S(1)} all-to-all(f32[32,4,128]{2,1,0:T(4,128)S(1)} %get-tuple-element.32), channel_id=1, replica_groups=mesh['dp'=4,'expert'=8] {'dp','expert'}, dimensions={0} | all-to-all | bytes 131072 | tf_op jit(solution)/shard_map/all_to_all | solution.py:393
  39.7 0.8 %gradient.1 = (f32[32,32]{1,0:T(8,128)}, f32[32,1024]{1,0:T(8,128)}) custom-call(f32[32,4,128]{2,1,0:T(4,128)S(1)} %all_to_all.5.blocks, f32[32,128]{1,0:T(8,128)S(1)} %get-tuple-element.33.probs_ref, f32[32,128]{1,0:T(8,128)S(1)} %get-tuple-element.34.chosen_ref, bf16[128,1024]{1,0:T(8,128)(2,1)S(1)} %get-tuple-element.35.mine), custom_call_target="tpu_custom_call" | custom-call | tf_op jit(solution)/shard_map/gradient/pallas_call | solution.py:395
Async XLA Ops:
  0.6 10.4 %collective-permute-start.3 = (bf16[32,4096]{1,0:T(8,128)(2,1)}, bf16[32,4096]{1,0:T(8,128)(2,1)S(1)}, u32[]{:S(2)}, u32[]{:S(2)}) collective-permute-start(bf16[32,4096]{1,0:T(8,128)(2,1)} %refs_0_.3), channel_id=1, source_target_pairs={{0,16},{8,24},{16,0},{24,8},{1,17},{9,25},{17,1},{25,9},{2,18},{10... | collective-permute-start | bytes 786440 | tf_op jit(solution)/shard_map/ppermute | solution.py:246
  4.7 12.6 %collective-permute-start.1 = (bf16[32,4224]{1,0:T(8,128)(2,1)S(1)}, bf16[32,4224]{1,0:T(8,128)(2,1)S(1)}, u32[]{:S(2)}, u32[]{:S(2)}) collective-permute-start(bf16[32,4224]{1,0:T(8,128)(2,1)S(1)} %pack.1.refs_2_.refs_0_), channel_id=1, source_target_pairs={{0,16},{8,24},{16,0},{24,8},{1,17},{9,25},{17,1},{25,9},{2,18},{10... | collective-permute-start | bytes 811016 | tf_op jit(solution)/shard_map/ppermute | solution.py:246
  4.8 6.8 %collective-permute-start.2 = (bf16[32,4096]{1,0:T(8,128)(2,1)}, bf16[32,4096]{1,0:T(8,128)(2,1)S(1)}, u32[]{:S(2)}, u32[]{:S(2)}) collective-permute-start(bf16[32,4096]{1,0:T(8,128)(2,1)} %refs_0_.3), channel_id=1, source_target_pairs={{0,8},{8,0},{16,24},{24,16},{1,9},{9,1},{17,25},{25,17},{2,10},{10... | collective-permute-start | bytes 786440 | tf_op jit(solution)/shard_map/ppermute | solution.py:246
  4.8 7.7 %copy-start = (bf16[32,4096]{1,0:T(8,128)(2,1)S(1)}, bf16[32,4096]{1,0:T(8,128)(2,1)}, u32[]{:S(2)}) copy-start(bf16[32,4096]{1,0:T(8,128)(2,1)} %refs_0_.3) | copy-start | bytes 786436
  11.0 1.5 %collective-permute-start.4 = (bf16[32,4096]{1,0:T(8,128)(2,1)S(1)}, bf16[32,4096]{1,0:T(8,128)(2,1)S(1)}, u32[]{:S(2)}, u32[]{:S(2)}) collective-permute-start(bf16[32,4096]{1,0:T(8,128)(2,1)S(1)} %collective-permute-done.3.refs_2_), channel_id=1, source_target_pairs={{0,8},{8,0},{16,24},{24,16},{1,9},{9,1},{17,25},{25,17},{2,10},{10... | collective-permute-start | bytes 786440 | tf_op jit(solution)/shard_map/ppermute | solution.py:246
  11.0 10.4 %collective-permute-start = (bf16[32,4224]{1,0:T(8,128)(2,1)S(1)}, bf16[32,4224]{1,0:T(8,128)(2,1)S(1)}, u32[]{:S(2)}, u32[]{:S(2)}) collective-permute-start(bf16[32,4224]{1,0:T(8,128)(2,1)S(1)} %pack.1.refs_2_.refs_0_), channel_id=1, source_target_pairs={{0,8},{8,0},{16,24},{24,16},{1,9},{9,1},{17,25},{25,17},{2,10},{10... | collective-permute-start | bytes 811016 | tf_op jit(solution)/shard_map/ppermute | solution.py:246
  17.3 4.1 %collective-permute-start.5 = (bf16[32,4224]{1,0:T(8,128)(2,1)S(1)}, bf16[32,4224]{1,0:T(8,128)(2,1)S(1)}, u32[]{:S(2)}, u32[]{:S(2)}) collective-permute-start(bf16[32,4224]{1,0:T(8,128)(2,1)S(1)} %collective-permute-done.1.refs_7_.refs_2_), channel_id=1, source_target_pairs={{0,8},{8,0},{16,24},{24,16},{1,9},{9,1},{17,25},{25,17},{2,10},{10... | collective-permute-start | bytes 811016 | tf_op jit(solution)/shard_map/ppermute | solution.py:246

commit v8 on v6

--- a/solution.py
+++ b/solution.py
@@ -115,6 +115,11 @@
         copy.wait()
 
 
+def load_kernel(plan, source, after, near, sems):
+    for copy in start_loads(plan, [source], [near], sems):
+        copy.wait()
+
+
 def blocks_of(buffers, unit):
     return [
         buffer.at[chunk, first : first + unit]
@@ -164,13 +169,13 @@
 def score_kernel(distances, plan, top, *refs, accs=()):
     count = len(distances)
     pieces, refs = refs[:count], refs[count:]
-    hidden, down_near, down_far, partial, probs, chosen, rows, down_late, sems = refs
+    hidden, down_near, down_mid, down_far, partial, probs, chosen, rows, down_late, sems = refs
     loads = start_loads(plan, [down_far], [down_late], sems)
     model_width = down_far.shape[2]
     experts_all = probs.shape[0]
     place_rows(pieces, distances, rows)
     local_experts = partial.shape[1]
-    blocks = blocks_of([down_near, down_late], hidden.shape[1])
+    blocks = blocks_of([down_near, down_mid, down_late], hidden.shape[1])
     per_expert = len(blocks) // local_experts
     size = len(blocks) // 4
     order = [
@@ -196,20 +201,21 @@
                 copy.wait()
 
     def finish(place, dots):
+        if place == 0:
+            routing()
         for lane, paired in zip(order, dots):
             block = lane[place]
             product = hidden[block] * paired
             expert = block // per_expert
             sums[expert] = product if sums[expert] is None else sums[expert] + product
 
-    routing()
     lanes = [[blocks[block] for block in lane] for lane in order]
     stream_dots(rows.at[:, :model_width], lanes, size, accs, ready, finish)
     lines = [jnp.sum(term, axis=0, keepdims=True) for term in sums]
     partial[...] = jnp.broadcast_to(jnp.concatenate(lines, axis=0)[None], partial.shape)
 
 
-def gradient_kernel(data_count, blocks, probs_ref, chosen_ref, mine, logit_grad, router_grad, grads):
+def gradient_kernel(data_count, blocks, probs_ref, chosen_ref, mine, logit_grad, router_grad, grads, held, sems):
     experts_all, total_tokens = probs_ref.shape
     scores = jnp.sum(blocks[...].reshape((data_count, experts_all, total_tokens)), axis=0)
     probs, chosen = probs_ref[...], chosen_ref[...]
@@ -217,10 +223,20 @@
     weighted = jnp.sum(probs * chosen * scores, axis=0, keepdims=True)
     prob_grad = scores / mass - chosen * weighted / (mass * mass)
     grad = probs * (prob_grad - jnp.sum(probs * prob_grad, axis=0, keepdims=True))
-    router_grad[...] = jnp.dot(grad.astype(jnp.bfloat16), mine[...], preferred_element_type=jnp.float32)
+    half = mine.shape[1] // 2
+    copies = []
+    for number in range(2):
+        part = pl.ds(number * half, half)
+        held[:, part] = jnp.dot(grad.astype(jnp.bfloat16), mine[:, part], preferred_element_type=jnp.float32)
+        copies.append(pltpu.make_async_copy(held.at[:, part], router_grad.at[:, part], sems.at[number]))
+        copies[number].start()
     grads[...] = grad.T
     tok_dev = logit_grad.shape[0]
-    logit_grad[...] = grads[pl.ds(pl.multiple_of(lax.axis_index("dp") * tok_dev, tok_dev), tok_dev), :]
+    start = pl.multiple_of(lax.axis_index("dp") * tok_dev, tok_dev)
+    copies.append(pltpu.make_async_copy(grads.at[pl.ds(start, tok_dev)], logit_grad, sems.at[2]))
+    copies[2].start()
+    for copy in copies:
+        copy.wait()
 
 
 def swap(value, axis, distance):
@@ -242,7 +258,7 @@
     extra = -(-(3 * experts_all + top) // 128) * 128
     chips = data_count // CORES
     distances = [chip * CORES + core for chip in range(chips) for core in range(CORES)]
-    up_cut = chunks // 2
+    up_cut = chunks // 3
     down_cut = 2 * chunks // 3
 
     vmem = pl.BlockSpec(memory_space=pltpu.VMEM)
@@ -329,8 +345,19 @@
     packed_pieces = [packed, packed_beside]
     for far in packed_far:
         packed_pieces += [far, swap(far, "dp", 1)]
-
-    plan = [(down_cut, chunks)]
+    plan = [(down_cut, down_cut + 1)]
+    down_mid = pl.pallas_call(
+        functools.partial(load_kernel, plan),
+        out_shape=near(*plan[0]),
+        in_specs=[hbm, anywhere],
+        out_specs=vmem,
+        scratch_shapes=[pltpu.SemaphoreType.DMA((1,))],
+        compiler_params=scoped(0),
+        cost_estimate=cost(1, 0),
+        name="load_down",
+    )(down, packed_far[0])
+
+    plan = [(down_cut + 1, chunks)]
     table = jax.ShapeDtypeStruct((experts_all, total_tokens), jnp.float32)
     partial, probs, chosen = pl.pallas_call(
         with_accs(functools.partial(score_kernel, distances, plan, top), accs(units // 4)),
@@ -339,17 +366,17 @@
             table,
             table,
         ),
-        in_specs=[vmem] * (data_count + 2) + [hbm],
+        in_specs=[vmem] * (data_count + 3) + [hbm],
         out_specs=(vmem, vmem, vmem),
         scratch_shapes=[
             pltpu.VMEM((total_tokens, model_width + extra), jnp.bfloat16),
             near(*plan[0]),
-            pltpu.SemaphoreType.DMA((chunks - down_cut,)),
+            pltpu.SemaphoreType.DMA((chunks - down_cut - 1,)),
         ],
-        compiler_params=scoped((chunks - down_cut) * cut[1] * cut[2] * 2 + 3 * row_bytes),
+        compiler_params=scoped((chunks - down_cut - 1) * cut[1] * cut[2] * 2 + 3 * row_bytes),
         cost_estimate=cost(chunks - down_cut, chunks),
         name="scores",
-    )(*packed_pieces, hidden, down_near, down)
+    )(*packed_pieces, hidden, down_near, down_mid, down)
 
     score_blocks = lax.all_to_all(partial, ("dp", "expert"), split_axis=0, concat_axis=0, tiled=True)
 
@@ -360,8 +387,12 @@
             jax.ShapeDtypeStruct((experts_all, model_width // data_count), jnp.float32),
         ),
         in_specs=[vmem] * 4,
-        out_specs=(vmem, vmem),
-        scratch_shapes=[pltpu.VMEM((total_tokens, experts_all), jnp.float32)],
+        out_specs=(hbm, hbm),
+        scratch_shapes=[
+            pltpu.VMEM((total_tokens, experts_all), jnp.float32),
+            pltpu.VMEM((experts_all, model_width // data_count), jnp.float32),
+            pltpu.SemaphoreType.DMA((3,)),
+        ],
         compiler_params=scoped(4 << 20),
         name="gradient",
     )(score_blocks, probs, chosen, mine)

time: 39.4 us -> 38.5 us (0.977)
  waiting for transfers between devices: 2.72 us -> 1.39 us
  Pallas kernels: 18.5 us -> 19 us
    pallas_call x0 -> x1, Pallas kernels: none -> 1.6 us  [per_device(): pl.pallas_call(functools.partial(load_kernel, plan), out_shape=near(*plan...]
    ppermute x6, waiting for transfers between devices: 2.72 us -> 1.39 us  [swap(): lax.ppermute(value, axis, [(index, index ^ distance) for index in range(l...]
    pallas_call x1, Pallas kernels: 6.68 us -> 6.08 us  [per_device(): pl.pallas_call(functools.partial(load_pack_kernel, plan), out_shape=(jax....]
    pallas_call x1, Pallas kernels: 4.08 us -> 3.56 us  [per_device(): pl.pallas_call(with_accs(functools.partial(score_kernel, distances, plan,...]
  transfers between devices with their start and end apart: 6 -> 6, of which waited for: 3 -> 3; matrix products, arithmetic and copies ran while one was open for 0% -> 0% of each run, Pallas kernels for 35% -> 38%
where the time goes in v8:
time: 38.5 us; the launch traced here: 38.4 us
  Pallas kernels  19 us (49%)
  blocking collectives  13.4 us (35%)
  starting transfers between devices  3.9 us (10%)
  waiting for transfers between devices  1.39 us (4%)
  between operations  0.7 us (2%)
    all_to_all x1, blocking collectives, per_device(): lax.all_to_all(partial, ('dp', 'expert'), split_axis=0, concat_axis=0, ti...  13.4 us
    pallas_call x1, Pallas kernels, per_device(): pl.pallas_call(with_accs(functools.partial(hidden_kernel, distances, plan...  6.92 us
    pallas_call x1, Pallas kernels, per_device(): pl.pallas_call(functools.partial(load_pack_kernel, plan), out_shape=(jax....  6.08 us
    ppermute x6, starting transfers between devices, swap(): lax.ppermute(value, axis, [(index, index ^ distance) for index in range(l...  3.9 us
    pallas_call x1, Pallas kernels, per_device(): pl.pallas_call(with_accs(functools.partial(score_kernel, distances, plan,...  3.56 us
    pallas_call x1, Pallas kernels, per_device(): pl.pallas_call(functools.partial(load_kernel, plan), out_shape=near(*plan...  1.6 us
    ppermute x6, waiting for transfers between devices, swap(): lax.ppermute(value, axis, [(index, index ^ distance) for index in range(l...  1.39 us
    pallas_call x1, Pallas kernels, per_device(): pl.pallas_call(functools.partial(gradient_kernel, data_count), out_shape=...  0.85 us
  transfers between devices with their start and end apart: 6, of which 3 were waited for; matrix products, arithmetic and copies ran while one was open for 0% of the time, Pallas kernels for 38%

profile of v8, /device:TPU:0, one launch (start us, length us, event | category | flops | bytes accessed | tf_op | source)
XLA Modules:
  0.0 38.4 jit_solution(14018780196032463747)
XLA Ops:
  0.6 3.0 %collective-permute-start.3 = (bf16[32,4096]{1,0:T(8,128)(2,1)}, bf16[32,4096]{1,0:T(8,128)(2,1)S(1)}, u32[]{:S(2)}, u32[]{:S(2)}) collective-permute-start(bf16[32,4096]{1,0:T(8,128)(2,1)} %refs_0_.1), channel_id=1, source_target_pairs={{0,16},{8,24},{16,0},{24,8},{1,17},{9,25},{17,1},{25,9},{2,18},{10... | collective-permute-start | bytes 786440 | tf_op jit(solution)/shard_map/ppermute | solution.py:243
  3.7 0.0 copy-start
  3.7 6.1 %load_pack.1 = (bf16[32,4224]{1,0:T(8,128)(2,1)S(1)}, bf16[6,256,4096]{2,1,0:T(8,128)(2,1)S(1)}, bf16[2,256,4096]{2,1,0:T(8,128)(2,1)S(1)}) custom-call(f32[32,32]{1,0:T(8,128)} %logits.1, s32[8,32]{1,0:T(8,128)} %bitcast.11, bf16[32,4096]{1,0:T(8,128)(2,1)} %cotangent.1, bf16[6,256,4096]{2,1,0:T(8,128)(2,1)} %bitcast.10, bf16[6,256,4096]{2,1,0:T(8,128)(2,1)} %bitcast.8), custom_call_target="tpu_custom_call" | custom-call | bytes 8 | tf_op jit(solution)/shard_map/load_pack/pallas_call | solution.py:296
  9.8 0.1 collective-permute-start.1
  9.8 0.0 copy-done
  9.8 0.1 collective-permute-start.2
  9.9 0.3 collective-permute-done.3.refs_2_
  10.2 0.2 collective-permute-start.4
  10.4 0.3 collective-permute-start
  10.7 0.8 %collective-permute-done.2.refs_1_ = bf16[32,4096]{1,0:T(8,128)(2,1)S(1)} collective-permute-done((bf16[32,4096]{1,0:T(8,128)(2,1)S(1)}, bf16[32,4096]{1,0:T(8,128)(2,1)S(1)}, u32[]{:S(2)}, u32[]{:S(2)}) %collective-permute-start.2) | collective-permute-done | bytes 262176 | tf_op jit(solution)/shard_map/ppermute | solution.py:243
  11.4 0.4 collective-permute-done.4.refs_3_
  11.8 6.9 %hidden.1 = (f32[12,128,128]{2,1,0:T(8,128)S(1)}, bf16[128,1024]{1,0:T(8,128)(2,1)S(1)}, bf16[4,256,4096]{2,1,0:T(8,128)(2,1)S(1)}) custom-call(bf16[32,4096]{1,0:T(8,128)(2,1)S(1)} %copy-done, bf16[32,4096]{1,0:T(8,128)(2,1)S(1)} %collective-permute-done.2.refs_1_, bf16[32,4096]{1,0:T(8,128)(2,1)S(1)} %collective-permute-done.3.refs_2_, ...), custom_call_target="tpu_custom_call" | custom-call | flops 12 | bytes 8 | tf_op jit(solution)/shard_map/hidden/pallas_call | solution.py:324
  18.7 0.0 collective-permute-done.1.after.refs_2_
  18.8 0.2 collective-permute-start.5
  19.0 1.6 %load_down.1.refs_6_ = bf16[1,256,4096]{2,1,0:T(8,128)(2,1)S(1)} custom-call(bf16[6,256,4096]{2,1,0:T(8,128)(2,1)} %bitcast.6, bf16[32,4224]{1,0:T(8,128)(2,1)S(1)} %collective-permute-done.1.after.refs_2_), custom_call_target="tpu_custom_call" | custom-call | bytes 1 | tf_op jit(solution)/shard_map/load_down/pallas_call | solution.py:349
  20.6 0.0 collective-permute-done.refs_1_
  20.6 0.0 collective-permute-done.5.refs_3_
  20.6 3.6 %scores.1 = (f32[32,4,128]{2,1,0:T(4,128)S(1)}, f32[32,128]{1,0:T(8,128)S(1)}, f32[32,128]{1,0:T(8,128)S(1)}) custom-call(bf16[32,4224]{1,0:T(8,128)(2,1)S(1)} %get-tuple-element.18.refs_0_, bf16[32,4224]{1,0:T(8,128)(2,1)S(1)} %collective-permute-done.refs_1_, bf16[32,4224]{1,0:T(8,128)(2,1)S(1)} %collective-permute-done.1.after.refs_2_, ...), custom_call_target="tpu_custom_call" | custom-call | flops 6 | bytes 2 | tf_op jit(solution)/shard_map/scores/pallas_call | solution.py:362
  24.2 13.4 %all_to_all.5.blocks = f32[32,4,128]{2,1,0:T(4,128)S(1)} all-to-all(f32[32,4,128]{2,1,0:T(4,128)S(1)} %get-tuple-element.28), channel_id=1, replica_groups=mesh['dp'=4,'expert'=8] {'dp','expert'}, dimensions={0} | all-to-all | bytes 131072 | tf_op jit(solution)/shard_map/all_to_all | solution.py:381
  37.5 0.8 %gradient.1 = (f32[32,32]{1,0:T(8,128)}, f32[32,1024]{1,0:T(8,128)}) custom-call(f32[32,4,128]{2,1,0:T(4,128)S(1)} %all_to_all.5.blocks, f32[32,128]{1,0:T(8,128)S(1)} %get-tuple-element.29.probs_ref, f32[32,128]{1,0:T(8,128)S(1)} %get-tuple-element.30.chosen_ref, bf16[128,1024]{1,0:T(8,128)(2,1)S(1)} %get-tuple-element.31.mine), custom_call_target="tpu_custom_call" | custom-call | tf_op jit(solution)/shard_map/gradient/pallas_call | solution.py:383
Async XLA Ops:
  0.6 9.5 %collective-permute-start.3 = (bf16[32,4096]{1,0:T(8,128)(2,1)}, bf16[32,4096]{1,0:T(8,128)(2,1)S(1)}, u32[]{:S(2)}, u32[]{:S(2)}) collective-permute-start(bf16[32,4096]{1,0:T(8,128)(2,1)} %refs_0_.1), channel_id=1, source_target_pairs={{0,16},{8,24},{16,0},{24,8},{1,17},{9,25},{17,1},{25,9},{2,18},{10... | collective-permute-start | bytes 786440 | tf_op jit(solution)/shard_map/ppermute | solution.py:243
  3.7 6.2 %copy-start = (bf16[32,4096]{1,0:T(8,128)(2,1)S(1)}, bf16[32,4096]{1,0:T(8,128)(2,1)}, u32[]{:S(2)}) copy-start(bf16[32,4096]{1,0:T(8,128)(2,1)} %refs_0_.1) | copy-start | bytes 786436
  9.8 9.0 %collective-permute-start.1 = (bf16[32,4224]{1,0:T(8,128)(2,1)S(1)}, bf16[32,4224]{1,0:T(8,128)(2,1)S(1)}, u32[]{:S(2)}, u32[]{:S(2)}) collective-permute-start(bf16[32,4224]{1,0:T(8,128)(2,1)S(1)} %get-tuple-element.18.refs_0_), channel_id=1, source_target_pairs={{0,16},{8,24},{16,0},{24,8},{1,17},{9,25},{17,1},{25,9},{2,18},{10... | collective-permute-start | bytes 811016 | tf_op jit(solution)/shard_map/ppermute | solution.py:243
  9.8 1.6 %collective-permute-start.2 = (bf16[32,4096]{1,0:T(8,128)(2,1)S(1)}, bf16[32,4096]{1,0:T(8,128)(2,1)S(1)}, u32[]{:S(2)}, u32[]{:S(2)}) collective-permute-start(bf16[32,4096]{1,0:T(8,128)(2,1)S(1)} %copy-done), channel_id=1, source_target_pairs={{0,8},{8,0},{16,24},{24,16},{1,9},{9,1},{17,25},{25,17},{2,10},{10... | collective-permute-start | bytes 786440 | tf_op jit(solution)/shard_map/ppermute | solution.py:243
  10.2 1.6 %collective-permute-start.4 = (bf16[32,4096]{1,0:T(8,128)(2,1)S(1)}, bf16[32,4096]{1,0:T(8,128)(2,1)S(1)}, u32[]{:S(2)}, u32[]{:S(2)}) collective-permute-start(bf16[32,4096]{1,0:T(8,128)(2,1)S(1)} %collective-permute-done.3.refs_2_), channel_id=1, source_target_pairs={{0,8},{8,0},{16,24},{24,16},{1,9},{9,1},{17,25},{25,17},{2,10},{10... | collective-permute-start | bytes 786440 | tf_op jit(solution)/shard_map/ppermute | solution.py:243
  10.4 10.1 %collective-permute-start = (bf16[32,4224]{1,0:T(8,128)(2,1)S(1)}, bf16[32,4224]{1,0:T(8,128)(2,1)S(1)}, u32[]{:S(2)}, u32[]{:S(2)}) collective-permute-start(bf16[32,4224]{1,0:T(8,128)(2,1)S(1)} %get-tuple-element.18.refs_0_), channel_id=1, source_target_pairs={{0,8},{8,0},{16,24},{24,16},{1,9},{9,1},{17,25},{25,17},{2,10},{10... | collective-permute-start | bytes 811016 | tf_op jit(solution)/shard_map/ppermute | solution.py:243
  18.8 1.8 %collective-permute-start.5 = (bf16[32,4224]{1,0:T(8,128)(2,1)S(1)}, bf16[32,4224]{1,0:T(8,128)(2,1)S(1)}, u32[]{:S(2)}, u32[]{:S(2)}) collective-permute-start(bf16[32,4224]{1,0:T(8,128)(2,1)S(1)} %collective-permute-done.1.after.refs_2_), channel_id=1, source_target_pairs={{0,8},{8,0},{16,24},{24,16},{1,9},{9,1},{17,25},{25,17},{2,10},{10... | collective-permute-start | bytes 811016 | tf_op jit(solution)/shard_map/ppermute | solution.py:243

commit v9 on v8

--- a/solution.py
+++ b/solution.py
@@ -15,7 +15,8 @@
 
 
 def stream_dots(rows, lanes, size, accs, ready, finish):
-    groups = [range(first, first + size) for first in range(0, len(lanes[0]), size)]
+    count = len(lanes[0])
+    groups = [range(first, min(first + size, count)) for first in range(0, count, size)]
 
     def dots_of(number, place):
         if not accs:
@@ -115,11 +116,6 @@
         copy.wait()
 
 
-def load_kernel(plan, source, after, near, sems):
-    for copy in start_loads(plan, [source], [near], sems):
-        copy.wait()
-
-
 def blocks_of(buffers, unit):
     return [
         buffer.at[chunk, first : first + unit]
@@ -134,48 +130,62 @@
     return gate_pre / (1.0 + jnp.exp(-gate_pre)) * up_pre
 
 
-def hidden_kernel(distances, plan, size, *refs, accs=()):
+def stream_hidden(rows, lanes, size, accs, ready, hidden):
+    def finish(place, dots):
+        gate_pre, up_pre = dots
+        hidden[place] = gate_pre / (1.0 + jnp.exp(-gate_pre)) * up_pre
+
+    stream_dots(rows, lanes, size, accs, ready, finish)
+
+
+def first_hidden_kernel(distances, plan, size, *refs, accs=()):
     count = len(distances)
     pieces, refs = refs[:count], refs[count:]
-    gate, up_near, up_far, down_far, hidden, mine, down_near, rows, up_late, sems, mine_sem = refs
-    loads = start_loads(plan, [up_far, down_far], [up_late, down_near], sems)
-    late = up_late.shape[0]
+    gate, up, gate_far, up_far, hidden, mine, gate_last, up_last, rows, gate_mid, up_mid, sems, mine_sem = refs
+    loads = start_loads(
+        plan, [gate_far, up_far, gate_far, up_far], [gate_mid, up_mid, gate_last, up_last], sems
+    )
     place_rows(pieces, distances, rows)
     width = mine.shape[1]
     start = pl.multiple_of(lax.axis_index("dp") * width, width)
     own = pltpu.make_async_copy(rows.at[:, pl.ds(start, width)], mine, mine_sem)
     own.start()
-    places, unit = hidden.shape[:2]
-    lanes = [blocks_of([gate], unit), blocks_of([up_near, up_late], unit)]
-    per_chunk = places // gate.shape[0]
+    unit = hidden.shape[1]
+    lanes = [blocks_of([gate, gate_mid], unit), blocks_of([up, up_mid], unit)]
+    there = gate.shape[0] * gate.shape[1] // unit
     waited = [0]
 
     def ready(group):
-        needed = -(-(group + 1) * size // per_chunk) - up_near.shape[0]
-        while waited[0] < min(needed, late):
-            loads[waited[0]].wait()
-            waited[0] += 1
-
-    def finish(place, dots):
-        gate_pre, up_pre = dots
-        hidden[place] = gate_pre / (1.0 + jnp.exp(-gate_pre)) * up_pre
-
-    stream_dots(rows, lanes, size, accs, ready, finish)
+        if (group + 1) * size > there and waited[0] == 0:
+            waited[0] = gate_mid.shape[0] + up_mid.shape[0]
+            for copy in loads[: waited[0]]:
+                copy.wait()
+
+    stream_hidden(rows, lanes, size, accs, ready, hidden)
     own.wait()
-    for copy in loads[late:]:
+    for copy in loads[waited[0] :]:
         copy.wait()
 
 
-def score_kernel(distances, plan, top, *refs, accs=()):
+def second_hidden_kernel(distances, size, *refs, accs=()):
+    count = len(distances)
+    pieces, (gate, up, after, hidden, rows) = refs[:count], refs[count:]
+    place_rows(pieces, distances, rows)
+    unit = hidden.shape[1]
+    lanes = [blocks_of([gate], unit), blocks_of([up], unit)]
+    stream_hidden(rows, lanes, size, accs, lambda group: None, hidden)
+
+
+def score_kernel(distances, top, *refs, accs=()):
     count = len(distances)
     pieces, refs = refs[:count], refs[count:]
-    hidden, down_near, down_mid, down_far, partial, probs, chosen, rows, down_late, sems = refs
-    loads = start_loads(plan, [down_far], [down_late], sems)
-    model_width = down_far.shape[2]
+    hidden_0, hidden_1, down, partial, probs, chosen, rows = refs
+    model_width = down.shape[2]
     experts_all = probs.shape[0]
     place_rows(pieces, distances, rows)
     local_experts = partial.shape[1]
-    blocks = blocks_of([down_near, down_mid, down_late], hidden.shape[1])
+    blocks = blocks_of([down], hidden_0.shape[1])
+    hidden = [held.at[place] for held in (hidden_0, hidden_1) for place in range(held.shape[0])]
     per_expert = len(blocks) // local_experts
     size = len(blocks) // 4
     order = [
@@ -195,22 +205,17 @@
             named = named + (packed[slot : slot + 1] == number).astype(jnp.float32)
         chosen[...] = named
 
-    def ready(group):
-        if group == 1:
-            for copy in loads:
-                copy.wait()
-
     def finish(place, dots):
         if place == 0:
             routing()
         for lane, paired in zip(order, dots):
             block = lane[place]
-            product = hidden[block] * paired
+            product = hidden[block][...] * paired
             expert = block // per_expert
             sums[expert] = product if sums[expert] is None else sums[expert] + product
 
     lanes = [[blocks[block] for block in lane] for lane in order]
-    stream_dots(rows.at[:, :model_width], lanes, size, accs, ready, finish)
+    stream_dots(rows.at[:, :model_width], lanes, size, accs, lambda group: None, finish)
     lines = [jnp.sum(term, axis=0, keepdims=True) for term in sums]
     partial[...] = jnp.broadcast_to(jnp.concatenate(lines, axis=0)[None], partial.shape)
 
@@ -258,8 +263,7 @@
     extra = -(-(3 * experts_all + top) // 128) * 128
     chips = data_count // CORES
     distances = [chip * CORES + core for chip in range(chips) for core in range(CORES)]
-    up_cut = chunks // 3
-    down_cut = 2 * chunks // 3
+    first = 2 * chunks // 3
 
     vmem = pl.BlockSpec(memory_space=pltpu.VMEM)
     hbm = pl.BlockSpec(memory_space=pltpu.HBM)
@@ -288,11 +292,12 @@
         return [pltpu.ACC(number)((unit, edge), jnp.float32) for number in range(2) for _ in range(2 * count)]
 
     cut = (chunks, chunk_rows, model_width)
-    gate, up, down = (keep_far(weight.reshape(cut)) for weight in (gate_weight, up_weight, down_weight))
+    gate, up = (keep_far(weight.reshape(cut)) for weight in (gate_weight, up_weight))
+    down = pltpu.with_memory_space_constraint(down_weight.reshape(cut), pltpu.VMEM)
 
     tokens_beside = swap(tokens, "dp", 1)
     tokens_far = [swap(tokens, "dp", chip * CORES) for chip in range(1, chips)]
-    plan = [(0, chunks), (0, up_cut)]
+    plan = [(0, first), (0, first)]
     packed, gate_near, up_near = pl.pallas_call(
         functools.partial(load_pack_kernel, plan),
         out_shape=(
@@ -307,10 +312,10 @@
             pltpu.VMEM((top, tok_dev), jnp.int32),
             pltpu.VMEM((tok_dev, extra), jnp.float32),
             pltpu.SemaphoreType.DMA((3,)),
-            pltpu.SemaphoreType.DMA((chunks + up_cut,)),
+            pltpu.SemaphoreType.DMA((2 * first,)),
         ],
         compiler_params=scoped(0),
-        cost_estimate=cost(chunks + up_cut, 0),
+        cost_estimate=cost(2 * first, 0),
         name="load_pack",
     )(keep_far(logits), keep_far(routes.T), keep_far(cotangent), gate, up)
     packed_far = [swap(packed, "dp", chip * CORES) for chip in range(1, chips)]
@@ -319,64 +324,64 @@
     token_pieces = [tokens, tokens_beside]
     for far in tokens_far:
         token_pieces += [far, swap(far, "dp", 1)]
-    plan = [(up_cut, chunks), (0, down_cut)]
-    loads = chunks - up_cut + down_cut
-    hidden, mine, down_near = pl.pallas_call(
-        with_accs(functools.partial(hidden_kernel, distances, plan, size), accs(size)),
+    plan = [(first, chunks - 1), (first, chunks - 1), (chunks - 1, chunks), (chunks - 1, chunks)]
+    loads = 2 * (chunks - first)
+    places = units // chunks
+    rows_scratch = pltpu.VMEM((total_tokens, model_width), jnp.bfloat16)
+    hidden_0, mine, gate_last, up_last = pl.pallas_call(
+        with_accs(functools.partial(first_hidden_kernel, distances, plan, size), accs(size)),
         out_shape=(
-            jax.ShapeDtypeStruct((units, unit, total_tokens), jnp.float32),
+            jax.ShapeDtypeStruct((units - places, unit, total_tokens), jnp.float32),
             jax.ShapeDtypeStruct((total_tokens, model_width // data_count), jnp.bfloat16),
-            near(*plan[1]),
+            near(*plan[2]),
+            near(*plan[3]),
         ),
         in_specs=[vmem] * (data_count + 2) + [hbm] * 2,
-        out_specs=(vmem,) * 3,
+        out_specs=(vmem,) * 4,
         scratch_shapes=[
-            pltpu.VMEM((total_tokens, model_width), jnp.bfloat16),
+            rows_scratch,
             near(*plan[0]),
+            near(*plan[1]),
             pltpu.SemaphoreType.DMA((loads,)),
             pltpu.SemaphoreType.DMA,
         ],
-        compiler_params=scoped((chunks - up_cut) * cut[1] * cut[2] * 2 + (1 if accs(size) else 3) * row_bytes),
+        compiler_params=scoped(loads * cut[1] * cut[2] * 2 + (1 if accs(size) else 3) * row_bytes),
         cost_estimate=cost(loads, 2 * chunks),
-        name="hidden",
-    )(*token_pieces, gate_near, up_near, up, down)
-
-    packed_far, hidden = lax.optimization_barrier((packed_far, hidden))
+        name="hidden_first",
+    )(*token_pieces, gate_near, up_near, gate, up)
+
+    packed_far, hidden_0 = lax.optimization_barrier((packed_far, hidden_0))
+    hidden_1 = pl.pallas_call(
+        with_accs(functools.partial(second_hidden_kernel, distances, size), accs(size)),
+        out_shape=jax.ShapeDtypeStruct((places, unit, total_tokens), jnp.float32),
+        in_specs=[vmem] * (data_count + 2) + [anywhere],
+        out_specs=vmem,
+        scratch_shapes=[rows_scratch],
+        compiler_params=scoped((1 if accs(size) else 3) * row_bytes),
+        cost_estimate=cost(1, 2),
+        name="hidden_second",
+    )(*token_pieces, gate_last, up_last, packed_far[0])
+
     packed_pieces = [packed, packed_beside]
     for far in packed_far:
         packed_pieces += [far, swap(far, "dp", 1)]
-    plan = [(down_cut, down_cut + 1)]
-    down_mid = pl.pallas_call(
-        functools.partial(load_kernel, plan),
-        out_shape=near(*plan[0]),
-        in_specs=[hbm, anywhere],
-        out_specs=vmem,
-        scratch_shapes=[pltpu.SemaphoreType.DMA((1,))],
-        compiler_params=scoped(0),
-        cost_estimate=cost(1, 0),
-        name="load_down",
-    )(down, packed_far[0])
-
-    plan = [(down_cut + 1, chunks)]
     table = jax.ShapeDtypeStruct((experts_all, total_tokens), jnp.float32)
     partial, probs, chosen = pl.pallas_call(
-        with_accs(functools.partial(score_kernel, distances, plan, top), accs(units // 4)),
+        with_accs(functools.partial(score_kernel, distances, top), accs(units // 4)),
         out_shape=(
             jax.ShapeDtypeStruct((data_count * expert_count, local_experts, total_tokens), jnp.float32),
             table,
             table,
         ),
-        in_specs=[vmem] * (data_count + 3) + [hbm],
+        in_specs=[vmem] * (data_count + 3),
         out_specs=(vmem, vmem, vmem),
         scratch_shapes=[
             pltpu.VMEM((total_tokens, model_width + extra), jnp.bfloat16),
-            near(*plan[0]),
-            pltpu.SemaphoreType.DMA((chunks - down_cut - 1,)),
         ],
-        compiler_params=scoped((chunks - down_cut - 1) * cut[1] * cut[2] * 2 + 3 * row_bytes),
-        cost_estimate=cost(chunks - down_cut, chunks),
+        compiler_params=scoped(3 * row_bytes),
+        cost_estimate=cost(1, 1),
         name="scores",
-    )(*packed_pieces, hidden, down_near, down_mid, down)
+    )(*packed_pieces, hidden_0, hidden_1, down)
 
     score_blocks = lax.all_to_all(partial, ("dp", "expert"), split_axis=0, concat_axis=0, tiled=True)
 

time: 38.5 us -> 37.3 us (0.969)
  Pallas kernels: 19 us -> 17.7 us
    pallas_call x3, Pallas kernels: 12.1 us -> 10.8 us  [the longest x1 5.81 us: per_device(): pl.pallas_call(with_accs(functools.partial(first_hidden_kernel, distances...]
  transfers between devices with their start and end apart: 6 -> 6, of which waited for: 3 -> 4; matrix products, arithmetic and copies ran while one was open for 0% -> 0% of each run, Pallas kernels for 38% -> 36%
where the time goes in v9:
time: 37.3 us; the launch traced here: 37.2 us
  Pallas kernels  17.7 us (47%)
  blocking collectives  13.3 us (36%)
  starting transfers between devices  3.87 us (10%)
  waiting for transfers between devices  1.51 us (4%)
  between operations  0.72 us (2%)
    all_to_all x1, blocking collectives, per_device(): lax.all_to_all(partial, ('dp', 'expert'), split_axis=0, concat_axis=0, ti...  13.3 us
    pallas_call x1, Pallas kernels, per_device(): pl.pallas_call(functools.partial(load_pack_kernel, plan), out_shape=(jax....  6.08 us
    pallas_call x1, Pallas kernels, per_device(): pl.pallas_call(with_accs(functools.partial(first_hidden_kernel, distances...  5.81 us
    ppermute x6, starting transfers between devices, swap(): lax.ppermute(value, axis, [(index, index ^ distance) for index in range(l...  3.87 us
    pallas_call x1, Pallas kernels, per_device(): pl.pallas_call(with_accs(functools.partial(score_kernel, distances, top),...  3.55 us
    ppermute x6, waiting for transfers between devices, swap(): lax.ppermute(value, axis, [(index, index ^ distance) for index in range(l...  1.51 us
    pallas_call x1, Pallas kernels, per_device(): pl.pallas_call(with_accs(functools.partial(second_hidden_kernel, distance...  1.41 us
    pallas_call x1, Pallas kernels, per_device(): pl.pallas_call(functools.partial(gradient_kernel, data_count), out_shape=...  0.85 us
  transfers between devices with their start and end apart: 6, of which 4 were waited for; matrix products, arithmetic and copies ran while one was open for 0% of the time, Pallas kernels for 36%

profile of v9, /device:TPU:0, one launch (start us, length us, event | category | flops | bytes accessed | tf_op | source)
XLA Modules:
  0.0 37.2 jit_solution(13738578672469770122)
XLA Ops:
  0.6 3.0 %collective-permute-start.3 = (bf16[32,4096]{1,0:T(8,128)(2,1)}, bf16[32,4096]{1,0:T(8,128)(2,1)S(1)}, u32[]{:S(2)}, u32[]{:S(2)}) collective-permute-start(bf16[32,4096]{1,0:T(8,128)(2,1)} %refs_0_.3), channel_id=1, source_target_pairs={{0,16},{8,24},{16,0},{24,8},{1,17},{9,25},{17,1},{25,9},{2,18},{10... | collective-permute-start | bytes 786440 | tf_op jit(solution)/shard_map/ppermute | solution.py:248
  3.7 0.0 copy-start
  3.7 6.1 %load_pack.1 = (bf16[32,4224]{1,0:T(8,128)(2,1)S(1)}, bf16[4,256,4096]{2,1,0:T(8,128)(2,1)S(1)}, bf16[4,256,4096]{2,1,0:T(8,128)(2,1)S(1)}) custom-call(f32[32,32]{1,0:T(8,128)} %logits.1, s32[8,32]{1,0:T(8,128)} %bitcast.12, bf16[32,4096]{1,0:T(8,128)(2,1)} %cotangent.1, bf16[6,256,4096]{2,1,0:T(8,128)(2,1)} %bitcast.8, bf16[6,256,4096]{2,1,0:T(8,128)(2,1)} %bitcast.10), custom_call_target="tpu_custom_call" | custom-call | bytes 8 | tf_op jit(solution)/shard_map/load_pack/pallas_call | solution.py:301
  9.8 0.1 collective-permute-start.1
  9.8 0.0 copy-done
  9.8 0.1 collective-permute-start.2
  9.9 0.3 collective-permute-done.3.refs_2_
  10.2 0.0 slice-start
  10.2 0.3 collective-permute-start.4
  10.5 0.2 collective-permute-start
  10.7 0.7 %collective-permute-done.2.refs_1_ = bf16[32,4096]{1,0:T(8,128)(2,1)S(1)} collective-permute-done((bf16[32,4096]{1,0:T(8,128)(2,1)S(1)}, bf16[32,4096]{1,0:T(8,128)(2,1)S(1)}, u32[]{:S(2)}, u32[]{:S(2)}) %collective-permute-start.2) | collective-permute-done | bytes 262176 | tf_op jit(solution)/shard_map/ppermute | solution.py:248
  11.4 0.4 %collective-permute-done.4.refs_3_ = bf16[32,4096]{1,0:T(8,128)(2,1)S(1)} collective-permute-done((bf16[32,4096]{1,0:T(8,128)(2,1)S(1)}, bf16[32,4096]{1,0:T(8,128)(2,1)S(1)}, u32[]{:S(2)}, u32[]{:S(2)}) %collective-permute-start.4) | collective-permute-done | bytes 262176 | tf_op jit(solution)/shard_map/ppermute | solution.py:248
  11.8 5.8 %hidden_first.1 = (f32[10,128,128]{2,1,0:T(8,128)S(1)}, bf16[128,1024]{1,0:T(8,128)(2,1)S(1)}, bf16[1,256,4096]{2,1,0:T(8,128)(2,1)S(1)}, bf16[1,256,4096]{2,1,0:T(8,128)(2,1)S(1)}) custom-call(bf16[32,4096]{1,0:T(8,128)(2,1)S(1)} %copy-done, bf16[32,4096]{1,0:T(8,128)(2,1)S(1)} %collective-permute-done.2.refs_1_, ...), custom_call_target="tpu_custom_call" | custom-call | flops 12 | bytes 4 | tf_op jit(solution)/shard_map/hidden_first/pallas_call | solution.py:331
  17.6 0.1 collective-permute-done.1.refs_6_.refs_2_
  17.8 0.2 collective-permute-start.5
  17.9 1.4 %hidden_second.1.refs_5_ = f32[2,128,128]{2,1,0:T(8,128)S(1)} custom-call(bf16[32,4096]{1,0:T(8,128)(2,1)S(1)} %copy-done, bf16[32,4096]{1,0:T(8,128)(2,1)S(1)} %collective-permute-done.2.refs_1_, bf16[32,4096]{1,0:T(8,128)(2,1)S(1)} %collective-permute-done.3.refs_2_, bf16[32,4096]{1,0:T(8,128)(2,1)S(1)} %collective-permute-done.4.refs_3_, ...), custom_call_target="tpu_custom_call" | custom-call | flops 2 | bytes 1 | tf_op jit(solution)/shard_map/hidden_second/pallas_call | solution.py:354
  19.3 0.0 collective-permute-done.refs_1_
  19.4 0.0 collective-permute-done.5.refs_3_
  19.4 0.0 slice-done
  19.4 0.0 slice-done.1
  19.4 0.0 slice-done.2
  19.4 3.5 %scores.1 = (f32[32,4,128]{2,1,0:T(4,128)S(1)}, f32[32,128]{1,0:T(8,128)S(1)}, f32[32,128]{1,0:T(8,128)S(1)}) custom-call(bf16[32,4224]{1,0:T(8,128)(2,1)S(1)} %get-tuple-element.19.refs_0_, bf16[32,4224]{1,0:T(8,128)(2,1)S(1)} %collective-permute-done.refs_1_, bf16[32,4224]{1,0:T(8,128)(2,1)S(1)} %collective-permute-done.1.refs_6_.refs_2_, ...), custom_call_target="tpu_custom_call" | custom-call | flops 1 | bytes 1 | tf_op jit(solution)/shard_map/scores/pallas_call | solution.py:369
  23.0 13.3 %all_to_all.5.blocks = f32[32,4,128]{2,1,0:T(4,128)S(1)} all-to-all(f32[32,4,128]{2,1,0:T(4,128)S(1)} %get-tuple-element.30), channel_id=1, replica_groups=mesh['dp'=4,'expert'=8] {'dp','expert'}, dimensions={0} | all-to-all | bytes 131072 | tf_op jit(solution)/shard_map/all_to_all | solution.py:386
  36.3 0.9 %gradient.1 = (f32[32,32]{1,0:T(8,128)}, f32[32,1024]{1,0:T(8,128)}) custom-call(f32[32,4,128]{2,1,0:T(4,128)S(1)} %all_to_all.5.blocks, f32[32,128]{1,0:T(8,128)S(1)} %get-tuple-element.31.probs_ref, f32[32,128]{1,0:T(8,128)S(1)} %get-tuple-element.32.chosen_ref, bf16[128,1024]{1,0:T(8,128)(2,1)S(1)} %get-tuple-element.33.mine), custom_call_target="tpu_custom_call" | custom-call | tf_op jit(solution)/shard_map/gradient/pallas_call | solution.py:388
  (3 shorter events, 0.0 us)
Async XLA Ops:
  0.6 9.5 %collective-permute-start.3 = (bf16[32,4096]{1,0:T(8,128)(2,1)}, bf16[32,4096]{1,0:T(8,128)(2,1)S(1)}, u32[]{:S(2)}, u32[]{:S(2)}) collective-permute-start(bf16[32,4096]{1,0:T(8,128)(2,1)} %refs_0_.3), channel_id=1, source_target_pairs={{0,16},{8,24},{16,0},{24,8},{1,17},{9,25},{17,1},{25,9},{2,18},{10... | collective-permute-start | bytes 786440 | tf_op jit(solution)/shard_map/ppermute | solution.py:248
  3.7 6.2 %copy-start = (bf16[32,4096]{1,0:T(8,128)(2,1)S(1)}, bf16[32,4096]{1,0:T(8,128)(2,1)}, u32[]{:S(2)}) copy-start(bf16[32,4096]{1,0:T(8,128)(2,1)} %refs_0_.3) | copy-start | bytes 786436
  9.8 8.0 %collective-permute-start.1 = (bf16[32,4224]{1,0:T(8,128)(2,1)S(1)}, bf16[32,4224]{1,0:T(8,128)(2,1)S(1)}, u32[]{:S(2)}, u32[]{:S(2)}) collective-permute-start(bf16[32,4224]{1,0:T(8,128)(2,1)S(1)} %get-tuple-element.19.refs_0_), channel_id=1, source_target_pairs={{0,16},{8,24},{16,0},{24,8},{1,17},{9,25},{17,1},{25,9},{2,18},{10... | collective-permute-start | bytes 811016 | tf_op jit(solution)/shard_map/ppermute | solution.py:248
  9.8 1.6 %collective-permute-start.2 = (bf16[32,4096]{1,0:T(8,128)(2,1)S(1)}, bf16[32,4096]{1,0:T(8,128)(2,1)S(1)}, u32[]{:S(2)}, u32[]{:S(2)}) collective-permute-start(bf16[32,4096]{1,0:T(8,128)(2,1)S(1)} %copy-done), channel_id=1, source_target_pairs={{0,8},{8,0},{16,24},{24,16},{1,9},{9,1},{17,25},{25,17},{2,10},{10... | collective-permute-start | bytes 786440 | tf_op jit(solution)/shard_map/ppermute | solution.py:248
  10.2 9.2 %slice-start = ((s8[12582912]{0:T(1024)(128)(4,1)}), s8[4194304]{0:T(1024)(128)(4,1)S(1)}, s32[]{:S(2)}) async-start(s8[12582912]{0:T(1024)(128)(4,1)} %bitcast.5), calls=%async_computation.1 | async-start | bytes 8388608
  10.2 9.2 %slice-start.1 = ((s8[12582912]{0:T(1024)(128)(4,1)}), s8[4194304]{0:T(1024)(128)(4,1)S(1)}, s32[]{:S(2)}) async-start(s8[12582912]{0:T(1024)(128)(4,1)} %bitcast.5), calls=%async_computation.2 | async-start | bytes 8388608
  10.2 9.2 %slice-start.2 = ((s8[12582912]{0:T(1024)(128)(4,1)}), s8[4194304]{0:T(1024)(128)(4,1)S(1)}, s32[]{:S(2)}) async-start(s8[12582912]{0:T(1024)(128)(4,1)} %bitcast.5), calls=%async_computation.3 | async-start | bytes 8388608
  10.2 1.6 %collective-permute-start.4 = (bf16[32,4096]{1,0:T(8,128)(2,1)S(1)}, bf16[32,4096]{1,0:T(8,128)(2,1)S(1)}, u32[]{:S(2)}, u32[]{:S(2)}) collective-permute-start(bf16[32,4096]{1,0:T(8,128)(2,1)S(1)} %collective-permute-done.3.refs_2_), channel_id=1, source_target_pairs={{0,8},{8,0},{16,24},{24,16},{1,9},{9,1},{17,25},{25,17},{2,10},{10... | collective-permute-start | bytes 786440 | tf_op jit(solution)/shard_map/ppermute | solution.py:248
  10.5 8.9 %collective-permute-start = (bf16[32,4224]{1,0:T(8,128)(2,1)S(1)}, bf16[32,4224]{1,0:T(8,128)(2,1)S(1)}, u32[]{:S(2)}, u32[]{:S(2)}) collective-permute-start(bf16[32,4224]{1,0:T(8,128)(2,1)S(1)} %get-tuple-element.19.refs_0_), channel_id=1, source_target_pairs={{0,8},{8,0},{16,24},{24,16},{1,9},{9,1},{17,25},{25,17},{2,10},{10... | collective-permute-start | bytes 811016 | tf_op jit(solution)/shard_map/ppermute | solution.py:248
  17.8 1.6 %collective-permute-start.5 = (bf16[32,4224]{1,0:T(8,128)(2,1)S(1)}, bf16[32,4224]{1,0:T(8,128)(2,1)S(1)}, u32[]{:S(2)}, u32[]{:S(2)}) collective-permute-start(bf16[32,4224]{1,0:T(8,128)(2,1)S(1)} %collective-permute-done.1.refs_6_.refs_2_), channel_id=1, source_target_pairs={{0,8},{8,0},{16,24},{24,16},{1,9},{9,1},{17,25},{25,17},{2,10},{10... | collective-permute-start | bytes 811016 | tf_op jit(solution)/shard_map/ppermute | solution.py:248

commit v10 on v9

--- a/solution.py
+++ b/solution.py
@@ -222,7 +222,11 @@
 
 def gradient_kernel(data_count, blocks, probs_ref, chosen_ref, mine, logit_grad, router_grad, grads, held, sems):
     experts_all, total_tokens = probs_ref.shape
-    scores = jnp.sum(blocks[...].reshape((data_count, experts_all, total_tokens)), axis=0)
+    rows_of = [
+        sum(blocks[first + part] for part in range(1, data_count)) + blocks[first]
+        for first in range(0, blocks.shape[0], data_count)
+    ]
+    scores = jnp.concatenate(rows_of, axis=0)
     probs, chosen = probs_ref[...], chosen_ref[...]
     mass = jnp.sum(probs * chosen, axis=0, keepdims=True)
     weighted = jnp.sum(probs * chosen * scores, axis=0, keepdims=True)
@@ -383,7 +387,7 @@
         name="scores",
     )(*packed_pieces, hidden_0, hidden_1, down)
 
-    score_blocks = lax.all_to_all(partial, ("dp", "expert"), split_axis=0, concat_axis=0, tiled=True)
+    score_blocks = lax.all_to_all(partial, ("expert", "dp"), split_axis=0, concat_axis=0, tiled=True)
 
     logit_grad, router_grad = pl.pallas_call(
         functools.partial(gradient_kernel, data_count),

time: 37.3 us -> 37.5 us (level)
  no operation moved by 1% of the time
where the time goes in v10:
time: 37.5 us; the launch traced here: 37.3 us
  Pallas kernels  17.7 us (47%)
  blocking collectives  13.5 us (36%)
  starting transfers between devices  3.87 us (10%)
  waiting for transfers between devices  1.51 us (4%)
  between operations  0.72 us (2%)
    all_to_all x1, blocking collectives, per_device(): lax.all_to_all(partial, ('expert', 'dp'), split_axis=0, concat_axis=0, ti...  13.5 us
    pallas_call x1, Pallas kernels, per_device(): pl.pallas_call(functools.partial(load_pack_kernel, plan), out_shape=(jax....  6.08 us
    pallas_call x1, Pallas kernels, per_device(): pl.pallas_call(with_accs(functools.partial(first_hidden_kernel, distances...  5.81 us
    ppermute x6, starting transfers between devices, swap(): lax.ppermute(value, axis, [(index, index ^ distance) for index in range(l...  3.87 us
    pallas_call x1, Pallas kernels, per_device(): pl.pallas_call(with_accs(functools.partial(score_kernel, distances, top),...  3.55 us
    ppermute x6, waiting for transfers between devices, swap(): lax.ppermute(value, axis, [(index, index ^ distance) for index in range(l...  1.51 us
    pallas_call x1, Pallas kernels, per_device(): pl.pallas_call(with_accs(functools.partial(second_hidden_kernel, distance...  1.41 us
    pallas_call x1, Pallas kernels, per_device(): pl.pallas_call(functools.partial(gradient_kernel, data_count), out_shape=...  0.86 us
  transfers between devices with their start and end apart: 6, of which 4 were waited for; matrix products, arithmetic and copies ran while one was open for 0% of the time, Pallas kernels for 36%

profile of v10, /device:TPU:0, one launch (start us, length us, event | category | flops | bytes accessed | tf_op | source)
XLA Modules:
  0.0 37.3 jit_solution(17655558472074764088)
XLA Ops:
  0.6 3.0 %collective-permute-start.3 = (bf16[32,4096]{1,0:T(8,128)(2,1)}, bf16[32,4096]{1,0:T(8,128)(2,1)S(1)}, u32[]{:S(2)}, u32[]{:S(2)}) collective-permute-start(bf16[32,4096]{1,0:T(8,128)(2,1)} %refs_0_.3), channel_id=1, source_target_pairs={{0,16},{8,24},{16,0},{24,8},{1,17},{9,25},{17,1},{25,9},{2,18},{10... | collective-permute-start | bytes 786440 | tf_op jit(solution)/shard_map/ppermute | solution.py:252
  3.7 0.0 copy-start
  3.7 6.1 %load_pack.1 = (bf16[32,4224]{1,0:T(8,128)(2,1)S(1)}, bf16[4,256,4096]{2,1,0:T(8,128)(2,1)S(1)}, bf16[4,256,4096]{2,1,0:T(8,128)(2,1)S(1)}) custom-call(f32[32,32]{1,0:T(8,128)} %logits.1, s32[8,32]{1,0:T(8,128)} %bitcast.12, bf16[32,4096]{1,0:T(8,128)(2,1)} %cotangent.1, bf16[6,256,4096]{2,1,0:T(8,128)(2,1)} %bitcast.8, bf16[6,256,4096]{2,1,0:T(8,128)(2,1)} %bitcast.10), custom_call_target="tpu_custom_call" | custom-call | bytes 8 | tf_op jit(solution)/shard_map/load_pack/pallas_call | solution.py:305
  9.8 0.1 collective-permute-start.1
  9.8 0.0 copy-done
  9.8 0.1 collective-permute-start.2
  9.9 0.3 collective-permute-done.3.refs_2_
  10.2 0.0 slice-start
  10.2 0.3 collective-permute-start.4
  10.5 0.2 collective-permute-start
  10.7 0.7 %collective-permute-done.2.refs_1_ = bf16[32,4096]{1,0:T(8,128)(2,1)S(1)} collective-permute-done((bf16[32,4096]{1,0:T(8,128)(2,1)S(1)}, bf16[32,4096]{1,0:T(8,128)(2,1)S(1)}, u32[]{:S(2)}, u32[]{:S(2)}) %collective-permute-start.2) | collective-permute-done | bytes 262176 | tf_op jit(solution)/shard_map/ppermute | solution.py:252
  11.4 0.4 %collective-permute-done.4.refs_3_ = bf16[32,4096]{1,0:T(8,128)(2,1)S(1)} collective-permute-done((bf16[32,4096]{1,0:T(8,128)(2,1)S(1)}, bf16[32,4096]{1,0:T(8,128)(2,1)S(1)}, u32[]{:S(2)}, u32[]{:S(2)}) %collective-permute-start.4) | collective-permute-done | bytes 262176 | tf_op jit(solution)/shard_map/ppermute | solution.py:252
  11.8 5.8 %hidden_first.1 = (f32[10,128,128]{2,1,0:T(8,128)S(1)}, bf16[128,1024]{1,0:T(8,128)(2,1)S(1)}, bf16[1,256,4096]{2,1,0:T(8,128)(2,1)S(1)}, bf16[1,256,4096]{2,1,0:T(8,128)(2,1)S(1)}) custom-call(bf16[32,4096]{1,0:T(8,128)(2,1)S(1)} %copy-done, bf16[32,4096]{1,0:T(8,128)(2,1)S(1)} %collective-permute-done.2.refs_1_, ...), custom_call_target="tpu_custom_call" | custom-call | flops 12 | bytes 4 | tf_op jit(solution)/shard_map/hidden_first/pallas_call | solution.py:335
  17.6 0.1 collective-permute-done.1.refs_6_.refs_2_
  17.8 0.2 collective-permute-start.5
  17.9 1.4 %hidden_second.1.refs_5_ = f32[2,128,128]{2,1,0:T(8,128)S(1)} custom-call(bf16[32,4096]{1,0:T(8,128)(2,1)S(1)} %copy-done, bf16[32,4096]{1,0:T(8,128)(2,1)S(1)} %collective-permute-done.2.refs_1_, bf16[32,4096]{1,0:T(8,128)(2,1)S(1)} %collective-permute-done.3.refs_2_, bf16[32,4096]{1,0:T(8,128)(2,1)S(1)} %collective-permute-done.4.refs_3_, ...), custom_call_target="tpu_custom_call" | custom-call | flops 2 | bytes 1 | tf_op jit(solution)/shard_map/hidden_second/pallas_call | solution.py:358
  19.3 0.0 collective-permute-done.refs_1_
  19.4 0.0 collective-permute-done.5.refs_3_
  19.4 0.0 slice-done
  19.4 0.0 slice-done.1
  19.4 0.0 slice-done.2
  19.4 3.5 %scores.1 = (f32[32,4,128]{2,1,0:T(4,128)S(1)}, f32[32,128]{1,0:T(8,128)S(1)}, f32[32,128]{1,0:T(8,128)S(1)}) custom-call(bf16[32,4224]{1,0:T(8,128)(2,1)S(1)} %get-tuple-element.19.refs_0_, bf16[32,4224]{1,0:T(8,128)(2,1)S(1)} %collective-permute-done.refs_1_, bf16[32,4224]{1,0:T(8,128)(2,1)S(1)} %collective-permute-done.1.refs_6_.refs_2_, ...), custom_call_target="tpu_custom_call" | custom-call | flops 1 | bytes 1 | tf_op jit(solution)/shard_map/scores/pallas_call | solution.py:373
  23.0 13.5 %all_to_all.5.blocks = f32[32,4,128]{2,1,0:T(4,128)S(1)} all-to-all(f32[32,4,128]{2,1,0:T(4,128)S(1)} %get-tuple-element.30), channel_id=1, replica_groups=mesh['dp'=4,'expert'=8] {'expert','dp'}, dimensions={0} | all-to-all | bytes 131072 | tf_op jit(solution)/shard_map/all_to_all | solution.py:390
  36.4 0.9 %gradient.1 = (f32[32,32]{1,0:T(8,128)}, f32[32,1024]{1,0:T(8,128)}) custom-call(f32[32,4,128]{2,1,0:T(4,128)S(1)} %all_to_all.5.blocks, f32[32,128]{1,0:T(8,128)S(1)} %get-tuple-element.31.probs_ref, f32[32,128]{1,0:T(8,128)S(1)} %get-tuple-element.32.chosen_ref, bf16[128,1024]{1,0:T(8,128)(2,1)S(1)} %get-tuple-element.33.mine), custom_call_target="tpu_custom_call" | custom-call | tf_op jit(solution)/shard_map/gradient/pallas_call | solution.py:392
  (3 shorter events, 0.0 us)
Async XLA Ops:
  0.6 9.5 %collective-permute-start.3 = (bf16[32,4096]{1,0:T(8,128)(2,1)}, bf16[32,4096]{1,0:T(8,128)(2,1)S(1)}, u32[]{:S(2)}, u32[]{:S(2)}) collective-permute-start(bf16[32,4096]{1,0:T(8,128)(2,1)} %refs_0_.3), channel_id=1, source_target_pairs={{0,16},{8,24},{16,0},{24,8},{1,17},{9,25},{17,1},{25,9},{2,18},{10... | collective-permute-start | bytes 786440 | tf_op jit(solution)/shard_map/ppermute | solution.py:252
  3.7 6.2 %copy-start = (bf16[32,4096]{1,0:T(8,128)(2,1)S(1)}, bf16[32,4096]{1,0:T(8,128)(2,1)}, u32[]{:S(2)}) copy-start(bf16[32,4096]{1,0:T(8,128)(2,1)} %refs_0_.3) | copy-start | bytes 786436
  9.8 8.0 %collective-permute-start.1 = (bf16[32,4224]{1,0:T(8,128)(2,1)S(1)}, bf16[32,4224]{1,0:T(8,128)(2,1)S(1)}, u32[]{:S(2)}, u32[]{:S(2)}) collective-permute-start(bf16[32,4224]{1,0:T(8,128)(2,1)S(1)} %get-tuple-element.19.refs_0_), channel_id=1, source_target_pairs={{0,16},{8,24},{16,0},{24,8},{1,17},{9,25},{17,1},{25,9},{2,18},{10... | collective-permute-start | bytes 811016 | tf_op jit(solution)/shard_map/ppermute | solution.py:252
  9.8 1.6 %collective-permute-start.2 = (bf16[32,4096]{1,0:T(8,128)(2,1)S(1)}, bf16[32,4096]{1,0:T(8,128)(2,1)S(1)}, u32[]{:S(2)}, u32[]{:S(2)}) collective-permute-start(bf16[32,4096]{1,0:T(8,128)(2,1)S(1)} %copy-done), channel_id=1, source_target_pairs={{0,8},{8,0},{16,24},{24,16},{1,9},{9,1},{17,25},{25,17},{2,10},{10... | collective-permute-start | bytes 786440 | tf_op jit(solution)/shard_map/ppermute | solution.py:252
  10.2 9.2 %slice-start = ((s8[12582912]{0:T(1024)(128)(4,1)}), s8[4194304]{0:T(1024)(128)(4,1)S(1)}, s32[]{:S(2)}) async-start(s8[12582912]{0:T(1024)(128)(4,1)} %bitcast.5), calls=%async_computation.1 | async-start | bytes 8388608
  10.2 9.2 %slice-start.1 = ((s8[12582912]{0:T(1024)(128)(4,1)}), s8[4194304]{0:T(1024)(128)(4,1)S(1)}, s32[]{:S(2)}) async-start(s8[12582912]{0:T(1024)(128)(4,1)} %bitcast.5), calls=%async_computation.2 | async-start | bytes 8388608
  10.2 9.2 %slice-start.2 = ((s8[12582912]{0:T(1024)(128)(4,1)}), s8[4194304]{0:T(1024)(128)(4,1)S(1)}, s32[]{:S(2)}) async-start(s8[12582912]{0:T(1024)(128)(4,1)} %bitcast.5), calls=%async_computation.3 | async-start | bytes 8388608
  10.2 1.6 %collective-permute-start.4 = (bf16[32,4096]{1,0:T(8,128)(2,1)S(1)}, bf16[32,4096]{1,0:T(8,128)(2,1)S(1)}, u32[]{:S(2)}, u32[]{:S(2)}) collective-permute-start(bf16[32,4096]{1,0:T(8,128)(2,1)S(1)} %collective-permute-done.3.refs_2_), channel_id=1, source_target_pairs={{0,8},{8,0},{16,24},{24,16},{1,9},{9,1},{17,25},{25,17},{2,10},{10... | collective-permute-start | bytes 786440 | tf_op jit(solution)/shard_map/ppermute | solution.py:252
  10.5 8.9 %collective-permute-start = (bf16[32,4224]{1,0:T(8,128)(2,1)S(1)}, bf16[32,4224]{1,0:T(8,128)(2,1)S(1)}, u32[]{:S(2)}, u32[]{:S(2)}) collective-permute-start(bf16[32,4224]{1,0:T(8,128)(2,1)S(1)} %get-tuple-element.19.refs_0_), channel_id=1, source_target_pairs={{0,8},{8,0},{16,24},{24,16},{1,9},{9,1},{17,25},{25,17},{2,10},{10... | collective-permute-start | bytes 811016 | tf_op jit(solution)/shard_map/ppermute | solution.py:252
  17.8 1.6 %collective-permute-start.5 = (bf16[32,4224]{1,0:T(8,128)(2,1)S(1)}, bf16[32,4224]{1,0:T(8,128)(2,1)S(1)}, u32[]{:S(2)}, u32[]{:S(2)}) collective-permute-start(bf16[32,4224]{1,0:T(8,128)(2,1)S(1)} %collective-permute-done.1.refs_6_.refs_2_), channel_id=1, source_target_pairs={{0,8},{8,0},{16,24},{24,16},{1,9},{9,1},{17,25},{25,17},{2,10},{10... | collective-permute-start | bytes 811016 | tf_op jit(solution)/shard_map/ppermute | solution.py:252

commit v11 on v9

--- a/solution.py
+++ b/solution.py
@@ -14,7 +14,7 @@
     return lax.dot_general(a, b, (((1,), (1,)), ((), ())), preferred_element_type=jnp.float32)
 
 
-def stream_dots(rows, lanes, size, accs, ready, finish):
+def stream_dots(pieces, rows, lanes, size, accs, ready, finish):
     count = len(lanes[0])
     groups = [range(first, min(first + size, count)) for first in range(0, count, size)]
 
@@ -29,6 +29,9 @@
             finish(place, dots_of(number, place))
 
     if not accs:
+        held = pieces[0].shape[0]
+        for number, piece in enumerate(pieces):
+            rows[number * held : (number + 1) * held, :] = piece[...]
         for number in range(len(groups)):
             ready(number)
             read(number)
@@ -38,7 +41,8 @@
 
     def push(turn):
         first = turn % steps * edge
-        both = jnp.concatenate([rows[:, first : first + edge]] * (edge // rows.shape[0]), axis=0)
+        parts = [piece[:, first : first + edge] for piece in pieces]
+        both = jnp.concatenate(parts * (edge // rows.shape[0]), axis=0)
         for unit in range(len(lanes)):
             pltpu.matmul_push_rhs(both, turn % 2, unit, transpose=True)
 
@@ -130,26 +134,29 @@
     return gate_pre / (1.0 + jnp.exp(-gate_pre)) * up_pre
 
 
-def stream_hidden(rows, lanes, size, accs, ready, hidden):
+def stream_hidden(pieces, rows, lanes, size, accs, ready, hidden):
     def finish(place, dots):
         gate_pre, up_pre = dots
         hidden[place] = gate_pre / (1.0 + jnp.exp(-gate_pre)) * up_pre
 
-    stream_dots(rows, lanes, size, accs, ready, finish)
+    stream_dots(pieces, rows, lanes, size, accs, ready, finish)
 
 
 def first_hidden_kernel(distances, plan, size, *refs, accs=()):
     count = len(distances)
     pieces, refs = refs[:count], refs[count:]
-    gate, up, gate_far, up_far, hidden, mine, gate_last, up_last, rows, gate_mid, up_mid, sems, mine_sem = refs
+    gate, up, gate_far, up_far, hidden, mine, gate_last, up_last, rows, gate_mid, up_mid, sems, mine_sems = refs
     loads = start_loads(
         plan, [gate_far, up_far, gate_far, up_far], [gate_mid, up_mid, gate_last, up_last], sems
     )
-    place_rows(pieces, distances, rows)
-    width = mine.shape[1]
-    start = pl.multiple_of(lax.axis_index("dp") * width, width)
-    own = pltpu.make_async_copy(rows.at[:, pl.ds(start, width)], mine, mine_sem)
-    own.start()
+    me = lax.axis_index("dp")
+    width, held = mine.shape[1], pieces[0].shape[0]
+    columns = pl.ds(pl.multiple_of(me * width, width), width)
+    own = []
+    for number, piece in enumerate(pieces):
+        start = pl.multiple_of(jnp.bitwise_xor(me, distances[number]) * held, held)
+        own.append(pltpu.make_async_copy(piece.at[:, columns], mine.at[pl.ds(start, held)], mine_sems.at[number]))
+        own[number].start()
     unit = hidden.shape[1]
     lanes = [blocks_of([gate, gate_mid], unit), blocks_of([up, up_mid], unit)]
     there = gate.shape[0] * gate.shape[1] // unit
@@ -161,28 +168,39 @@
             for copy in loads[: waited[0]]:
                 copy.wait()
 
-    stream_hidden(rows, lanes, size, accs, ready, hidden)
-    own.wait()
-    for copy in loads[waited[0] :]:
+    stream_hidden(pieces, rows, lanes, size, accs, ready, hidden)
+    for copy in own + loads[waited[0] :]:
         copy.wait()
 
 
-def second_hidden_kernel(distances, size, *refs, accs=()):
-    count = len(distances)
+def second_hidden_kernel(count, size, *refs, accs=()):
     pieces, (gate, up, after, hidden, rows) = refs[:count], refs[count:]
-    place_rows(pieces, distances, rows)
     unit = hidden.shape[1]
     lanes = [blocks_of([gate], unit), blocks_of([up], unit)]
-    stream_hidden(rows, lanes, size, accs, lambda group: None, hidden)
+    stream_hidden(pieces, rows, lanes, size, accs, lambda group: None, hidden)
+
+
+def token_order(lines, count):
+    me = lax.axis_index("dp")
+    tokens = lines.shape[1]
+    lane = lax.broadcasted_iota(jnp.int32, lines.shape, 1)
+    distance = 1
+    while distance < count:
+        step = distance * (tokens // count)
+        above, below = pltpu.roll(lines, tokens - step, 1), pltpu.roll(lines, step, 1)
+        swapped = jnp.where(jnp.bitwise_and(lane, step) == 0, above, below)
+        lines = jnp.where(jnp.bitwise_and(me, distance) != 0, swapped, lines)
+        distance *= 2
+    return lines
 
 
 def score_kernel(distances, top, *refs, accs=()):
     count = len(distances)
     pieces, refs = refs[:count], refs[count:]
-    hidden_0, hidden_1, down, partial, probs, chosen, rows = refs
+    hidden_0, hidden_1, down, partial, probs, chosen, rows, routing_rows = refs
     model_width = down.shape[2]
     experts_all = probs.shape[0]
-    place_rows(pieces, distances, rows)
+    place_rows([piece.at[:, model_width:] for piece in pieces], distances, routing_rows)
     local_experts = partial.shape[1]
     blocks = blocks_of([down], hidden_0.shape[1])
     hidden = [held.at[place] for held in (hidden_0, hidden_1) for place in range(held.shape[0])]
@@ -194,7 +212,7 @@
     sums = [None] * local_experts
 
     def routing():
-        packed = rows[:, model_width:].astype(jnp.float32).T
+        packed = routing_rows[...].astype(jnp.float32).T
         terms = [packed[term * experts_all : (term + 1) * experts_all] for term in range(3)]
         logits = terms[0] + terms[1] + terms[2]
         raised = jnp.exp(logits - jnp.max(logits, axis=0, keepdims=True))
@@ -215,9 +233,10 @@
             sums[expert] = product if sums[expert] is None else sums[expert] + product
 
     lanes = [[blocks[block] for block in lane] for lane in order]
-    stream_dots(rows.at[:, :model_width], lanes, size, accs, lambda group: None, finish)
+    stream_dots([piece.at[:, :model_width] for piece in pieces], rows, lanes, size, accs, lambda group: None, finish)
     lines = [jnp.sum(term, axis=0, keepdims=True) for term in sums]
-    partial[...] = jnp.broadcast_to(jnp.concatenate(lines, axis=0)[None], partial.shape)
+    scores = token_order(jnp.concatenate(lines, axis=0), count)
+    partial[...] = jnp.broadcast_to(scores[None], partial.shape)
 
 
 def gradient_kernel(data_count, blocks, probs_ref, chosen_ref, mine, logit_grad, router_grad, grads, held, sems):
@@ -343,7 +362,7 @@
             near(*plan[0]),
             near(*plan[1]),
             pltpu.SemaphoreType.DMA((loads,)),
-            pltpu.SemaphoreType.DMA,
+            pltpu.SemaphoreType.DMA((data_count,)),
         ],
         compiler_params=scoped(loads * cut[1] * cut[2] * 2 + (1 if accs(size) else 3) * row_bytes),
         cost_estimate=cost(loads, 2 * chunks),
@@ -352,7 +371,7 @@
 
     packed_far, hidden_0 = lax.optimization_barrier((packed_far, hidden_0))
     hidden_1 = pl.pallas_call(
-        with_accs(functools.partial(second_hidden_kernel, distances, size), accs(size)),
+        with_accs(functools.partial(second_hidden_kernel, data_count, size), accs(size)),
         out_shape=jax.ShapeDtypeStruct((places, unit, total_tokens), jnp.float32),
         in_specs=[vmem] * (data_count + 2) + [anywhere],
         out_specs=vmem,
@@ -376,7 +395,8 @@
         in_specs=[vmem] * (data_count + 3),
         out_specs=(vmem, vmem, vmem),
         scratch_shapes=[
-            pltpu.VMEM((total_tokens, model_width + extra), jnp.bfloat16),
+            rows_scratch,
+            pltpu.VMEM((total_tokens, extra), jnp.bfloat16),
         ],
         compiler_params=scoped(3 * row_bytes),
         cost_estimate=cost(1, 1),

time: 37.3 us -> 37.3 us (level)
  no operation moved by 1% of the time
where the time goes in v11:
time: 37.3 us; the launch traced here: 37.2 us
  Pallas kernels  17.7 us (47%)
  blocking collectives  13.4 us (36%)
  starting transfers between devices  3.9 us (10%)
  waiting for transfers between devices  1.47 us (4%)
  between operations  0.72 us (2%)
    all_to_all x1, blocking collectives, per_device(): lax.all_to_all(partial, ('dp', 'expert'), split_axis=0, concat_axis=0, ti...  13.4 us
    pallas_call x1, Pallas kernels, per_device(): pl.pallas_call(functools.partial(load_pack_kernel, plan), out_shape=(jax....  6.08 us
    pallas_call x1, Pallas kernels, per_device(): pl.pallas_call(with_accs(functools.partial(first_hidden_kernel, distances...  5.85 us
    ppermute x6, starting transfers between devices, swap(): lax.ppermute(value, axis, [(index, index ^ distance) for index in range(l...  3.9 us
    pallas_call x1, Pallas kernels, per_device(): pl.pallas_call(with_accs(functools.partial(score_kernel, distances, top),...  3.58 us
    ppermute x6, waiting for transfers between devices, swap(): lax.ppermute(value, axis, [(index, index ^ distance) for index in range(l...  1.47 us
    pallas_call x1, Pallas kernels, per_device(): pl.pallas_call(with_accs(functools.partial(second_hidden_kernel, data_cou...  1.33 us
    pallas_call x1, Pallas kernels, per_device(): pl.pallas_call(functools.partial(gradient_kernel, data_count), out_shape=...  0.86 us
  transfers between devices with their start and end apart: 6, of which 4 were waited for; matrix products, arithmetic and copies ran while one was open for 0% of the time, Pallas kernels for 36%

profile of v11, /device:TPU:0, one launch (start us, length us, event | category | flops | bytes accessed | tf_op | source)
XLA Modules:
  0.0 37.2 jit_solution(8433376057002549118)
XLA Ops:
  0.6 3.0 %collective-permute-start.3 = (bf16[32,4096]{1,0:T(8,128)(2,1)}, bf16[32,4096]{1,0:T(8,128)(2,1)S(1)}, u32[]{:S(2)}, u32[]{:S(2)}) collective-permute-start(bf16[32,4096]{1,0:T(8,128)(2,1)} %refs_0_.3), channel_id=1, source_target_pairs={{0,16},{8,24},{16,0},{24,8},{1,17},{9,25},{17,1},{25,9},{2,18},{10... | collective-permute-start | bytes 786440 | tf_op jit(solution)/shard_map/ppermute | solution.py:267
  3.7 0.0 copy-start
  3.7 6.1 %load_pack.1 = (bf16[32,4224]{1,0:T(8,128)(2,1)S(1)}, bf16[4,256,4096]{2,1,0:T(8,128)(2,1)S(1)}, bf16[4,256,4096]{2,1,0:T(8,128)(2,1)S(1)}) custom-call(f32[32,32]{1,0:T(8,128)} %logits.1, s32[8,32]{1,0:T(8,128)} %bitcast.12, bf16[32,4096]{1,0:T(8,128)(2,1)} %cotangent.1, bf16[6,256,4096]{2,1,0:T(8,128)(2,1)} %bitcast.8, bf16[6,256,4096]{2,1,0:T(8,128)(2,1)} %bitcast.10), custom_call_target="tpu_custom_call" | custom-call | bytes 8 | tf_op jit(solution)/shard_map/load_pack/pallas_call | solution.py:320
  9.8 0.1 collective-permute-start.1
  9.8 0.0 copy-done
  9.8 0.1 collective-permute-start.2
  9.9 0.3 collective-permute-done.3.refs_2_
  10.2 0.0 slice-start
  10.2 0.3 collective-permute-start.4
  10.5 0.2 collective-permute-start
  10.7 0.7 %collective-permute-done.2.refs_1_ = bf16[32,4096]{1,0:T(8,128)(2,1)S(1)} collective-permute-done((bf16[32,4096]{1,0:T(8,128)(2,1)S(1)}, bf16[32,4096]{1,0:T(8,128)(2,1)S(1)}, u32[]{:S(2)}, u32[]{:S(2)}) %collective-permute-start.2) | collective-permute-done | bytes 262176 | tf_op jit(solution)/shard_map/ppermute | solution.py:267
  11.4 0.4 %collective-permute-done.4.refs_3_ = bf16[32,4096]{1,0:T(8,128)(2,1)S(1)} collective-permute-done((bf16[32,4096]{1,0:T(8,128)(2,1)S(1)}, bf16[32,4096]{1,0:T(8,128)(2,1)S(1)}, u32[]{:S(2)}, u32[]{:S(2)}) %collective-permute-start.4) | collective-permute-done | bytes 262176 | tf_op jit(solution)/shard_map/ppermute | solution.py:267
  11.8 5.8 %hidden_first.1 = (f32[10,128,128]{2,1,0:T(8,128)S(1)}, bf16[128,1024]{1,0:T(8,128)(2,1)S(1)}, bf16[1,256,4096]{2,1,0:T(8,128)(2,1)S(1)}, bf16[1,256,4096]{2,1,0:T(8,128)(2,1)S(1)}) custom-call(bf16[32,4096]{1,0:T(8,128)(2,1)S(1)} %copy-done, bf16[32,4096]{1,0:T(8,128)(2,1)S(1)} %collective-permute-done.2.refs_1_, ...), custom_call_target="tpu_custom_call" | custom-call | flops 12 | bytes 4 | tf_op jit(solution)/shard_map/hidden_first/pallas_call | solution.py:350
  17.7 0.1 collective-permute-done.1.refs_6_.refs_2_
  17.8 0.2 collective-permute-start.5
  18.0 1.3 %hidden_second.1.refs_5_ = f32[2,128,128]{2,1,0:T(8,128)S(1)} custom-call(bf16[32,4096]{1,0:T(8,128)(2,1)S(1)} %copy-done, bf16[32,4096]{1,0:T(8,128)(2,1)S(1)} %collective-permute-done.2.refs_1_, bf16[32,4096]{1,0:T(8,128)(2,1)S(1)} %collective-permute-done.3.refs_2_, bf16[32,4096]{1,0:T(8,128)(2,1)S(1)} %collective-permute-done.4.refs_3_, ...), custom_call_target="tpu_custom_call" | custom-call | flops 2 | bytes 1 | tf_op jit(solution)/shard_map/hidden_second/pallas_call | solution.py:373
  19.3 0.0 collective-permute-done.refs_1_
  19.3 0.0 collective-permute-done.5.refs_3_
  19.3 0.0 slice-done
  19.3 0.0 slice-done.1
  19.3 0.0 slice-done.2
  19.4 3.6 %scores.1 = (f32[32,4,128]{2,1,0:T(4,128)S(1)}, f32[32,128]{1,0:T(8,128)S(1)}, f32[32,128]{1,0:T(8,128)S(1)}) custom-call(bf16[32,4224]{1,0:T(8,128)(2,1)S(1)} %get-tuple-element.19.refs_0_, bf16[32,4224]{1,0:T(8,128)(2,1)S(1)} %collective-permute-done.refs_1_, bf16[32,4224]{1,0:T(8,128)(2,1)S(1)} %collective-permute-done.1.refs_6_.refs_2_, ...), custom_call_target="tpu_custom_call" | custom-call | flops 1 | bytes 1 | tf_op jit(solution)/shard_map/scores/pallas_call | solution.py:388
  22.9 13.4 %all_to_all.5.blocks = f32[32,4,128]{2,1,0:T(4,128)S(1)} all-to-all(f32[32,4,128]{2,1,0:T(4,128)S(1)} %get-tuple-element.30), channel_id=1, replica_groups=mesh['dp'=4,'expert'=8] {'dp','expert'}, dimensions={0} | all-to-all | bytes 131072 | tf_op jit(solution)/shard_map/all_to_all | solution.py:406
  36.3 0.9 %gradient.1 = (f32[32,32]{1,0:T(8,128)}, f32[32,1024]{1,0:T(8,128)}) custom-call(f32[32,4,128]{2,1,0:T(4,128)S(1)} %all_to_all.5.blocks, f32[32,128]{1,0:T(8,128)S(1)} %get-tuple-element.31.probs_ref, f32[32,128]{1,0:T(8,128)S(1)} %get-tuple-element.32.chosen_ref, bf16[128,1024]{1,0:T(8,128)(2,1)S(1)} %get-tuple-element.33.mine), custom_call_target="tpu_custom_call" | custom-call | tf_op jit(solution)/shard_map/gradient/pallas_call | solution.py:408
  (3 shorter events, 0.0 us)
Async XLA Ops:
  0.6 9.5 %collective-permute-start.3 = (bf16[32,4096]{1,0:T(8,128)(2,1)}, bf16[32,4096]{1,0:T(8,128)(2,1)S(1)}, u32[]{:S(2)}, u32[]{:S(2)}) collective-permute-start(bf16[32,4096]{1,0:T(8,128)(2,1)} %refs_0_.3), channel_id=1, source_target_pairs={{0,16},{8,24},{16,0},{24,8},{1,17},{9,25},{17,1},{25,9},{2,18},{10... | collective-permute-start | bytes 786440 | tf_op jit(solution)/shard_map/ppermute | solution.py:267
  3.7 6.2 %copy-start = (bf16[32,4096]{1,0:T(8,128)(2,1)S(1)}, bf16[32,4096]{1,0:T(8,128)(2,1)}, u32[]{:S(2)}) copy-start(bf16[32,4096]{1,0:T(8,128)(2,1)} %refs_0_.3) | copy-start | bytes 786436
  9.8 8.0 %collective-permute-start.1 = (bf16[32,4224]{1,0:T(8,128)(2,1)S(1)}, bf16[32,4224]{1,0:T(8,128)(2,1)S(1)}, u32[]{:S(2)}, u32[]{:S(2)}) collective-permute-start(bf16[32,4224]{1,0:T(8,128)(2,1)S(1)} %get-tuple-element.19.refs_0_), channel_id=1, source_target_pairs={{0,16},{8,24},{16,0},{24,8},{1,17},{9,25},{17,1},{25,9},{2,18},{10... | collective-permute-start | bytes 811016 | tf_op jit(solution)/shard_map/ppermute | solution.py:267
  9.8 1.6 %collective-permute-start.2 = (bf16[32,4096]{1,0:T(8,128)(2,1)S(1)}, bf16[32,4096]{1,0:T(8,128)(2,1)S(1)}, u32[]{:S(2)}, u32[]{:S(2)}) collective-permute-start(bf16[32,4096]{1,0:T(8,128)(2,1)S(1)} %copy-done), channel_id=1, source_target_pairs={{0,8},{8,0},{16,24},{24,16},{1,9},{9,1},{17,25},{25,17},{2,10},{10... | collective-permute-start | bytes 786440 | tf_op jit(solution)/shard_map/ppermute | solution.py:267
  10.2 9.1 %slice-start = ((s8[12582912]{0:T(1024)(128)(4,1)}), s8[4194304]{0:T(1024)(128)(4,1)S(1)}, s32[]{:S(2)}) async-start(s8[12582912]{0:T(1024)(128)(4,1)} %bitcast.5), calls=%async_computation.1 | async-start | bytes 8388608
  10.2 9.1 %slice-start.1 = ((s8[12582912]{0:T(1024)(128)(4,1)}), s8[4194304]{0:T(1024)(128)(4,1)S(1)}, s32[]{:S(2)}) async-start(s8[12582912]{0:T(1024)(128)(4,1)} %bitcast.5), calls=%async_computation.2 | async-start | bytes 8388608
  10.2 9.2 %slice-start.2 = ((s8[12582912]{0:T(1024)(128)(4,1)}), s8[4194304]{0:T(1024)(128)(4,1)S(1)}, s32[]{:S(2)}) async-start(s8[12582912]{0:T(1024)(128)(4,1)} %bitcast.5), calls=%async_computation.3 | async-start | bytes 8388608
  10.2 1.6 %collective-permute-start.4 = (bf16[32,4096]{1,0:T(8,128)(2,1)S(1)}, bf16[32,4096]{1,0:T(8,128)(2,1)S(1)}, u32[]{:S(2)}, u32[]{:S(2)}) collective-permute-start(bf16[32,4096]{1,0:T(8,128)(2,1)S(1)} %collective-permute-done.3.refs_2_), channel_id=1, source_target_pairs={{0,8},{8,0},{16,24},{24,16},{1,9},{9,1},{17,25},{25,17},{2,10},{10... | collective-permute-start | bytes 786440 | tf_op jit(solution)/shard_map/ppermute | solution.py:267
  10.5 8.8 %collective-permute-start = (bf16[32,4224]{1,0:T(8,128)(2,1)S(1)}, bf16[32,4224]{1,0:T(8,128)(2,1)S(1)}, u32[]{:S(2)}, u32[]{:S(2)}) collective-permute-start(bf16[32,4224]{1,0:T(8,128)(2,1)S(1)} %get-tuple-element.19.refs_0_), channel_id=1, source_target_pairs={{0,8},{8,0},{16,24},{24,16},{1,9},{9,1},{17,25},{25,17},{2,10},{10... | collective-permute-start | bytes 811016 | tf_op jit(solution)/shard_map/ppermute | solution.py:267
  17.8 1.6 %collective-permute-start.5 = (bf16[32,4224]{1,0:T(8,128)(2,1)S(1)}, bf16[32,4224]{1,0:T(8,128)(2,1)S(1)}, u32[]{:S(2)}, u32[]{:S(2)}) collective-permute-start(bf16[32,4224]{1,0:T(8,128)(2,1)S(1)} %collective-permute-done.1.refs_6_.refs_2_), channel_id=1, source_target_pairs={{0,8},{8,0},{16,24},{24,16},{1,9},{9,1},{17,25},{25,17},{2,10},{10... | collective-permute-start | bytes 811016 | tf_op jit(solution)/shard_map/ppermute | solution.py:267

commit v12 on v11

--- a/solution.py
+++ b/solution.py
@@ -14,7 +14,7 @@
     return lax.dot_general(a, b, (((1,), (1,)), ((), ())), preferred_element_type=jnp.float32)
 
 
-def stream_dots(pieces, rows, lanes, size, accs, ready, finish):
+def stream_dots(pieces, rows, lanes, size, accs, ready, finish, meanwhile=lambda: None):
     count = len(lanes[0])
     groups = [range(first, min(first + size, count)) for first in range(0, count, size)]
 
@@ -29,6 +29,7 @@
             finish(place, dots_of(number, place))
 
     if not accs:
+        meanwhile()
         held = pieces[0].shape[0]
         for number, piece in enumerate(pieces):
             rows[number * held : (number + 1) * held, :] = piece[...]
@@ -60,6 +61,8 @@
                 push(turn + 1)
         if step == 0 and number > 0:
             read(number - 1)
+        if turn == 1:
+            meanwhile()
     read(len(groups) - 1)
 
 
@@ -224,8 +227,6 @@
         chosen[...] = named
 
     def finish(place, dots):
-        if place == 0:
-            routing()
         for lane, paired in zip(order, dots):
             block = lane[place]
             product = hidden[block][...] * paired
@@ -233,7 +234,7 @@
             sums[expert] = product if sums[expert] is None else sums[expert] + product
 
     lanes = [[blocks[block] for block in lane] for lane in order]
-    stream_dots([piece.at[:, :model_width] for piece in pieces], rows, lanes, size, accs, lambda group: None, finish)
+    stream_dots([piece.at[:, :model_width] for piece in pieces], rows, lanes, 2 * size, accs, lambda group: None, finish, routing)
     lines = [jnp.sum(term, axis=0, keepdims=True) for term in sums]
     scores = token_order(jnp.concatenate(lines, axis=0), count)
     partial[...] = jnp.broadcast_to(scores[None], partial.shape)
@@ -245,8 +246,9 @@
     probs, chosen = probs_ref[...], chosen_ref[...]
     mass = jnp.sum(probs * chosen, axis=0, keepdims=True)
     weighted = jnp.sum(probs * chosen * scores, axis=0, keepdims=True)
+    total = jnp.sum(probs * scores, axis=0, keepdims=True) / mass - mass * weighted / (mass * mass)
     prob_grad = scores / mass - chosen * weighted / (mass * mass)
-    grad = probs * (prob_grad - jnp.sum(probs * prob_grad, axis=0, keepdims=True))
+    grad = probs * (prob_grad - total)
     half = mine.shape[1] // 2
     copies = []
     for number in range(2):

time: 37.3 us -> 37.3 us (level)
  no operation moved by 1% of the time
where the time goes in v12:
time: 37.3 us; the launch traced here: 37.1 us
  Pallas kernels  17.7 us (47%)
  blocking collectives  13.4 us (36%)
  starting transfers between devices  3.9 us (10%)
  waiting for transfers between devices  1.47 us (4%)
  between operations  0.72 us (2%)
    all_to_all x1, blocking collectives, per_device(): lax.all_to_all(partial, ('dp', 'expert'), split_axis=0, concat_axis=0, ti...  13.4 us
    pallas_call x1, Pallas kernels, per_device(): pl.pallas_call(functools.partial(load_pack_kernel, plan), out_shape=(jax....  6.08 us
    pallas_call x1, Pallas kernels, per_device(): pl.pallas_call(with_accs(functools.partial(first_hidden_kernel, distances...  5.85 us
    ppermute x6, starting transfers between devices, swap(): lax.ppermute(value, axis, [(index, index ^ distance) for index in range(l...  3.9 us
    pallas_call x1, Pallas kernels, per_device(): pl.pallas_call(with_accs(functools.partial(score_kernel, distances, top),...  3.58 us
    ppermute x6, waiting for transfers between devices, swap(): lax.ppermute(value, axis, [(index, index ^ distance) for index in range(l...  1.47 us
    pallas_call x1, Pallas kernels, per_device(): pl.pallas_call(with_accs(functools.partial(second_hidden_kernel, data_cou...  1.33 us
    pallas_call x1, Pallas kernels, per_device(): pl.pallas_call(functools.partial(gradient_kernel, data_count), out_shape=...  0.84 us
  transfers between devices with their start and end apart: 6, of which 4 were waited for; matrix products, arithmetic and copies ran while one was open for 0% of the time, Pallas kernels for 36%

profile of v12, /device:TPU:0, one launch (start us, length us, event | category | flops | bytes accessed | tf_op | source)
XLA Modules:
  0.0 37.1 jit_solution(9537809360664026593)
XLA Ops:
  0.6 3.0 %collective-permute-start.3 = (bf16[32,4096]{1,0:T(8,128)(2,1)}, bf16[32,4096]{1,0:T(8,128)(2,1)S(1)}, u32[]{:S(2)}, u32[]{:S(2)}) collective-permute-start(bf16[32,4096]{1,0:T(8,128)(2,1)} %refs_0_.3), channel_id=1, source_target_pairs={{0,16},{8,24},{16,0},{24,8},{1,17},{9,25},{17,1},{25,9},{2,18},{10... | collective-permute-start | bytes 786440 | tf_op jit(solution)/shard_map/ppermute | solution.py:269
  3.7 0.0 copy-start
  3.7 6.1 %load_pack.1 = (bf16[32,4224]{1,0:T(8,128)(2,1)S(1)}, bf16[4,256,4096]{2,1,0:T(8,128)(2,1)S(1)}, bf16[4,256,4096]{2,1,0:T(8,128)(2,1)S(1)}) custom-call(f32[32,32]{1,0:T(8,128)} %logits.1, s32[8,32]{1,0:T(8,128)} %bitcast.12, bf16[32,4096]{1,0:T(8,128)(2,1)} %cotangent.1, bf16[6,256,4096]{2,1,0:T(8,128)(2,1)} %bitcast.8, bf16[6,256,4096]{2,1,0:T(8,128)(2,1)} %bitcast.10), custom_call_target="tpu_custom_call" | custom-call | bytes 8 | tf_op jit(solution)/shard_map/load_pack/pallas_call | solution.py:322
  9.8 0.1 collective-permute-start.1
  9.8 0.0 copy-done
  9.8 0.1 collective-permute-start.2
  9.9 0.3 collective-permute-done.3.refs_2_
  10.2 0.0 slice-start
  10.2 0.3 collective-permute-start.4
  10.5 0.2 collective-permute-start
  10.7 0.7 %collective-permute-done.2.refs_1_ = bf16[32,4096]{1,0:T(8,128)(2,1)S(1)} collective-permute-done((bf16[32,4096]{1,0:T(8,128)(2,1)S(1)}, bf16[32,4096]{1,0:T(8,128)(2,1)S(1)}, u32[]{:S(2)}, u32[]{:S(2)}) %collective-permute-start.2) | collective-permute-done | bytes 262176 | tf_op jit(solution)/shard_map/ppermute | solution.py:269
  11.4 0.4 %collective-permute-done.4.refs_3_ = bf16[32,4096]{1,0:T(8,128)(2,1)S(1)} collective-permute-done((bf16[32,4096]{1,0:T(8,128)(2,1)S(1)}, bf16[32,4096]{1,0:T(8,128)(2,1)S(1)}, u32[]{:S(2)}, u32[]{:S(2)}) %collective-permute-start.4) | collective-permute-done | bytes 262176 | tf_op jit(solution)/shard_map/ppermute | solution.py:269
  11.8 5.8 %hidden_first.1 = (f32[10,128,128]{2,1,0:T(8,128)S(1)}, bf16[128,1024]{1,0:T(8,128)(2,1)S(1)}, bf16[1,256,4096]{2,1,0:T(8,128)(2,1)S(1)}, bf16[1,256,4096]{2,1,0:T(8,128)(2,1)S(1)}) custom-call(bf16[32,4096]{1,0:T(8,128)(2,1)S(1)} %copy-done, bf16[32,4096]{1,0:T(8,128)(2,1)S(1)} %collective-permute-done.2.refs_1_, ...), custom_call_target="tpu_custom_call" | custom-call | flops 12 | bytes 4 | tf_op jit(solution)/shard_map/hidden_first/pallas_call | solution.py:352
  17.7 0.1 collective-permute-done.1.refs_6_.refs_2_
  17.8 0.2 collective-permute-start.5
  18.0 1.3 %hidden_second.1.refs_5_ = f32[2,128,128]{2,1,0:T(8,128)S(1)} custom-call(bf16[32,4096]{1,0:T(8,128)(2,1)S(1)} %copy-done, bf16[32,4096]{1,0:T(8,128)(2,1)S(1)} %collective-permute-done.2.refs_1_, bf16[32,4096]{1,0:T(8,128)(2,1)S(1)} %collective-permute-done.3.refs_2_, bf16[32,4096]{1,0:T(8,128)(2,1)S(1)} %collective-permute-done.4.refs_3_, ...), custom_call_target="tpu_custom_call" | custom-call | flops 2 | bytes 1 | tf_op jit(solution)/shard_map/hidden_second/pallas_call | solution.py:375
  19.3 0.0 collective-permute-done.refs_1_
  19.3 0.0 collective-permute-done.5.refs_3_
  19.3 0.0 slice-done
  19.3 0.0 slice-done.1
  19.3 0.0 slice-done.2
  19.4 3.6 %scores.1 = (f32[32,4,128]{2,1,0:T(4,128)S(1)}, f32[32,128]{1,0:T(8,128)S(1)}, f32[32,128]{1,0:T(8,128)S(1)}) custom-call(bf16[32,4224]{1,0:T(8,128)(2,1)S(1)} %get-tuple-element.19.refs_0_, bf16[32,4224]{1,0:T(8,128)(2,1)S(1)} %collective-permute-done.refs_1_, bf16[32,4224]{1,0:T(8,128)(2,1)S(1)} %collective-permute-done.1.refs_6_.refs_2_, ...), custom_call_target="tpu_custom_call" | custom-call | flops 1 | bytes 1 | tf_op jit(solution)/shard_map/scores/pallas_call | solution.py:390
  22.9 13.4 %all_to_all.5.blocks = f32[32,4,128]{2,1,0:T(4,128)S(1)} all-to-all(f32[32,4,128]{2,1,0:T(4,128)S(1)} %get-tuple-element.30), channel_id=1, replica_groups=mesh['dp'=4,'expert'=8] {'dp','expert'}, dimensions={0} | all-to-all | bytes 131072 | tf_op jit(solution)/shard_map/all_to_all | solution.py:408
  36.3 0.8 %gradient.1 = (f32[32,32]{1,0:T(8,128)}, f32[32,1024]{1,0:T(8,128)}) custom-call(f32[32,4,128]{2,1,0:T(4,128)S(1)} %all_to_all.5.blocks, f32[32,128]{1,0:T(8,128)S(1)} %get-tuple-element.31.probs_ref, f32[32,128]{1,0:T(8,128)S(1)} %get-tuple-element.32.chosen_ref, bf16[128,1024]{1,0:T(8,128)(2,1)S(1)} %get-tuple-element.33.mine), custom_call_target="tpu_custom_call" | custom-call | tf_op jit(solution)/shard_map/gradient/pallas_call | solution.py:410
  (3 shorter events, 0.0 us)
Async XLA Ops:
  0.6 9.5 %collective-permute-start.3 = (bf16[32,4096]{1,0:T(8,128)(2,1)}, bf16[32,4096]{1,0:T(8,128)(2,1)S(1)}, u32[]{:S(2)}, u32[]{:S(2)}) collective-permute-start(bf16[32,4096]{1,0:T(8,128)(2,1)} %refs_0_.3), channel_id=1, source_target_pairs={{0,16},{8,24},{16,0},{24,8},{1,17},{9,25},{17,1},{25,9},{2,18},{10... | collective-permute-start | bytes 786440 | tf_op jit(solution)/shard_map/ppermute | solution.py:269
  3.7 6.2 %copy-start = (bf16[32,4096]{1,0:T(8,128)(2,1)S(1)}, bf16[32,4096]{1,0:T(8,128)(2,1)}, u32[]{:S(2)}) copy-start(bf16[32,4096]{1,0:T(8,128)(2,1)} %refs_0_.3) | copy-start | bytes 786436
  9.8 8.0 %collective-permute-start.1 = (bf16[32,4224]{1,0:T(8,128)(2,1)S(1)}, bf16[32,4224]{1,0:T(8,128)(2,1)S(1)}, u32[]{:S(2)}, u32[]{:S(2)}) collective-permute-start(bf16[32,4224]{1,0:T(8,128)(2,1)S(1)} %get-tuple-element.19.refs_0_), channel_id=1, source_target_pairs={{0,16},{8,24},{16,0},{24,8},{1,17},{9,25},{17,1},{25,9},{2,18},{10... | collective-permute-start | bytes 811016 | tf_op jit(solution)/shard_map/ppermute | solution.py:269
  9.8 1.6 %collective-permute-start.2 = (bf16[32,4096]{1,0:T(8,128)(2,1)S(1)}, bf16[32,4096]{1,0:T(8,128)(2,1)S(1)}, u32[]{:S(2)}, u32[]{:S(2)}) collective-permute-start(bf16[32,4096]{1,0:T(8,128)(2,1)S(1)} %copy-done), channel_id=1, source_target_pairs={{0,8},{8,0},{16,24},{24,16},{1,9},{9,1},{17,25},{25,17},{2,10},{10... | collective-permute-start | bytes 786440 | tf_op jit(solution)/shard_map/ppermute | solution.py:269
  10.2 9.1 %slice-start = ((s8[12582912]{0:T(1024)(128)(4,1)}), s8[4194304]{0:T(1024)(128)(4,1)S(1)}, s32[]{:S(2)}) async-start(s8[12582912]{0:T(1024)(128)(4,1)} %bitcast.5), calls=%async_computation.1 | async-start | bytes 8388608
  10.2 9.1 %slice-start.1 = ((s8[12582912]{0:T(1024)(128)(4,1)}), s8[4194304]{0:T(1024)(128)(4,1)S(1)}, s32[]{:S(2)}) async-start(s8[12582912]{0:T(1024)(128)(4,1)} %bitcast.5), calls=%async_computation.2 | async-start | bytes 8388608
  10.2 9.2 %slice-start.2 = ((s8[12582912]{0:T(1024)(128)(4,1)}), s8[4194304]{0:T(1024)(128)(4,1)S(1)}, s32[]{:S(2)}) async-start(s8[12582912]{0:T(1024)(128)(4,1)} %bitcast.5), calls=%async_computation.3 | async-start | bytes 8388608
  10.2 1.6 %collective-permute-start.4 = (bf16[32,4096]{1,0:T(8,128)(2,1)S(1)}, bf16[32,4096]{1,0:T(8,128)(2,1)S(1)}, u32[]{:S(2)}, u32[]{:S(2)}) collective-permute-start(bf16[32,4096]{1,0:T(8,128)(2,1)S(1)} %collective-permute-done.3.refs_2_), channel_id=1, source_target_pairs={{0,8},{8,0},{16,24},{24,16},{1,9},{9,1},{17,25},{25,17},{2,10},{10... | collective-permute-start | bytes 786440 | tf_op jit(solution)/shard_map/ppermute | solution.py:269
  10.5 8.8 %collective-permute-start = (bf16[32,4224]{1,0:T(8,128)(2,1)S(1)}, bf16[32,4224]{1,0:T(8,128)(2,1)S(1)}, u32[]{:S(2)}, u32[]{:S(2)}) collective-permute-start(bf16[32,4224]{1,0:T(8,128)(2,1)S(1)} %get-tuple-element.19.refs_0_), channel_id=1, source_target_pairs={{0,8},{8,0},{16,24},{24,16},{1,9},{9,1},{17,25},{25,17},{2,10},{10... | collective-permute-start | bytes 811016 | tf_op jit(solution)/shard_map/ppermute | solution.py:269
  17.8 1.6 %collective-permute-start.5 = (bf16[32,4224]{1,0:T(8,128)(2,1)S(1)}, bf16[32,4224]{1,0:T(8,128)(2,1)S(1)}, u32[]{:S(2)}, u32[]{:S(2)}) collective-permute-start(bf16[32,4224]{1,0:T(8,128)(2,1)S(1)} %collective-permute-done.1.refs_6_.refs_2_), channel_id=1, source_target_pairs={{0,8},{8,0},{16,24},{24,16},{1,9},{9,1},{17,25},{25,17},{2,10},{10... | collective-permute-start | bytes 811016 | tf_op jit(solution)/shard_map/ppermute | solution.py:269

commit v13 on v11

--- a/solution.py
+++ b/solution.py
@@ -82,13 +82,13 @@
         rows[pl.ds(start, tok_dev), :] = piece[...]
 
 
-def start_loads(plan, sources, nears, sems):
+def start_loads(plan, sources, nears, sems, most=None):
     copies, number = [], 0
     for (first, last), source, near in zip(plan, sources, nears):
         for chunk in range(first, last):
             copies.append(pltpu.make_async_copy(source.at[chunk], near.at[chunk - first], sems.at[number]))
             number += 1
-    for copy in copies:
+    for copy in copies[:most]:
         copy.start()
     return copies
 
@@ -103,7 +103,8 @@
     ]
     for copy in copies:
         copy.start()
-    loads = start_loads(plan, [gate, up], [gate_near, up_near], load_sems)
+    most = 3
+    loads = start_loads(plan, [gate, up], [gate_near, up_near], load_sems, most)
     columns[...] = jnp.zeros(columns.shape, jnp.float32)
     copies[0].wait()
     left = logits_near[...]
@@ -116,8 +117,10 @@
     columns[:, 3 * experts_all : 3 * experts_all + routes.shape[0]] = routes_near[...].astype(jnp.float32).T
     packed[:, model_width:] = columns[...].astype(jnp.bfloat16)
     copies[2].wait()
-    for copy in loads:
+    for number, copy in enumerate(loads):
         copy.wait()
+        if number + most < len(loads):
+            loads[number + most].start()
 
 
 def blocks_of(buffers, unit):

time: 37.3 us -> 37.9 us (1.016)
  Pallas kernels: 17.7 us -> 18.2 us
    pallas_call x1, Pallas kernels: 6.08 us -> 6.61 us  [per_device(): pl.pallas_call(functools.partial(load_pack_kernel, plan), out_shape=(jax....]
  transfers between devices with their start and end apart: 6 -> 6, of which waited for: 4 -> 3; matrix products, arithmetic and copies ran while one was open for 0% -> 0% of each run, Pallas kernels for 36% -> 37%
where the time goes in v13:
time: 37.9 us; the launch traced here: 37.7 us
  Pallas kernels  18.2 us (48%)
  blocking collectives  13.4 us (35%)
  starting transfers between devices  4 us (11%)
  waiting for transfers between devices  1.34 us (4%)
  between operations  0.75 us (2%)
    all_to_all x1, blocking collectives, per_device(): lax.all_to_all(partial, ('dp', 'expert'), split_axis=0, concat_axis=0, ti...  13.4 us
    pallas_call x1, Pallas kernels, per_device(): pl.pallas_call(functools.partial(load_pack_kernel, plan), out_shape=(jax....  6.61 us
    pallas_call x1, Pallas kernels, per_device(): pl.pallas_call(with_accs(functools.partial(first_hidden_kernel, distances...  5.84 us
    ppermute x6, starting transfers between devices, swap(): lax.ppermute(value, axis, [(index, index ^ distance) for index in range(l...  4 us
    pallas_call x1, Pallas kernels, per_device(): pl.pallas_call(with_accs(functools.partial(score_kernel, distances, top),...  3.58 us
    ppermute x6, waiting for transfers between devices, swap(): lax.ppermute(value, axis, [(index, index ^ distance) for index in range(l...  1.34 us
    pallas_call x1, Pallas kernels, per_device(): pl.pallas_call(with_accs(functools.partial(second_hidden_kernel, data_cou...  1.34 us
    pallas_call x1, Pallas kernels, per_device(): pl.pallas_call(functools.partial(gradient_kernel, data_count), out_shape=...  0.86 us
  transfers between devices with their start and end apart: 6, of which 3 were waited for; matrix products, arithmetic and copies ran while one was open for 0% of the time, Pallas kernels for 37%

profile of v13, /device:TPU:0, one launch (start us, length us, event | category | flops | bytes accessed | tf_op | source)
XLA Modules:
  0.0 37.7 jit_solution(16247164520084735302)
XLA Ops:
  0.6 3.0 %collective-permute-start.3 = (bf16[32,4096]{1,0:T(8,128)(2,1)}, bf16[32,4096]{1,0:T(8,128)(2,1)S(1)}, u32[]{:S(2)}, u32[]{:S(2)}) collective-permute-start(bf16[32,4096]{1,0:T(8,128)(2,1)} %refs_0_.3), channel_id=1, source_target_pairs={{0,16},{8,24},{16,0},{24,8},{1,17},{9,25},{17,1},{25,9},{2,18},{10... | collective-permute-start | bytes 786440 | tf_op jit(solution)/shard_map/ppermute | solution.py:270
  3.7 6.6 %load_pack.1 = (bf16[32,4224]{1,0:T(8,128)(2,1)S(1)}, bf16[4,256,4096]{2,1,0:T(8,128)(2,1)S(1)}, bf16[4,256,4096]{2,1,0:T(8,128)(2,1)S(1)}) custom-call(f32[32,32]{1,0:T(8,128)} %logits.1, s32[8,32]{1,0:T(8,128)} %bitcast.12, bf16[32,4096]{1,0:T(8,128)(2,1)} %cotangent.1, bf16[6,256,4096]{2,1,0:T(8,128)(2,1)} %bitcast.8, bf16[6,256,4096]{2,1,0:T(8,128)(2,1)} %bitcast.10), custom_call_target="tpu_custom_call" | custom-call | bytes 8 | tf_op jit(solution)/shard_map/load_pack/pallas_call | solution.py:323
  10.3 0.1 collective-permute-start.1
  10.4 0.0 copy-done
  10.4 0.1 collective-permute-start.2
  10.5 0.0 collective-permute-done.3.refs_2_
  10.5 0.0 slice-start
  10.5 0.0 slice-start.1
  10.5 0.0 slice-start.2
  10.5 0.5 %collective-permute-start.4 = (bf16[32,4096]{1,0:T(8,128)(2,1)S(1)}, bf16[32,4096]{1,0:T(8,128)(2,1)S(1)}, u32[]{:S(2)}, u32[]{:S(2)}) collective-permute-start(bf16[32,4096]{1,0:T(8,128)(2,1)S(1)} %collective-permute-done.3.refs_2_), channel_id=1, source_target_pairs={{0,8},{8,0},{16,24},{24,16},{1,9},{9,1},{17,25},{25,17},{2,10},{10... | collective-permute-start | bytes 786440 | tf_op jit(solution)/shard_map/ppermute | solution.py:270
  11.0 0.1 collective-permute-start
  11.1 0.9 %collective-permute-done.2.refs_1_ = bf16[32,4096]{1,0:T(8,128)(2,1)S(1)} collective-permute-done((bf16[32,4096]{1,0:T(8,128)(2,1)S(1)}, bf16[32,4096]{1,0:T(8,128)(2,1)S(1)}, u32[]{:S(2)}, u32[]{:S(2)}) %collective-permute-start.2) | collective-permute-done | bytes 262176 | tf_op jit(solution)/shard_map/ppermute | solution.py:270
  12.0 0.4 collective-permute-done.4.refs_3_
  12.4 5.8 %hidden_first.1 = (f32[10,128,128]{2,1,0:T(8,128)S(1)}, bf16[128,1024]{1,0:T(8,128)(2,1)S(1)}, bf16[1,256,4096]{2,1,0:T(8,128)(2,1)S(1)}, bf16[1,256,4096]{2,1,0:T(8,128)(2,1)S(1)}) custom-call(bf16[32,4096]{1,0:T(8,128)(2,1)S(1)} %copy-done, bf16[32,4096]{1,0:T(8,128)(2,1)S(1)} %collective-permute-done.2.refs_1_, ...), custom_call_target="tpu_custom_call" | custom-call | flops 12 | bytes 4 | tf_op jit(solution)/shard_map/hidden_first/pallas_call | solution.py:353
  18.2 0.1 collective-permute-done.1.refs_6_.refs_2_
  18.3 0.2 collective-permute-start.5
  18.5 1.3 %hidden_second.1.refs_5_ = f32[2,128,128]{2,1,0:T(8,128)S(1)} custom-call(bf16[32,4096]{1,0:T(8,128)(2,1)S(1)} %copy-done, bf16[32,4096]{1,0:T(8,128)(2,1)S(1)} %collective-permute-done.2.refs_1_, bf16[32,4096]{1,0:T(8,128)(2,1)S(1)} %collective-permute-done.3.refs_2_, bf16[32,4096]{1,0:T(8,128)(2,1)S(1)} %collective-permute-done.4.refs_3_, ...), custom_call_target="tpu_custom_call" | custom-call | flops 2 | bytes 1 | tf_op jit(solution)/shard_map/hidden_second/pallas_call | solution.py:376
  19.8 0.0 collective-permute-done.refs_1_
  19.8 0.0 collective-permute-done.5.refs_3_
  19.9 0.0 slice-done
  19.9 0.0 slice-done.1
  19.9 3.6 %scores.1 = (f32[32,4,128]{2,1,0:T(4,128)S(1)}, f32[32,128]{1,0:T(8,128)S(1)}, f32[32,128]{1,0:T(8,128)S(1)}) custom-call(bf16[32,4224]{1,0:T(8,128)(2,1)S(1)} %get-tuple-element.19.refs_0_, bf16[32,4224]{1,0:T(8,128)(2,1)S(1)} %collective-permute-done.refs_1_, bf16[32,4224]{1,0:T(8,128)(2,1)S(1)} %collective-permute-done.1.refs_6_.refs_2_, ...), custom_call_target="tpu_custom_call" | custom-call | flops 1 | bytes 1 | tf_op jit(solution)/shard_map/scores/pallas_call | solution.py:391
  23.5 13.4 %all_to_all.5.blocks = f32[32,4,128]{2,1,0:T(4,128)S(1)} all-to-all(f32[32,4,128]{2,1,0:T(4,128)S(1)} %get-tuple-element.30), channel_id=1, replica_groups=mesh['dp'=4,'expert'=8] {'dp','expert'}, dimensions={0} | all-to-all | bytes 131072 | tf_op jit(solution)/shard_map/all_to_all | solution.py:409
  36.8 0.9 %gradient.1 = (f32[32,32]{1,0:T(8,128)}, f32[32,1024]{1,0:T(8,128)}) custom-call(f32[32,4,128]{2,1,0:T(4,128)S(1)} %all_to_all.5.blocks, f32[32,128]{1,0:T(8,128)S(1)} %get-tuple-element.31.probs_ref, f32[32,128]{1,0:T(8,128)S(1)} %get-tuple-element.32.chosen_ref, bf16[128,1024]{1,0:T(8,128)(2,1)S(1)} %get-tuple-element.33.mine), custom_call_target="tpu_custom_call" | custom-call | tf_op jit(solution)/shard_map/gradient/pallas_call | solution.py:411
  (3 shorter events, 0.0 us)
Async XLA Ops:
  0.6 9.8 %collective-permute-start.3 = (bf16[32,4096]{1,0:T(8,128)(2,1)}, bf16[32,4096]{1,0:T(8,128)(2,1)S(1)}, u32[]{:S(2)}, u32[]{:S(2)}) collective-permute-start(bf16[32,4096]{1,0:T(8,128)(2,1)} %refs_0_.3), channel_id=1, source_target_pairs={{0,16},{8,24},{16,0},{24,8},{1,17},{9,25},{17,1},{25,9},{2,18},{10... | collective-permute-start | bytes 786440 | tf_op jit(solution)/shard_map/ppermute | solution.py:270
  3.7 6.7 %copy-start = (bf16[32,4096]{1,0:T(8,128)(2,1)S(1)}, bf16[32,4096]{1,0:T(8,128)(2,1)}, u32[]{:S(2)}) copy-start(bf16[32,4096]{1,0:T(8,128)(2,1)} %refs_0_.3) | copy-start | bytes 786436
  10.3 8.0 %collective-permute-start.1 = (bf16[32,4224]{1,0:T(8,128)(2,1)S(1)}, bf16[32,4224]{1,0:T(8,128)(2,1)S(1)}, u32[]{:S(2)}, u32[]{:S(2)}) collective-permute-start(bf16[32,4224]{1,0:T(8,128)(2,1)S(1)} %get-tuple-element.19.refs_0_), channel_id=1, source_target_pairs={{0,16},{8,24},{16,0},{24,8},{1,17},{9,25},{17,1},{25,9},{2,18},{10... | collective-permute-start | bytes 811016 | tf_op jit(solution)/shard_map/ppermute | solution.py:270
  10.4 1.6 %collective-permute-start.2 = (bf16[32,4096]{1,0:T(8,128)(2,1)S(1)}, bf16[32,4096]{1,0:T(8,128)(2,1)S(1)}, u32[]{:S(2)}, u32[]{:S(2)}) collective-permute-start(bf16[32,4096]{1,0:T(8,128)(2,1)S(1)} %copy-done), channel_id=1, source_target_pairs={{0,8},{8,0},{16,24},{24,16},{1,9},{9,1},{17,25},{25,17},{2,10},{10... | collective-permute-start | bytes 786440 | tf_op jit(solution)/shard_map/ppermute | solution.py:270
  10.5 9.4 %slice-start = ((s8[12582912]{0:T(1024)(128)(4,1)}), s8[4194304]{0:T(1024)(128)(4,1)S(1)}, s32[]{:S(2)}) async-start(s8[12582912]{0:T(1024)(128)(4,1)} %bitcast.5), calls=%async_computation.1 | async-start | bytes 8388608
  10.5 9.4 %slice-start.1 = ((s8[12582912]{0:T(1024)(128)(4,1)}), s8[4194304]{0:T(1024)(128)(4,1)S(1)}, s32[]{:S(2)}) async-start(s8[12582912]{0:T(1024)(128)(4,1)} %bitcast.5), calls=%async_computation.2 | async-start | bytes 8388608
  10.5 9.4 %slice-start.2 = ((s8[12582912]{0:T(1024)(128)(4,1)}), s8[4194304]{0:T(1024)(128)(4,1)S(1)}, s32[]{:S(2)}) async-start(s8[12582912]{0:T(1024)(128)(4,1)} %bitcast.5), calls=%async_computation.3 | async-start | bytes 8388608
  10.5 1.9 %collective-permute-start.4 = (bf16[32,4096]{1,0:T(8,128)(2,1)S(1)}, bf16[32,4096]{1,0:T(8,128)(2,1)S(1)}, u32[]{:S(2)}, u32[]{:S(2)}) collective-permute-start(bf16[32,4096]{1,0:T(8,128)(2,1)S(1)} %collective-permute-done.3.refs_2_), channel_id=1, source_target_pairs={{0,8},{8,0},{16,24},{24,16},{1,9},{9,1},{17,25},{25,17},{2,10},{10... | collective-permute-start | bytes 786440 | tf_op jit(solution)/shard_map/ppermute | solution.py:270
  11.0 8.8 %collective-permute-start = (bf16[32,4224]{1,0:T(8,128)(2,1)S(1)}, bf16[32,4224]{1,0:T(8,128)(2,1)S(1)}, u32[]{:S(2)}, u32[]{:S(2)}) collective-permute-start(bf16[32,4224]{1,0:T(8,128)(2,1)S(1)} %get-tuple-element.19.refs_0_), channel_id=1, source_target_pairs={{0,8},{8,0},{16,24},{24,16},{1,9},{9,1},{17,25},{25,17},{2,10},{10... | collective-permute-start | bytes 811016 | tf_op jit(solution)/shard_map/ppermute | solution.py:270
  18.3 1.6 %collective-permute-start.5 = (bf16[32,4224]{1,0:T(8,128)(2,1)S(1)}, bf16[32,4224]{1,0:T(8,128)(2,1)S(1)}, u32[]{:S(2)}, u32[]{:S(2)}) collective-permute-start(bf16[32,4224]{1,0:T(8,128)(2,1)S(1)} %collective-permute-done.1.refs_6_.refs_2_), channel_id=1, source_target_pairs={{0,8},{8,0},{16,24},{24,16},{1,9},{9,1},{17,25},{25,17},{2,10},{10... | collective-permute-start | bytes 811016 | tf_op jit(solution)/shard_map/ppermute | solution.py:270

commit v14 on v11

--- a/solution.py
+++ b/solution.py
@@ -338,7 +338,6 @@
         name="load_pack",
     )(keep_far(logits), keep_far(routes.T), keep_far(cotangent), gate, up)
     packed_far = [swap(packed, "dp", chip * CORES) for chip in range(1, chips)]
-    packed_beside = swap(packed, "dp", 1)
     tokens_far, gate_near, up_near = lax.optimization_barrier((tokens_far, gate_near, up_near))
     token_pieces = [tokens, tokens_beside]
     for far in tokens_far:
@@ -369,7 +368,8 @@
         name="hidden_first",
     )(*token_pieces, gate_near, up_near, gate, up)
 
-    packed_far, hidden_0 = lax.optimization_barrier((packed_far, hidden_0))
+    packed_far, packed_own, hidden_0 = lax.optimization_barrier((packed_far, packed, hidden_0))
+    packed_beside = swap(packed_own, "dp", 1)
     hidden_1 = pl.pallas_call(
         with_accs(functools.partial(second_hidden_kernel, data_count, size), accs(size)),
         out_shape=jax.ShapeDtypeStruct((places, unit, total_tokens), jnp.float32),

time: 37.3 us -> 37.7 us (1.011)
  transfers between devices with their start and end apart: 6 -> 6, of which waited for: 4 -> 5; matrix products, arithmetic and copies ran while one was open for 0% -> 0% of each run, Pallas kernels for 36% -> 35%
where the time goes in v14:
time: 37.7 us; the launch traced here: 37.5 us
  Pallas kernels  17.7 us (47%)
  blocking collectives  13.3 us (35%)
  starting transfers between devices  4.01 us (11%)
  waiting for transfers between devices  1.74 us (5%)
  between operations  0.7 us (2%)
    all_to_all x1, blocking collectives, per_device(): lax.all_to_all(partial, ('dp', 'expert'), split_axis=0, concat_axis=0, ti...  13.3 us
    pallas_call x1, Pallas kernels, per_device(): pl.pallas_call(functools.partial(load_pack_kernel, plan), out_shape=(jax....  6.08 us
    pallas_call x1, Pallas kernels, per_device(): pl.pallas_call(with_accs(functools.partial(first_hidden_kernel, distances...  5.85 us
    ppermute x6, starting transfers between devices, swap(): lax.ppermute(value, axis, [(index, index ^ distance) for index in range(l...  4.01 us
    pallas_call x1, Pallas kernels, per_device(): pl.pallas_call(with_accs(functools.partial(score_kernel, distances, top),...  3.59 us
    ppermute x6, waiting for transfers between devices, swap(): lax.ppermute(value, axis, [(index, index ^ distance) for index in range(l...  1.74 us
    pallas_call x1, Pallas kernels, per_device(): pl.pallas_call(with_accs(functools.partial(second_hidden_kernel, data_cou...  1.34 us
    pallas_call x1, Pallas kernels, per_device(): pl.pallas_call(functools.partial(gradient_kernel, data_count), out_shape=...  0.85 us
  transfers between devices with their start and end apart: 6, of which 5 were waited for; matrix products, arithmetic and copies ran while one was open for 0% of the time, Pallas kernels for 35%

profile of v14, /device:TPU:0, one launch (start us, length us, event | category | flops | bytes accessed | tf_op | source)
XLA Modules:
  0.0 37.5 jit_solution(12260210209455313263)
XLA Ops:
  0.6 3.0 %collective-permute-start.2 = (bf16[32,4096]{1,0:T(8,128)(2,1)}, bf16[32,4096]{1,0:T(8,128)(2,1)S(1)}, u32[]{:S(2)}, u32[]{:S(2)}) collective-permute-start(bf16[32,4096]{1,0:T(8,128)(2,1)} %refs_0_.3), channel_id=1, source_target_pairs={{0,16},{8,24},{16,0},{24,8},{1,17},{9,25},{17,1},{25,9},{2,18},{10... | collective-permute-start | bytes 786440 | tf_op jit(solution)/shard_map/ppermute | solution.py:267
  3.7 0.0 copy-start
  3.7 6.1 %load_pack.1 = (bf16[32,4224]{1,0:T(8,128)(2,1)S(1)}, bf16[4,256,4096]{2,1,0:T(8,128)(2,1)S(1)}, bf16[4,256,4096]{2,1,0:T(8,128)(2,1)S(1)}) custom-call(f32[32,32]{1,0:T(8,128)} %logits.1, s32[8,32]{1,0:T(8,128)} %bitcast.12, bf16[32,4096]{1,0:T(8,128)(2,1)} %cotangent.1, bf16[6,256,4096]{2,1,0:T(8,128)(2,1)} %bitcast.8, bf16[6,256,4096]{2,1,0:T(8,128)(2,1)} %bitcast.10), custom_call_target="tpu_custom_call" | custom-call | bytes 8 | tf_op jit(solution)/shard_map/load_pack/pallas_call | solution.py:320
  9.8 0.1 collective-permute-start
  9.8 0.0 copy-done
  9.8 0.1 collective-permute-start.1
  9.9 0.3 collective-permute-done.2.refs_2_
  10.2 0.0 slice-start
  10.2 0.3 collective-permute-start.3
  10.5 0.9 %collective-permute-done.1.refs_1_ = bf16[32,4096]{1,0:T(8,128)(2,1)S(1)} collective-permute-done((bf16[32,4096]{1,0:T(8,128)(2,1)S(1)}, bf16[32,4096]{1,0:T(8,128)(2,1)S(1)}, u32[]{:S(2)}, u32[]{:S(2)}) %collective-permute-start.1) | collective-permute-done | bytes 262176 | tf_op jit(solution)/shard_map/ppermute | solution.py:267
  11.4 0.4 collective-permute-done.3.refs_3_
  11.8 5.8 %hidden_first.1 = (f32[10,128,128]{2,1,0:T(8,128)S(1)}, bf16[128,1024]{1,0:T(8,128)(2,1)S(1)}, bf16[1,256,4096]{2,1,0:T(8,128)(2,1)S(1)}, bf16[1,256,4096]{2,1,0:T(8,128)(2,1)S(1)}) custom-call(bf16[32,4096]{1,0:T(8,128)(2,1)S(1)} %copy-done, bf16[32,4096]{1,0:T(8,128)(2,1)S(1)} %collective-permute-done.1.refs_1_, ...), custom_call_target="tpu_custom_call" | custom-call | flops 12 | bytes 4 | tf_op jit(solution)/shard_map/hidden_first/pallas_call | solution.py:349
  17.7 0.1 collective-permute-done.refs_6_.refs_2_
  17.8 0.2 collective-permute-start.4
  18.0 0.3 collective-permute-start.5
  18.3 1.3 %hidden_second.1.refs_5_ = f32[2,128,128]{2,1,0:T(8,128)S(1)} custom-call(bf16[32,4096]{1,0:T(8,128)(2,1)S(1)} %copy-done, bf16[32,4096]{1,0:T(8,128)(2,1)S(1)} %collective-permute-done.1.refs_1_, bf16[32,4096]{1,0:T(8,128)(2,1)S(1)} %collective-permute-done.2.refs_2_, bf16[32,4096]{1,0:T(8,128)(2,1)S(1)} %collective-permute-done.3.refs_3_, ...), custom_call_target="tpu_custom_call" | custom-call | flops 2 | bytes 1 | tf_op jit(solution)/shard_map/hidden_second/pallas_call | solution.py:373
  19.6 0.0 collective-permute-done.4.refs_1_
  19.6 0.1 collective-permute-done.5.refs_3_
  19.7 0.0 slice-done
  19.7 0.0 slice-done.1
  19.7 0.0 slice-done.2
  19.7 3.6 %scores.1 = (f32[32,4,128]{2,1,0:T(4,128)S(1)}, f32[32,128]{1,0:T(8,128)S(1)}, f32[32,128]{1,0:T(8,128)S(1)}) custom-call(bf16[32,4224]{1,0:T(8,128)(2,1)S(1)} %get-tuple-element.27.refs_0_, bf16[32,4224]{1,0:T(8,128)(2,1)S(1)} %collective-permute-done.4.refs_1_, bf16[32,4224]{1,0:T(8,128)(2,1)S(1)} %collective-permute-done.refs_6_.refs_2_, ...), custom_call_target="tpu_custom_call" | custom-call | flops 1 | bytes 1 | tf_op jit(solution)/shard_map/scores/pallas_call | solution.py:388
  23.3 13.3 %all_to_all.5.blocks = f32[32,4,128]{2,1,0:T(4,128)S(1)} all-to-all(f32[32,4,128]{2,1,0:T(4,128)S(1)} %get-tuple-element.32), channel_id=1, replica_groups=mesh['dp'=4,'expert'=8] {'dp','expert'}, dimensions={0} | all-to-all | bytes 131072 | tf_op jit(solution)/shard_map/all_to_all | solution.py:406
  36.7 0.8 %gradient.1 = (f32[32,32]{1,0:T(8,128)}, f32[32,1024]{1,0:T(8,128)}) custom-call(f32[32,4,128]{2,1,0:T(4,128)S(1)} %all_to_all.5.blocks, f32[32,128]{1,0:T(8,128)S(1)} %get-tuple-element.33.probs_ref, f32[32,128]{1,0:T(8,128)S(1)} %get-tuple-element.34.chosen_ref, bf16[128,1024]{1,0:T(8,128)(2,1)S(1)} %get-tuple-element.35.mine), custom_call_target="tpu_custom_call" | custom-call | tf_op jit(solution)/shard_map/gradient/pallas_call | solution.py:408
  (3 shorter events, 0.0 us)
Async XLA Ops:
  0.6 9.5 %collective-permute-start.2 = (bf16[32,4096]{1,0:T(8,128)(2,1)}, bf16[32,4096]{1,0:T(8,128)(2,1)S(1)}, u32[]{:S(2)}, u32[]{:S(2)}) collective-permute-start(bf16[32,4096]{1,0:T(8,128)(2,1)} %refs_0_.3), channel_id=1, source_target_pairs={{0,16},{8,24},{16,0},{24,8},{1,17},{9,25},{17,1},{25,9},{2,18},{10... | collective-permute-start | bytes 786440 | tf_op jit(solution)/shard_map/ppermute | solution.py:267
  3.7 6.2 %copy-start = (bf16[32,4096]{1,0:T(8,128)(2,1)S(1)}, bf16[32,4096]{1,0:T(8,128)(2,1)}, u32[]{:S(2)}) copy-start(bf16[32,4096]{1,0:T(8,128)(2,1)} %refs_0_.3) | copy-start | bytes 786436
  9.8 8.0 %collective-permute-start = (bf16[32,4224]{1,0:T(8,128)(2,1)S(1)}, bf16[32,4224]{1,0:T(8,128)(2,1)S(1)}, u32[]{:S(2)}, u32[]{:S(2)}) collective-permute-start(bf16[32,4224]{1,0:T(8,128)(2,1)S(1)} %get-tuple-element.27.refs_0_), channel_id=1, source_target_pairs={{0,16},{8,24},{16,0},{24,8},{1,17},{9,25},{17,1},{25,9},{2,18},{10... | collective-permute-start | bytes 811016 | tf_op jit(solution)/shard_map/ppermute | solution.py:267
  9.8 1.6 %collective-permute-start.1 = (bf16[32,4096]{1,0:T(8,128)(2,1)S(1)}, bf16[32,4096]{1,0:T(8,128)(2,1)S(1)}, u32[]{:S(2)}, u32[]{:S(2)}) collective-permute-start(bf16[32,4096]{1,0:T(8,128)(2,1)S(1)} %copy-done), channel_id=1, source_target_pairs={{0,8},{8,0},{16,24},{24,16},{1,9},{9,1},{17,25},{25,17},{2,10},{10... | collective-permute-start | bytes 786440 | tf_op jit(solution)/shard_map/ppermute | solution.py:267
  10.2 9.5 %slice-start = ((s8[12582912]{0:T(1024)(128)(4,1)}), s8[4194304]{0:T(1024)(128)(4,1)S(1)}, s32[]{:S(2)}) async-start(s8[12582912]{0:T(1024)(128)(4,1)} %bitcast.5), calls=%async_computation.1 | async-start | bytes 8388608
  10.2 9.5 %slice-start.1 = ((s8[12582912]{0:T(1024)(128)(4,1)}), s8[4194304]{0:T(1024)(128)(4,1)S(1)}, s32[]{:S(2)}) async-start(s8[12582912]{0:T(1024)(128)(4,1)} %bitcast.5), calls=%async_computation.2 | async-start | bytes 8388608
  10.2 9.5 %slice-start.2 = ((s8[12582912]{0:T(1024)(128)(4,1)}), s8[4194304]{0:T(1024)(128)(4,1)S(1)}, s32[]{:S(2)}) async-start(s8[12582912]{0:T(1024)(128)(4,1)} %bitcast.5), calls=%async_computation.3 | async-start | bytes 8388608
  10.2 1.6 %collective-permute-start.3 = (bf16[32,4096]{1,0:T(8,128)(2,1)S(1)}, bf16[32,4096]{1,0:T(8,128)(2,1)S(1)}, u32[]{:S(2)}, u32[]{:S(2)}) collective-permute-start(bf16[32,4096]{1,0:T(8,128)(2,1)S(1)} %collective-permute-done.2.refs_2_), channel_id=1, source_target_pairs={{0,8},{8,0},{16,24},{24,16},{1,9},{9,1},{17,25},{25,17},{2,10},{10... | collective-permute-start | bytes 786440 | tf_op jit(solution)/shard_map/ppermute | solution.py:267
  17.8 1.9 %collective-permute-start.4 = (bf16[32,4224]{1,0:T(8,128)(2,1)S(1)}, bf16[32,4224]{1,0:T(8,128)(2,1)S(1)}, u32[]{:S(2)}, u32[]{:S(2)}) collective-permute-start(bf16[32,4224]{1,0:T(8,128)(2,1)S(1)} %get-tuple-element.27.refs_0_), channel_id=1, source_target_pairs={{0,8},{8,0},{16,24},{24,16},{1,9},{9,1},{17,25},{25,17},{2,10},{10... | collective-permute-start | bytes 811016 | tf_op jit(solution)/shard_map/ppermute | solution.py:267
  18.0 1.7 %collective-permute-start.5 = (bf16[32,4224]{1,0:T(8,128)(2,1)S(1)}, bf16[32,4224]{1,0:T(8,128)(2,1)S(1)}, u32[]{:S(2)}, u32[]{:S(2)}) collective-permute-start(bf16[32,4224]{1,0:T(8,128)(2,1)S(1)} %collective-permute-done.refs_6_.refs_2_), channel_id=1, source_target_pairs={{0,8},{8,0},{16,24},{24,16},{1,9},{9,1},{17,25},{25,17},{2,10},{10... | collective-permute-start | bytes 811016 | tf_op jit(solution)/shard_map/ppermute | solution.py:267
